TPU v7x, 512 devices: a whole 4x4x16 slice. The times are simulated.
512 devices in a mesh: gy: 16 (over y, x), gz: 32 (over z, core).
Axes of the slice: x: 4, y: 4, z: 16, core: 2. Of those that a mesh axis runs over, the one named last changes fastest.
Arguments:
- conduct: float32 [256, 1024, 128], P('gy', 'gz'), may hold values from 0.3 to 3
- seeds: int32 [256, 1024, 128], P('gy', 'gz'), may hold values 0 or 1
- labels: int32 [256, 1024, 128], P('gy', 'gz'), may hold values 0 or 1
- start: float32 [256, 1024, 128], P('gy', 'gz'), may hold values from 0 to 1
- cotangent: float32 [256, 1024, 128], P('gy', 'gz'), may hold values from -12 to 12
Outputs:
- probability: float32 [256, 1024, 128], P('gy', 'gz')
- adjoint: float32 [256, 1024, 128], P('gy', 'gz')
- grad_conduct: float32 [256, 1024, 128], P('gy', 'gz')
All inputs are finite; a program needn't handle non-finite values. No bound on the sum of `seeds` or of `labels` on one device may be relied on, other than what follows from the above.
Results may differ from a plain program's by a relative error of at most 0.0001.
Values sent between devices are 32-bit elements; how exact they have to be, the bound alone decides.
No kernel may reach another device: no remote copies, remote signals or barrier semaphores. Data moves between devices by JAX's collectives and lax.ppermute only.
A program may use at most 64 MiB of HBM per device.

v0:
```python
import jax
import jax.numpy as jnp
from jax import lax
from jax.sharding import Mesh
from jax.sharding import PartitionSpec as P

ITERS = 2
GY = ("gy_0", "gy_1")
GZ = ("gz_0", "gz_1")


seed_pull = 4.0
screening = 0.05


def with_halo(shard, sides, width):
    edges = {}
    for axis, dim in sides:
        devices, length = (lax.axis_size(axis), shard.shape[dim])
        up = [(i, (i + 1) % devices) for i in range(devices - 1)]
        last = lax.slice_in_dim(shard, length - width, length, axis=dim)
        initial = lax.slice_in_dim(shard, 0, width, axis=dim)
        edges[dim] = (
            lax.ppermute(last, axis, up),
            lax.ppermute(initial, axis, [(b, a) for a, b in up]),
        )
    done = []
    for _, dim in sides:
        low, high = edges[dim]
        around = [(width, width) if d in done else (0, 0) for d in range(shard.ndim)]
        shard = jnp.concatenate([jnp.pad(low, around), shard, jnp.pad(high, around)], axis=dim)
        done.append(dim)
    return shard


def from_everyone(shard, axis):
    copies = jnp.broadcast_to(shard, (lax.axis_size(axis), *shard.shape))
    return lax.all_to_all(copies, axis, split_axis=0, concat_axis=0, tiled=True)


def over_copies(shard, axis):
    everything = from_everyone(shard, axis)
    return jnp.sum(everything, axis=0)


def by_axis(shard, axes):
    far, near = axes
    return over_copies(over_copies(shard, near), far)


def packed_total(arrays, axis):
    line, at, finished = (jnp.concatenate([a.reshape(-1) for a in arrays]), 0, [])
    total = by_axis(line, axis)
    for a in arrays:
        finished.append(total[at : at + a.size].reshape(a.shape))
        at += a.size
    return tuple(finished)


def harmonic(first, second):
    return 2.0 * first * second / (first + second)


def faces(field):
    return with_halo(field, ((GY, 0), (GZ, 1)), 1)


def stacked_faces(field):
    return with_halo(field, ((GY, 1), (GZ, 2)), 1)


def coefficients(padded_cond, seeds):
    core = padded_cond[1:-1, 1:-1]
    along = jnp.pad(core, ((0, 0), (0, 0), (1, 1)))
    weights = (
        harmonic(core, padded_cond[2:, 1:-1]),
        harmonic(core, padded_cond[:-2, 1:-1]),
        harmonic(core, padded_cond[1:-1, 2:]),
        harmonic(core, padded_cond[1:-1, :-2]),
        harmonic(core, along[..., 2:]),
        harmonic(core, along[..., :-2]),
    )
    diagonal = weights[0] + weights[1] + weights[2] + weights[3] + weights[4] + weights[5]
    diagonal = diagonal + seed_pull * seeds.astype(jnp.float32) + screening
    return (diagonal,) + weights


def operate(padded, coeffs):
    field = padded[1:-1, 1:-1]
    along = jnp.pad(field, ((0, 0), (0, 0), (1, 1)))
    out = coeffs[0] * field - coeffs[1] * padded[2:, 1:-1] - coeffs[2] * padded[:-2, 1:-1]
    out = out - coeffs[3] * padded[1:-1, 2:] - coeffs[4] * padded[1:-1, :-2]
    return out - coeffs[5] * along[..., 2:] - coeffs[6] * along[..., :-2]


def edge_term(ci, cj, ui, uj, vi, vj):
    total = ci + cj
    return -2.0 * cj * cj / (total * total) * (ui - uj) * (vi - vj)


def gradient(cond_pad, prob_pad, adj_pad):
    ci = cond_pad[1:-1, 1:-1]
    ui = prob_pad[1:-1, 1:-1]
    vi = adj_pad[1:-1, 1:-1]
    out = edge_term(ci, cond_pad[2:, 1:-1], ui, prob_pad[2:, 1:-1], vi, adj_pad[2:, 1:-1])
    out = out + edge_term(ci, cond_pad[:-2, 1:-1], ui, prob_pad[:-2, 1:-1], vi, adj_pad[:-2, 1:-1])
    out = out + edge_term(ci, cond_pad[1:-1, 2:], ui, prob_pad[1:-1, 2:], vi, adj_pad[1:-1, 2:])
    out = out + edge_term(ci, cond_pad[1:-1, :-2], ui, prob_pad[1:-1, :-2], vi, adj_pad[1:-1, :-2])
    cx = jnp.pad(ci, ((0, 0), (0, 0), (1, 1)))
    ux = jnp.pad(ui, ((0, 0), (0, 0), (1, 1)))
    vx = jnp.pad(vi, ((0, 0), (0, 0), (1, 1)))
    out = out + edge_term(ci, cx[..., 2:], ui, ux[..., 2:], vi, vx[..., 2:])
    return out + edge_term(ci, cx[..., :-2], ui, ux[..., :-2], vi, vx[..., :-2])


def pair_products(resid, image):
    return packed_total(
        (jnp.sum(resid * resid, axis=(1, 2, 3)), jnp.sum(resid * image, axis=(1, 2, 3))),
        (("gy_0", "gy_1"), ("gz_0", "gz_1")),
    )


def widen(scalars):
    return scalars[:, None, None, None]


def conjugate_pair(iterate, iterate_pad, resid, coeffs):
    apply_both = jax.vmap(operate, in_axes=(0, None))
    resid_pad = stacked_faces(resid)
    image = apply_both(resid_pad, coeffs)
    norm_now, product = pair_products(resid, image)
    alpha = norm_now / product
    direction, direction_pad, along = (resid, resid_pad, image)
    for step in range(ITERS):
        iterate = iterate + widen(alpha) * direction
        iterate_pad = iterate_pad + widen(alpha) * direction_pad
        resid = resid - widen(alpha) * along
        if step + 1 < ITERS:
            resid_pad = stacked_faces(resid)
            image = apply_both(resid_pad, coeffs)
            norm_next, product = pair_products(resid, image)
            ratio = norm_next / norm_now
            alpha = norm_next / (product - ratio * norm_next / alpha)
            direction = resid + widen(ratio) * direction
            direction_pad = resid_pad + widen(ratio) * direction_pad
            along = image + widen(ratio) * along
            norm_now = norm_next
    return (iterate, iterate_pad)


def per_device(conduct, seeds, labels, start, cotangent):
    cond_pad = with_halo(conduct, ((GY, 0), (GZ, 1)), 1)
    start_pad = faces(start)
    coeffs = coefficients(cond_pad, seeds)
    rhs = seed_pull * (seeds * labels).astype(jnp.float32)
    first_resid = rhs - operate(start_pad, coeffs)
    both_iterates = jnp.stack([start, jnp.zeros_like(cotangent)])
    both_pads = jnp.stack([start_pad, jnp.zeros_like(start_pad)])
    both_resids = jnp.stack([first_resid, cotangent])
    results, result_pads = conjugate_pair(both_iterates, both_pads, both_resids, coeffs)
    probability, adjoint = (results[0], results[1])
    prob_pad, adj_pad = (result_pads[0], result_pads[1])
    grad_conduct = gradient(cond_pad, prob_pad, adj_pad)
    return (probability, adjoint, grad_conduct)


def solution(mesh):
    split = Mesh(mesh.devices.reshape(4, 4, 16, 2), ("gy_0", "gy_1", "gz_0", "gz_1"))
    return jax.shard_map(
        per_device,
        mesh=split,
        in_specs=(
            P(GY, GZ, None),
            P(GY, GZ, None),
            P(GY, GZ, None),
            P(GY, GZ, None),
            P(GY, GZ, None),
        ),
        out_specs=(P(GY, GZ, None), P(GY, GZ, None), P(GY, GZ, None)),
        check_vma=False,
    )
```

profile of v0, /device:TPU:1, one launch (start us, length us, event | category | flops | bytes accessed | tf_op | source)
XLA Modules:
  0.0 142.8 jit_solution(13902117427177647148)
XLA Ops:
  1.4 3.9 %collective-permute-start.1 = (f32[1,32,128]{2,1,0:T(8,128)S(1)}, f32[1,32,128]{2,1,0:T(8,128)S(1)}, u32[]{:S(2)}, u32[]{:S(2)}) collective-permute-start(f32[1,32,128]{2,1,0:T(8,128)S(1)} %get-tuple-element.35), channel_id=1, source_target_pairs={{0,32},{32,64},{64,96},{96,128},{128,160},{160,192},{192,224},{224... | collective-permute-start | bytes 49160 | tf_op jit(solution)/shard_map/ppermute | solution.py:24
  5.4 1.3 collective-permute-start
  7.6 6.1 %collective-permute-start.2 = (f32[16,1,128]{2,1,0:T(1,128)S(1)}, f32[16,1,128]{2,1,0:T(1,128)S(1)}, u32[]{:S(2)}, u32[]{:S(2)}) collective-permute-start(f32[16,1,128]{2,1,0:T(1,128)S(1)} %get-tuple-element.34), channel_id=1, source_target_pairs={{1,0},{2,1},{3,2},{4,3},{5,4},{6,5},{7,6},{8,7},{9,8},{10,9},{11,1... | collective-permute-start | bytes 24584 | tf_op jit(solution)/shard_map/ppermute | solution.py:25
  14.6 1.9 %collective-permute-start.6 = (f32[16,1,128]{2,1,0:T(1,128)S(1)}, f32[16,1,128]{2,1,0:T(1,128)S(1)}, u32[]{:S(2)}, u32[]{:S(2)}) collective-permute-start(f32[16,1,128]{2,1,0:T(1,128)S(1)} %get-tuple-element.29), channel_id=1, source_target_pairs={{1,0},{2,1},{3,2},{4,3},{5,4},{6,5},{7,6},{8,7},{9,8},{10,9},{11,1... | collective-permute-start | bytes 24584 | tf_op jit(solution)/shard_map/ppermute | solution.py:25
  16.5 3.6 %collective-permute-start.7 = (f32[16,1,128]{2,1,0:T(1,128)S(1)}, f32[16,1,128]{2,1,0:T(1,128)S(1)}, u32[]{:S(2)}, u32[]{:S(2)}) collective-permute-start(f32[16,1,128]{2,1,0:T(1,128)S(1)} %get-tuple-element.30), channel_id=1, source_target_pairs={{0,1},{1,2},{2,3},{3,4},{4,5},{5,6},{6,7},{7,8},{8,9},{9,10},{10,1... | collective-permute-start | bytes 24584 | tf_op jit(solution)/shard_map/ppermute | solution.py:24
  20.9 1.9 %collective-permute-start.3 = (f32[16,1,128]{2,1,0:T(1,128)S(1)}, f32[16,1,128]{2,1,0:T(1,128)S(1)}, u32[]{:S(2)}, u32[]{:S(2)}) collective-permute-start(f32[16,1,128]{2,1,0:T(1,128)S(1)} %get-tuple-element.33), channel_id=1, source_target_pairs={{0,1},{1,2},{2,3},{3,4},{4,5},{5,6},{6,7},{7,8},{8,9},{9,10},{10,1... | collective-permute-start | bytes 24584 | tf_op jit(solution)/shard_map/ppermute | solution.py:24
  22.9 4.3 %collective-permute-start.5 = (f32[1,32,128]{2,1,0:T(8,128)S(1)}, f32[1,32,128]{2,1,0:T(8,128)S(1)}, u32[]{:S(2)}, u32[]{:S(2)}) collective-permute-start(f32[1,32,128]{2,1,0:T(8,128)S(1)} %get-tuple-element.32), channel_id=1, source_target_pairs={{0,32},{32,64},{64,96},{96,128},{128,160},{160,192},{192,224},{224... | collective-permute-start | bytes 49160 | tf_op jit(solution)/shard_map/ppermute | solution.py:24
  27.2 1.3 collective-permute-start.4
  29.5 2.2 %collective-permute-done.4 = f32[1,32,128]{2,1,0:T(8,128)S(1)} collective-permute-done((f32[1,32,128]{2,1,0:T(8,128)S(1)}, f32[1,32,128]{2,1,0:T(8,128)S(1)}, u32[]{:S(2)}, u32[]{:S(2)}) %collective-permute-start.4) | collective-permute-done | bytes 16416 | tf_op jit(solution)/shard_map/ppermute | solution.py:25
  33.7 1.3 collective-permute-start.8
  35.0 4.0 %collective-permute-start.9 = (f32[2,1,32,128]{3,2,1,0:T(8,128)S(1)}, f32[2,1,32,128]{3,2,1,0:T(8,128)S(1)}, u32[]{:S(2)}, u32[]{:S(2)}) collective-permute-start(f32[2,1,32,128]{3,2,1,0:T(8,128)S(1)} %get-tuple-element.27), channel_id=1, source_target_pairs={{0,32},{32,64},{64,96},{96,128},{128,160},{160,192},{192,224},{224... | collective-permute-start | bytes 98312 | tf_op jit(solution)/shard_map/ppermute | solution.py:24
  39.0 4.4 %collective-permute-start.10 = (f32[2,16,1,128]{3,2,1,0:T(1,128)S(1)}, f32[2,16,1,128]{3,2,1,0:T(1,128)S(1)}, u32[]{:S(2)}, u32[]{:S(2)}) collective-permute-start(f32[2,16,1,128]{3,2,1,0:T(1,128)S(1)} %get-tuple-element.25), channel_id=1, source_target_pairs={{1,0},{2,1},{3,2},{4,3},{5,4},{6,5},{7,6},{8,7},{9,8},{10,9},{11,1... | collective-permute-start | bytes 49160 | tf_op jit(solution)/shard_map/ppermute | solution.py:25
  43.4 1.9 %collective-permute-start.11 = (f32[2,16,1,128]{3,2,1,0:T(1,128)S(1)}, f32[2,16,1,128]{3,2,1,0:T(1,128)S(1)}, u32[]{:S(2)}, u32[]{:S(2)}) collective-permute-start(f32[2,16,1,128]{3,2,1,0:T(1,128)S(1)} %get-tuple-element.26), channel_id=1, source_target_pairs={{0,1},{1,2},{2,3},{3,4},{4,5},{5,6},{6,7},{7,8},{8,9},{9,10},{10,1... | collective-permute-start | bytes 49160 | tf_op jit(solution)/shard_map/ppermute | solution.py:24
  46.5 1.3 multiply_reduce_fusion.2
  47.9 26.8 %all_to_all.24 = f32[32,1,4]{2,1,0:T(1,128)S(1)} all-to-all(f32[32,1,4]{2,1,0:T(1,128)S(1)} %broadcast_in_dim.8), channel_id=1, replica_groups=mesh['gy_0'=4,'gy_1'=4,'gz_0'=16,'gz_1'=2] {'gz_0','gz_1'}, dimensions={0} | all-to-all | bytes 1024 | tf_op jit(solution)/shard_map/all_to_all | solution.py:38
  74.8 18.7 %all_to_all.25 = f32[16,1,4]{2,1,0:T(1,128)S(1)} all-to-all(f32[16,1,4]{2,1,0:T(1,128)S(1)} %broadcast_in_dim.9), channel_id=1, replica_groups=mesh['gy_0'=4,'gy_1'=4,'gz_0'=16,'gz_1'=2] {'gy_0','gy_1'}, dimensions={0} | all-to-all | bytes 512 | tf_op jit(solution)/shard_map/all_to_all | solution.py:38
  94.6 1.3 multiply_reduce_fusion
  97.2 4.0 %collective-permute-start.13 = (f32[2,1,32,128]{3,2,1,0:T(8,128)S(1)}, f32[2,1,32,128]{3,2,1,0:T(8,128)S(1)}, u32[]{:S(2)}, u32[]{:S(2)}) collective-permute-start(f32[2,1,32,128]{3,2,1,0:T(8,128)S(1)} %get-tuple-element.23), channel_id=1, source_target_pairs={{0,32},{32,64},{64,96},{96,128},{128,160},{160,192},{192,224},{224... | collective-permute-start | bytes 98312 | tf_op jit(solution)/shard_map/ppermute | solution.py:24
  101.2 4.8 %collective-permute-start.14 = (f32[2,16,1,128]{3,2,1,0:T(1,128)S(1)}, f32[2,16,1,128]{3,2,1,0:T(1,128)S(1)}, u32[]{:S(2)}, u32[]{:S(2)}) collective-permute-start(f32[2,16,1,128]{3,2,1,0:T(1,128)S(1)} %get-tuple-element.21), channel_id=1, source_target_pairs={{1,0},{2,1},{3,2},{4,3},{5,4},{6,5},{7,6},{8,7},{9,8},{10,9},{11,1... | collective-permute-start | bytes 49160 | tf_op jit(solution)/shard_map/ppermute | solution.py:25
  106.1 2.1 %collective-permute-start.15 = (f32[2,16,1,128]{3,2,1,0:T(1,128)S(1)}, f32[2,16,1,128]{3,2,1,0:T(1,128)S(1)}, u32[]{:S(2)}, u32[]{:S(2)}) collective-permute-start(f32[2,16,1,128]{3,2,1,0:T(1,128)S(1)} %get-tuple-element.22), channel_id=1, source_target_pairs={{0,1},{1,2},{2,3},{3,4},{4,5},{5,6},{6,7},{7,8},{8,9},{9,10},{10,1... | collective-permute-start | bytes 49160 | tf_op jit(solution)/shard_map/ppermute | solution.py:24
  109.9 16.9 %all_to_all.26 = f32[32,1,4]{2,1,0:T(1,128)S(1)} all-to-all(f32[32,1,4]{2,1,0:T(1,128)S(1)} %broadcast_in_dim.10), channel_id=1, replica_groups=mesh['gy_0'=4,'gy_1'=4,'gz_0'=16,'gz_1'=2] {'gz_0','gz_1'}, dimensions={0} | all-to-all | bytes 1024 | tf_op jit(solution)/shard_map/all_to_all | solution.py:38
  127.4 5.1 %all-to-all-start.3 = ((f32[16,1,4]{2,1,0:T(1,128)}), f32[16,1,4]{2,1,0:T(1,128)S(1)}, u32[]{:S(2)}, u32[]{:S(2)}) async-start(f32[16,1,4]{2,1,0:T(1,128)} %broadcast_in_dim.11), calls=%async_computation.3 | async-start | bytes 16384 | tf_op jit(solution)/shard_map/all_to_all | solution.py:38
  133.6 5.3 %all-to-all-done.3 = f32[16,1,4]{2,1,0:T(1,128)S(1)} async-done(((f32[16,1,4]{2,1,0:T(1,128)}), f32[16,1,4]{2,1,0:T(1,128)S(1)}, u32[]{:S(2)}, u32[]{:S(2)}) %all-to-all-start.3) | async-done | bytes 288 | tf_op jit(solution)/shard_map/all_to_all | solution.py:38
  141.4 1.4 %fusion.35 = f32[16,32,128]{2,1,0:T(8,128)} fusion(f32[16,32,128]{2,1,0:T(8,128)S(1)} %slice.285, f32[16,32,128]{2,1,0:T(8,128)S(1)} %slice.288, f32[18,34,128]{2,1,0:T(8,128)S(1)} %get-tuple-element.17, f32[18,34,128]{2,1,0:T(8,128)S(1)} %get-tuple-element.18, f32[16,32,128]{2,1,0:T(8,128)S(1)} %copy-done.2, f32[1,32,128]{2,1,0:T(8,128)S(1)} %collective-permute-done.1, ...), kind=kLoop, calls=%fused_computation.92 | loop fusion | flops 4521984 | bytes 3489792 | tf_op jit(solution)/shard_map/add | solution.py:113
  (109 shorter events, 15.7 us)
Async XLA Ops:
  0.6 27.9 %copy-start.2 = (f32[16,32,128]{2,1,0:T(8,128)S(1)}, f32[16,32,128]{2,1,0:T(8,128)}, u32[]{:S(2)}) copy-start(f32[16,32,128]{2,1,0:T(8,128)} %param.5) | copy-start | bytes 786436
  1.4 25.7 %collective-permute-start.1 = (f32[1,32,128]{2,1,0:T(8,128)S(1)}, f32[1,32,128]{2,1,0:T(8,128)S(1)}, u32[]{:S(2)}, u32[]{:S(2)}) collective-permute-start(f32[1,32,128]{2,1,0:T(8,128)S(1)} %get-tuple-element.35), channel_id=1, source_target_pairs={{0,32},{32,64},{64,96},{96,128},{128,160},{160,192},{192,224},{224... | collective-permute-start | bytes 49160 | tf_op jit(solution)/shard_map/ppermute | solution.py:24
  5.4 24.1 %collective-permute-start = (f32[1,32,128]{2,1,0:T(8,128)S(1)}, f32[1,32,128]{2,1,0:T(8,128)S(1)}, u32[]{:S(2)}, u32[]{:S(2)}) collective-permute-start(f32[1,32,128]{2,1,0:T(8,128)S(1)} %get-tuple-element.36), channel_id=1, source_target_pairs={{32,0},{64,32},{96,64},{128,96},{160,128},{192,160},{224,192},{256... | collective-permute-start | bytes 49160 | tf_op jit(solution)/shard_map/ppermute | solution.py:25
  7.6 24.1 %collective-permute-start.2 = (f32[16,1,128]{2,1,0:T(1,128)S(1)}, f32[16,1,128]{2,1,0:T(1,128)S(1)}, u32[]{:S(2)}, u32[]{:S(2)}) collective-permute-start(f32[16,1,128]{2,1,0:T(1,128)S(1)} %get-tuple-element.34), channel_id=1, source_target_pairs={{1,0},{2,1},{3,2},{4,3},{5,4},{6,5},{7,6},{8,7},{9,8},{10,9},{11,1... | collective-permute-start | bytes 24584 | tf_op jit(solution)/shard_map/ppermute | solution.py:25
  14.6 6.3 %collective-permute-start.6 = (f32[16,1,128]{2,1,0:T(1,128)S(1)}, f32[16,1,128]{2,1,0:T(1,128)S(1)}, u32[]{:S(2)}, u32[]{:S(2)}) collective-permute-start(f32[16,1,128]{2,1,0:T(1,128)S(1)} %get-tuple-element.29), channel_id=1, source_target_pairs={{1,0},{2,1},{3,2},{4,3},{5,4},{6,5},{7,6},{8,7},{9,8},{10,9},{11,1... | collective-permute-start | bytes 24584 | tf_op jit(solution)/shard_map/ppermute | solution.py:25
  16.5 6.3 %collective-permute-start.7 = (f32[16,1,128]{2,1,0:T(1,128)S(1)}, f32[16,1,128]{2,1,0:T(1,128)S(1)}, u32[]{:S(2)}, u32[]{:S(2)}) collective-permute-start(f32[16,1,128]{2,1,0:T(1,128)S(1)} %get-tuple-element.30), channel_id=1, source_target_pairs={{0,1},{1,2},{2,3},{3,4},{4,5},{5,6},{6,7},{7,8},{8,9},{9,10},{10,1... | collective-permute-start | bytes 24584 | tf_op jit(solution)/shard_map/ppermute | solution.py:24
  20.9 10.8 %collective-permute-start.3 = (f32[16,1,128]{2,1,0:T(1,128)S(1)}, f32[16,1,128]{2,1,0:T(1,128)S(1)}, u32[]{:S(2)}, u32[]{:S(2)}) collective-permute-start(f32[16,1,128]{2,1,0:T(1,128)S(1)} %get-tuple-element.33), channel_id=1, source_target_pairs={{0,1},{1,2},{2,3},{3,4},{4,5},{5,6},{6,7},{7,8},{8,9},{9,10},{10,1... | collective-permute-start | bytes 24584 | tf_op jit(solution)/shard_map/ppermute | solution.py:24
  22.9 9.5 %copy-start.14 = (f32[18,1,128]{2,1,0:T(1,128)}, f32[18,1,128]{2,1,0:T(1,128)S(1)}, u32[]{:S(2)}) copy-start(f32[18,1,128]{2,1,0:T(1,128)S(1)} %pad.52) | copy-start | bytes 27652
  22.9 5.7 %collective-permute-start.5 = (f32[1,32,128]{2,1,0:T(8,128)S(1)}, f32[1,32,128]{2,1,0:T(8,128)S(1)}, u32[]{:S(2)}, u32[]{:S(2)}) collective-permute-start(f32[1,32,128]{2,1,0:T(8,128)S(1)} %get-tuple-element.32), channel_id=1, source_target_pairs={{0,32},{32,64},{64,96},{96,128},{128,160},{160,192},{192,224},{224... | collective-permute-start | bytes 49160 | tf_op jit(solution)/shard_map/ppermute | solution.py:24
  27.2 5.2 %copy-start.16 = (f32[18,1,128]{2,1,0:T(1,128)}, f32[18,1,128]{2,1,0:T(1,128)S(1)}, u32[]{:S(2)}) copy-start(f32[18,1,128]{2,1,0:T(1,128)S(1)} %pad.53) | copy-start | bytes 27652
  27.2 4.5 %collective-permute-start.4 = (f32[1,32,128]{2,1,0:T(8,128)S(1)}, f32[1,32,128]{2,1,0:T(8,128)S(1)}, u32[]{:S(2)}, u32[]{:S(2)}) collective-permute-start(f32[1,32,128]{2,1,0:T(8,128)S(1)} %get-tuple-element.31), channel_id=1, source_target_pairs={{32,0},{64,32},{96,64},{128,96},{160,128},{192,160},{224,192},{256... | collective-permute-start | bytes 49160 | tf_op jit(solution)/shard_map/ppermute | solution.py:25
  33.7 12.8 %collective-permute-start.8 = (f32[2,1,32,128]{3,2,1,0:T(8,128)S(1)}, f32[2,1,32,128]{3,2,1,0:T(8,128)S(1)}, u32[]{:S(2)}, u32[]{:S(2)}) collective-permute-start(f32[2,1,32,128]{3,2,1,0:T(8,128)S(1)} %get-tuple-element.28), channel_id=1, source_target_pairs={{32,0},{64,32},{96,64},{128,96},{160,128},{192,160},{224,192},{256... | collective-permute-start | bytes 98312 | tf_op jit(solution)/shard_map/ppermute | solution.py:25
  35.0 11.5 %collective-permute-start.9 = (f32[2,1,32,128]{3,2,1,0:T(8,128)S(1)}, f32[2,1,32,128]{3,2,1,0:T(8,128)S(1)}, u32[]{:S(2)}, u32[]{:S(2)}) collective-permute-start(f32[2,1,32,128]{3,2,1,0:T(8,128)S(1)} %get-tuple-element.27), channel_id=1, source_target_pairs={{0,32},{32,64},{64,96},{96,128},{128,160},{160,192},{192,224},{224... | collective-permute-start | bytes 98312 | tf_op jit(solution)/shard_map/ppermute | solution.py:24
  39.0 6.4 %collective-permute-start.10 = (f32[2,16,1,128]{3,2,1,0:T(1,128)S(1)}, f32[2,16,1,128]{3,2,1,0:T(1,128)S(1)}, u32[]{:S(2)}, u32[]{:S(2)}) collective-permute-start(f32[2,16,1,128]{3,2,1,0:T(1,128)S(1)} %get-tuple-element.25), channel_id=1, source_target_pairs={{1,0},{2,1},{3,2},{4,3},{5,4},{6,5},{7,6},{8,7},{9,8},{10,9},{11,1... | collective-permute-start | bytes 49160 | tf_op jit(solution)/shard_map/ppermute | solution.py:25
  43.4 3.1 %collective-permute-start.11 = (f32[2,16,1,128]{3,2,1,0:T(1,128)S(1)}, f32[2,16,1,128]{3,2,1,0:T(1,128)S(1)}, u32[]{:S(2)}, u32[]{:S(2)}) collective-permute-start(f32[2,16,1,128]{3,2,1,0:T(1,128)S(1)} %get-tuple-element.26), channel_id=1, source_target_pairs={{0,1},{1,2},{2,3},{3,4},{4,5},{5,6},{6,7},{7,8},{8,9},{9,10},{10,1... | collective-permute-start | bytes 49160 | tf_op jit(solution)/shard_map/ppermute | solution.py:24
  95.9 13.2 %collective-permute-start.12 = (f32[2,1,32,128]{3,2,1,0:T(8,128)S(1)}, f32[2,1,32,128]{3,2,1,0:T(8,128)S(1)}, u32[]{:S(2)}, u32[]{:S(2)}) collective-permute-start(f32[2,1,32,128]{3,2,1,0:T(8,128)S(1)} %get-tuple-element.24), channel_id=1, source_target_pairs={{32,0},{64,32},{96,64},{128,96},{160,128},{192,160},{224,192},{256... | collective-permute-start | bytes 98312 | tf_op jit(solution)/shard_map/ppermute | solution.py:25
  97.2 12.0 %collective-permute-start.13 = (f32[2,1,32,128]{3,2,1,0:T(8,128)S(1)}, f32[2,1,32,128]{3,2,1,0:T(8,128)S(1)}, u32[]{:S(2)}, u32[]{:S(2)}) collective-permute-start(f32[2,1,32,128]{3,2,1,0:T(8,128)S(1)} %get-tuple-element.23), channel_id=1, source_target_pairs={{0,32},{32,64},{64,96},{96,128},{128,160},{160,192},{192,224},{224... | collective-permute-start | bytes 98312 | tf_op jit(solution)/shard_map/ppermute | solution.py:24
  101.2 6.9 %collective-permute-start.14 = (f32[2,16,1,128]{3,2,1,0:T(1,128)S(1)}, f32[2,16,1,128]{3,2,1,0:T(1,128)S(1)}, u32[]{:S(2)}, u32[]{:S(2)}) collective-permute-start(f32[2,16,1,128]{3,2,1,0:T(1,128)S(1)} %get-tuple-element.21), channel_id=1, source_target_pairs={{1,0},{2,1},{3,2},{4,3},{5,4},{6,5},{7,6},{8,7},{9,8},{10,9},{11,1... | collective-permute-start | bytes 49160 | tf_op jit(solution)/shard_map/ppermute | solution.py:25
  106.1 3.1 %collective-permute-start.15 = (f32[2,16,1,128]{3,2,1,0:T(1,128)S(1)}, f32[2,16,1,128]{3,2,1,0:T(1,128)S(1)}, u32[]{:S(2)}, u32[]{:S(2)}) collective-permute-start(f32[2,16,1,128]{3,2,1,0:T(1,128)S(1)} %get-tuple-element.22), channel_id=1, source_target_pairs={{0,1},{1,2},{2,3},{3,4},{4,5},{5,6},{6,7},{7,8},{8,9},{9,10},{10,1... | collective-permute-start | bytes 49160 | tf_op jit(solution)/shard_map/ppermute | solution.py:24
  127.4 11.5 %all-to-all-start.3 = ((f32[16,1,4]{2,1,0:T(1,128)}), f32[16,1,4]{2,1,0:T(1,128)S(1)}, u32[]{:S(2)}, u32[]{:S(2)}) async-start(f32[16,1,4]{2,1,0:T(1,128)} %broadcast_in_dim.11), calls=%async_computation.3 | async-start | bytes 16384 | tf_op jit(solution)/shard_map/all_to_all | solution.py:38
  132.6 6.4 %copy-start.22 = (f32[4]{0:T(128)S(1)}, f32[4]{0:T(128)}, u32[]{:S(2)}) copy-start(f32[4]{0:T(128)} %copy-done.21) | copy-start | bytes 52
  132.6 6.5 %copy-start.9 = (f32[2,1,32,128]{3,2,1,0:T(8,128)S(1)}, f32[2,1,32,128]{3,2,1,0:T(8,128)}, u32[]{:S(2)}) copy-start(f32[2,1,32,128]{3,2,1,0:T(8,128)} %copy-done.8) | copy-start | bytes 98308
  132.6 6.5 %copy-start.11 = (f32[2,1,32,128]{3,2,1,0:T(8,128)S(1)}, f32[2,1,32,128]{3,2,1,0:T(8,128)}, u32[]{:S(2)}) copy-start(f32[2,1,32,128]{3,2,1,0:T(8,128)} %copy-done.10) | copy-start | bytes 98308
  132.6 6.5 %copy-start.13 = (f32[2,1,32,128]{3,2,1,0:T(8,128)S(1)}, f32[2,1,32,128]{3,2,1,0:T(8,128)}, u32[]{:S(2)}) copy-start(f32[2,1,32,128]{3,2,1,0:T(8,128)} %copy-done.12) | copy-start | bytes 98308
  (18 other events, 22.1 us)
where the time goes:
time: 144 us; the launch traced here: 143 us
  blocking collectives  62.4 us (43%)
  starting transfers between devices  53.3 us (37%)
  waiting for transfers between devices  9.53 us (7%)
  local copies, waits for them, and re-layouts  8.86 us (6%)
  other arithmetic  7.52 us (5%)
    all_to_all x3, blocking collectives, from_everyone(): return lax.all_to_all(copies, axis, split_axis=0, concat_axis=0, tiled=True)  62.4 us
    ppermute x8, starting transfers between devices, with_halo(): lax.ppermute(last, axis, up)  25.7 us
    ppermute x8, starting transfers between devices, with_halo(): lax.ppermute(initial, axis, [(b, a) for a, b in up])  22.4 us
    all_to_all x1, waiting for transfers between devices, from_everyone(): return lax.all_to_all(copies, axis, split_axis=0, concat_axis=0, tiled=True)  5.33 us
    all_to_all x1, starting transfers between devices, from_everyone(): return lax.all_to_all(copies, axis, split_axis=0, concat_axis=0, tiled=True)  5.13 us
    unnamed x54, local copies, waits for them, and re-layouts  3.88 us
  transfers between devices with their start and end apart: 17, of which 4 were waited for; matrix products, arithmetic and copies ran while one was open for 3% of the time, Pallas kernels for 0%

commit v1 on v0

v1 whole, which is shorter than its diff:
```python
import jax
import jax.numpy as jnp
from jax import lax
from jax.sharding import Mesh
from jax.sharding import PartitionSpec as P

GY = ("gy_0", "gy_1")
GZ = ("gz_0", "gz_1")

seed_pull = 4.0
screening = 0.05


def neighbours(last, first, axis):
    devices = lax.axis_size(axis)
    up = [(i, i + 1) for i in range(devices - 1)]
    return lax.ppermute(last, axis, up), lax.ppermute(first, axis, [(b, a) for a, b in up])


def extend(fields, widths, axis, dim):
    def face(f, w, end):
        n = f.shape[dim]
        part = lax.slice_in_dim(f, n - w if end else 0, n if end else w, axis=dim)
        other = 1 - dim
        short = fields[0].shape[other] - f.shape[other]
        return jnp.pad(part, [(short // 2, short // 2) if d == other else (0, 0) for d in range(3)])

    last = jnp.concatenate([face(f, w, True) for f, w in zip(fields, widths)], axis=dim)
    first = jnp.concatenate([face(f, w, False) for f, w in zip(fields, widths)], axis=dim)
    low, high = neighbours(last, first, axis)
    out, at = [], 0
    for f, w in zip(fields, widths):
        other = 1 - dim
        short = (fields[0].shape[other] - f.shape[other]) // 2
        a = lax.slice_in_dim(low, at, at + w, axis=dim)
        b = lax.slice_in_dim(high, at, at + w, axis=dim)
        a = lax.slice_in_dim(a, short, a.shape[other] - short, axis=other)
        b = lax.slice_in_dim(b, short, b.shape[other] - short, axis=other)
        out.append(jnp.concatenate([a, f, b], axis=dim))
        at += w
    return out


def over_copies(shard, axis):
    copies = jnp.broadcast_to(shard, (lax.axis_size(axis), *shard.shape))
    return jnp.sum(lax.all_to_all(copies, axis, split_axis=0, concat_axis=0, tiled=True), axis=0)


def harmonic(first, second):
    return 2.0 * first * second / jnp.maximum(first + second, 1e-30)


def coefficients(padded_cond, seeds):
    core = padded_cond[1:-1, 1:-1]
    along = jnp.pad(core, ((0, 0), (0, 0), (1, 1)))
    weights = (
        harmonic(core, padded_cond[2:, 1:-1]),
        harmonic(core, padded_cond[:-2, 1:-1]),
        harmonic(core, padded_cond[1:-1, 2:]),
        harmonic(core, padded_cond[1:-1, :-2]),
        harmonic(core, along[..., 2:]),
        harmonic(core, along[..., :-2]),
    )
    diagonal = weights[0] + weights[1] + weights[2] + weights[3] + weights[4] + weights[5]
    diagonal = diagonal + seed_pull * seeds + screening
    return (diagonal,) + weights


def inner(arrays, n):
    return tuple(a[n:-n, n:-n] for a in arrays)


def operate(padded, coeffs):
    field = padded[1:-1, 1:-1]
    along = jnp.pad(field, ((0, 0), (0, 0), (1, 1)))
    out = coeffs[0] * field - coeffs[1] * padded[2:, 1:-1] - coeffs[2] * padded[:-2, 1:-1]
    out = out - coeffs[3] * padded[1:-1, 2:] - coeffs[4] * padded[1:-1, :-2]
    return out - coeffs[5] * along[..., 2:] - coeffs[6] * along[..., :-2]


def edge_term(ci, cj, ui, uj, vi, vj):
    total = ci + cj
    return -2.0 * cj * cj / (total * total) * (ui - uj) * (vi - vj)


def gradient(cond_pad, prob_pad, adj_pad):
    ci = cond_pad[1:-1, 1:-1]
    ui = prob_pad[1:-1, 1:-1]
    vi = adj_pad[1:-1, 1:-1]
    out = edge_term(ci, cond_pad[2:, 1:-1], ui, prob_pad[2:, 1:-1], vi, adj_pad[2:, 1:-1])
    out = out + edge_term(ci, cond_pad[:-2, 1:-1], ui, prob_pad[:-2, 1:-1], vi, adj_pad[:-2, 1:-1])
    out = out + edge_term(ci, cond_pad[1:-1, 2:], ui, prob_pad[1:-1, 2:], vi, adj_pad[1:-1, 2:])
    out = out + edge_term(ci, cond_pad[1:-1, :-2], ui, prob_pad[1:-1, :-2], vi, adj_pad[1:-1, :-2])
    cx = jnp.pad(ci, ((0, 0), (0, 0), (1, 1)))
    ux = jnp.pad(ui, ((0, 0), (0, 0), (1, 1)))
    vx = jnp.pad(vi, ((0, 0), (0, 0), (1, 1)))
    out = out + edge_term(ci, cx[..., 2:], ui, ux[..., 2:], vi, vx[..., 2:])
    return out + edge_term(ci, cx[..., :-2], ui, ux[..., :-2], vi, vx[..., :-2])


def moments(r, v, av):
    return [jnp.sum(r * r), jnp.sum(r * v), jnp.sum(v * v), jnp.sum(v * av)]


def steps(m0, m1, m2, m3):
    a0 = m0 / m1
    new = a0 * a0 * m2 - m0
    grow = 1.0 + new / m0
    a1 = new / (grow * grow * m1 - 2.0 * grow * a0 * m2 + a0 * a0 * m3)
    return a0 + a1 * grow, -a1 * a0


def per_device(conduct, seeds, labels, start, cotangent):
    free = seeds.astype(jnp.float32)
    rhs = seed_pull * (seeds * labels).astype(jnp.float32)
    fields, widths = [conduct, start, cotangent, free, rhs], [3, 3, 2, 2, 2]
    fields = extend(fields, widths, GY, 0)
    cond, begin, cot, free, rhs = extend(fields, widths, GZ, 1)
    coeffs = coefficients(cond, free)
    resid = rhs - operate(begin, coeffs)
    near, mid = inner(coeffs, 1), inner(coeffs, 2)
    image, image_cot = operate(resid, near), operate(cot, near)
    second, second_cot = operate(image, mid), operate(image_cot, mid)
    line = jnp.stack(
        moments(resid[2:-2, 2:-2], image[1:-1, 1:-1], second)
        + moments(cot[2:-2, 2:-2], image_cot[1:-1, 1:-1], second_cot)
    )
    total = over_copies(over_copies(line, GZ), GY)
    on_r, on_v = steps(total[0], total[1], total[2], total[3])
    on_s, on_u = steps(total[4], total[5], total[6], total[7])
    prob_pad = begin[2:-2, 2:-2] + on_r * resid[1:-1, 1:-1] + on_v * image
    adj_pad = on_s * cot[1:-1, 1:-1] + on_u * image_cot
    grad_conduct = gradient(cond[2:-2, 2:-2], prob_pad, adj_pad)
    return prob_pad[1:-1, 1:-1], adj_pad[1:-1, 1:-1], grad_conduct


def solution(mesh):
    split = Mesh(mesh.devices.reshape(4, 4, 16, 2), ("gy_0", "gy_1", "gz_0", "gz_1"))
    spec = P(GY, GZ, None)
    return jax.shard_map(per_device, mesh=split, in_specs=(spec,) * 5, out_specs=(spec,) * 3, check_vma=False)
```

time: 144 us -> 92.4 us (0.64)
  starting transfers between devices: 53.3 us -> 17.3 us
  blocking collectives: 62.4 us -> 41.7 us
  between operations: 1.2 us -> 11.4 us
  waiting for transfers between devices: 9.53 us -> 4.96 us
    ppermute x16 -> x4, starting transfers between devices: 48.2 us -> 17.3 us  [the longest x2 10.8 us: neighbours(): lax.ppermute(first, axis, [(b, a) for a, b in up])]
    all_to_all x3 -> x2, blocking collectives: 62.4 us -> 41.7 us  [over_copies(): lax.all_to_all(copies, axis, split_axis=0, concat_axis=0, tiled=True)]
    all_to_all x1 -> x0, waiting for transfers between devices: 5.33 us -> none  [from_everyone(): return lax.all_to_all(copies, axis, split_axis=0, concat_axis=0, tiled=True)]
    all_to_all x1 -> x0, starting transfers between devices: 5.13 us -> none  [from_everyone(): return lax.all_to_all(copies, axis, split_axis=0, concat_axis=0, tiled=True)]
    another operation x0 -> x1, local copies, waits for them, and re-layouts: none -> 5.12 us  [per_device(): jnp.stack(moments(resid[2:-2, 2:-2], image[1:-1, 1:-1], second) + moments...]
    slice x8 -> x17, local copies, waits for them, and re-layouts: 3.38 us -> 1 us  [the longest x1 0.67 us: per_device(): on_s, on_u = steps(total[4], total[5], total[6], total[7])]
    sub x0 -> x3, other arithmetic: none -> 1.67 us  [the longest x2 1.07 us: operate(): return out - coeffs[5] * along[..., 2:] - coeffs[6] * along[..., :-2]]
    another operation x5 -> x0, other arithmetic: 1.51 us -> none  [the longest x1 1.02 us: per_device(): both_pads = jnp.stack([start_pad, jnp.zeros_like(start_pad)])]
  transfers between devices with their start and end apart: 17 -> 4, of which waited for: 4 -> 3; matrix products, arithmetic and copies ran while one was open for 3% -> 0% of each run, Pallas kernels for 0% -> 0%
where the time goes in v1:
time: 92.4 us; the launch traced here: 91.8 us
  blocking collectives  41.7 us (45%)
  starting transfers between devices  17.3 us (19%)
  between operations  11.4 us (12%)
  local copies, waits for them, and re-layouts  8.83 us (10%)
  other arithmetic  7.73 us (8%)
  waiting for transfers between devices  4.96 us (5%)
    all_to_all x2, blocking collectives, over_copies(): lax.all_to_all(copies, axis, split_axis=0, concat_axis=0, tiled=True)  41.7 us
    ppermute x2, starting transfers between devices, neighbours(): lax.ppermute(first, axis, [(b, a) for a, b in up])  10.8 us
    ppermute x2, starting transfers between devices, neighbours(): lax.ppermute(last, axis, up)  6.51 us
    another operation x1, local copies, waits for them, and re-layouts, per_device(): jnp.stack(moments(resid[2:-2, 2:-2], image[1:-1, 1:-1], second) + moments...  5.12 us
    ppermute x2, waiting for transfers between devices, neighbours(): lax.ppermute(last, axis, up)  3.85 us
    unnamed x18, local copies, waits for them, and re-layouts  2.46 us
    reduce_sum x2, other arithmetic, moments(): return [jnp.sum(r * r), jnp.sum(r * v), jnp.sum(v * v), jnp.sum(v * av)]  2.32 us
  transfers between devices with their start and end apart: 4, of which 3 were waited for; matrix products, arithmetic and copies ran while one was open for 0% of the time, Pallas kernels for 0%

profile of v1, /device:TPU:1, one launch (start us, length us, event | category | flops | bytes accessed | tf_op | source)
XLA Modules:
  0.0 91.8 jit_solution(12739580123375898529)
XLA Ops:
  0.6 0.8 slice_dynamic-update-slice_fusion.3
  1.5 1.0 %convert_element_type.25 = f32[16,32,128]{2,1,0:T(8,128)S(1)} convert(s32[16,32,128]{2,1,0:T(8,128)} %param.6) | non-fusion elementwise | flops 65536 | bytes 524288 | tf_op jit(solution)/shard_map/convert_element_type | solution.py:114
  2.6 0.9 copy-done.2
  3.6 1.4 %collective-permute-start.1 = (f32[12,32,128]{2,1,0:T(8,128)S(1)}, f32[12,32,128]{2,1,0:T(8,128)S(1)}, u32[]{:S(2)}, u32[]{:S(2)}) collective-permute-start(f32[12,32,128]{2,1,0:T(8,128)S(1)} %get-tuple-element.29), channel_id=1, source_target_pairs={{32,0},{64,32},{96,64},{128,96},{160,128},{192,160},{224,192},{256... | collective-permute-start | bytes 589832 | tf_op jit(solution)/shard_map/ppermute | solution.py:17
  5.1 4.6 %collective-permute-start = (f32[12,32,128]{2,1,0:T(8,128)S(1)}, f32[12,32,128]{2,1,0:T(8,128)S(1)}, u32[]{:S(2)}, u32[]{:S(2)}) collective-permute-start(f32[12,32,128]{2,1,0:T(8,128)S(1)} %get-tuple-element.28), channel_id=1, source_target_pairs={{0,32},{32,64},{64,96},{96,128},{128,160},{160,192},{192,224},{224... | collective-permute-start | bytes 589832 | tf_op jit(solution)/shard_map/ppermute | solution.py:17
  9.7 1.1 %collective-permute-done.1 = f32[12,32,128]{2,1,0:T(8,128)S(1)} collective-permute-done((f32[12,32,128]{2,1,0:T(8,128)S(1)}, f32[12,32,128]{2,1,0:T(8,128)S(1)}, u32[]{:S(2)}, u32[]{:S(2)}) %collective-permute-start.1) | collective-permute-done | bytes 196640 | tf_op jit(solution)/shard_map/ppermute | solution.py:17
  10.8 1.5 %collective-permute-done = f32[12,32,128]{2,1,0:T(8,128)S(1)} collective-permute-done((f32[12,32,128]{2,1,0:T(8,128)S(1)}, f32[12,32,128]{2,1,0:T(8,128)S(1)}, u32[]{:S(2)}, u32[]{:S(2)}) %collective-permute-start) | collective-permute-done | bytes 196640 | tf_op jit(solution)/shard_map/ppermute | solution.py:17
  12.5 9.3 %collective-permute-start.3 = (f32[22,12,128]{2,1,0:T(8,128)S(1)}, f32[22,12,128]{2,1,0:T(8,128)S(1)}, u32[]{:S(2)}, u32[]{:S(2)}) collective-permute-start(f32[22,12,128]{2,1,0:T(8,128)S(1)} %concatenate.68), channel_id=1, source_target_pairs={{1,0},{2,1},{3,2},{4,3},{5,4},{6,5},{7,6},{8,7},{9,8},{10,9},{11,1... | collective-permute-start | bytes 405512 | tf_op jit(solution)/shard_map/ppermute | solution.py:17
  22.0 1.9 %collective-permute-start.2 = (f32[22,12,128]{2,1,0:T(8,128)S(1)}, f32[22,12,128]{2,1,0:T(8,128)S(1)}, u32[]{:S(2)}, u32[]{:S(2)}) collective-permute-start(f32[22,12,128]{2,1,0:T(8,128)S(1)} %concatenate.67), channel_id=1, source_target_pairs={{0,1},{1,2},{2,3},{3,4},{4,5},{5,6},{6,7},{7,8},{8,9},{9,10},{10,1... | collective-permute-start | bytes 405512 | tf_op jit(solution)/shard_map/ppermute | solution.py:17
  24.0 2.4 %collective-permute-done.2 = f32[22,12,128]{2,1,0:T(8,128)S(1)} collective-permute-done((f32[22,12,128]{2,1,0:T(8,128)S(1)}, f32[22,12,128]{2,1,0:T(8,128)S(1)}, u32[]{:S(2)}, u32[]{:S(2)}) %collective-permute-start.2) | collective-permute-done | bytes 135200 | tf_op jit(solution)/shard_map/ppermute | solution.py:17
  26.4 0.1 pad_maximum_fusion
  26.6 0.7 fusion.10
  27.3 0.6 fusion.3
  28.0 0.5 fusion.13
  28.5 1.1 %multiply_reduce_fusion.4 = (f32[]{:T(128)}, f32[]{:T(128)}, f32[]{:T(128)}, f32[]{:T(128)}) fusion(f32[20,36,128]{2,1,0:T(8,128)S(1)} %fusion.3, f32[18,34,128]{2,1,0:T(8,128)S(1)} %fusion.13, f32[16,32,128]{2,1,0:T(8,128)S(1)} %slice.584, f32[20,36,128]{2,1,0:T(8,128)S(1)} %get-tuple-element.16, f32[20,36,128]{2,1,0:T(8,128)S(1)} %get-tuple-element.17, ...), kind=kLoop, calls=%fused_computation.161 | loop fusion | flops 1376252 | bytes 3670032 | tf_op jit(solution)/shard_map/reduce_sum | solution.py:102
  29.8 0.5 fusion.17
  30.3 1.2 %fusion.63 = (f32[]{:T(128)}, f32[]{:T(128)}, f32[]{:T(128)}, f32[]{:T(128)}) fusion(f32[16,32,128]{2,1,0:T(8,128)S(1)} %slice.601, f32[18,34,128]{2,1,0:T(8,128)S(1)} %fusion.17, f32[20,36,128]{2,1,0:T(8,128)S(1)} %get-tuple-element.16, f32[20,36,128]{2,1,0:T(8,128)S(1)} %get-tuple-element.17, f32[20,36,128]{2,1,0:T(8,128)S(1)} %get-tuple-element.15, ...), kind=kLoop, calls=%fused_computation.115 | loop fusion | flops 1376252 | bytes 3670032 | tf_op jit(solution)/shard_map/reduce_sum | solution.py:102
  31.5 5.1 %stack.35 = f32[8]{0:T(128)S(1)} concatenate(f32[1]{0:T(128)} %bitcast, f32[1]{0:T(128)} %bitcast.1, f32[1]{0:T(128)} %bitcast.2, f32[1]{0:T(128)} %bitcast.3, f32[1]{0:T(128)} %bitcast.4, f32[1]{0:T(128)} %bitcast.5, f32[1]{0:T(128)} %bitcast.6, f32[1]{0:T(128)} %bitcast.7), dimensions={0} | concatenate | bytes 64 | tf_op jit(solution)/shard_map/stack | solution.py:124
  36.6 25.8 %all_to_all.12 = f32[32,1,8]{2,1,0:T(1,128)S(1)} all-to-all(f32[32,1,8]{2,1,0:T(1,128)S(1)} %broadcast_in_dim.6), channel_id=1, replica_groups=mesh['gy_0'=4,'gy_1'=4,'gz_0'=16,'gz_1'=2] {'gz_0','gz_1'}, dimensions={0} | all-to-all | bytes 2048 | tf_op jit(solution)/shard_map/all_to_all | solution.py:46
  62.6 15.8 %all_to_all.13 = f32[16,1,8]{2,1,0:T(1,128)S(1)} all-to-all(f32[16,1,8]{2,1,0:T(1,128)S(1)} %broadcast_in_dim.7), channel_id=1, replica_groups=mesh['gy_0'=4,'gy_1'=4,'gz_0'=16,'gz_1'=2] {'gy_0','gy_1'}, dimensions={0} | all-to-all | bytes 1024 | tf_op jit(solution)/shard_map/all_to_all | solution.py:46
  78.4 0.7 fusion.89
  89.5 0.1 fusion.29
  89.8 0.6 copy-done.4
  90.4 1.4 %fusion.37 = f32[16,32,128]{2,1,0:T(8,128)} fusion(f32[16,32,128]{2,1,0:T(8,128)S(1)} %slice.606, f32[16,32,128]{2,1,0:T(8,128)S(1)} %slice.607, f32[18,34,128]{2,1,0:T(8,128)S(1)} %multiply_add_fusion, f32[18,34,128]{2,1,0:T(8,128)S(1)} %fusion.29, f32[16,32,128]{2,1,0:T(8,128)S(1)} %copy-done.1, f32[3,32,128]{2,1,0:T(8,128)S(1)} %get-tuple-element.45, ...), kind=kLoop, calls=%fused_computation.89 | loop fusion | flops 4390912 | bytes 3311616 | tf_op jit(solution)/shard_map/add | solution.py:98
  (47 shorter events, 1.1 us)
Async XLA Ops:
  1.5 1.0 %copy-start.3 = (s32[16,32,128]{2,1,0:T(8,128)S(1)}, s32[16,32,128]{2,1,0:T(8,128)}, u32[]{:S(2)}) copy-start(s32[16,32,128]{2,1,0:T(8,128)} %param.6) | copy-start | bytes 786436
  1.5 1.1 %copy-start.6 = (s32[16,32,128]{2,1,0:T(8,128)S(1)}, s32[16,32,128]{2,1,0:T(8,128)}, u32[]{:S(2)}) copy-start(s32[16,32,128]{2,1,0:T(8,128)} %param.7) | copy-start | bytes 786436
  2.6 0.9 %copy-start.2 = (f32[16,32,128]{2,1,0:T(8,128)S(1)}, f32[16,32,128]{2,1,0:T(8,128)}, u32[]{:S(2)}) copy-start(f32[16,32,128]{2,1,0:T(8,128)} %param.8) | copy-start | bytes 786436
  2.6 1.0 %copy-start = (f32[16,32,128]{2,1,0:T(8,128)S(1)}, f32[16,32,128]{2,1,0:T(8,128)}, u32[]{:S(2)}) copy-start(f32[16,32,128]{2,1,0:T(8,128)} %param.9) | copy-start | bytes 786436
  3.6 8.6 %copy-start.1 = (f32[16,32,128]{2,1,0:T(8,128)S(1)}, f32[16,32,128]{2,1,0:T(8,128)}, u32[]{:S(2)}) copy-start(f32[16,32,128]{2,1,0:T(8,128)} %param.5) | copy-start | bytes 786436
  3.6 7.1 %collective-permute-start.1 = (f32[12,32,128]{2,1,0:T(8,128)S(1)}, f32[12,32,128]{2,1,0:T(8,128)S(1)}, u32[]{:S(2)}, u32[]{:S(2)}) collective-permute-start(f32[12,32,128]{2,1,0:T(8,128)S(1)} %get-tuple-element.29), channel_id=1, source_target_pairs={{32,0},{64,32},{96,64},{128,96},{160,128},{192,160},{224,192},{256... | collective-permute-start | bytes 589832 | tf_op jit(solution)/shard_map/ppermute | solution.py:17
  5.1 7.2 %collective-permute-start = (f32[12,32,128]{2,1,0:T(8,128)S(1)}, f32[12,32,128]{2,1,0:T(8,128)S(1)}, u32[]{:S(2)}, u32[]{:S(2)}) collective-permute-start(f32[12,32,128]{2,1,0:T(8,128)S(1)} %get-tuple-element.28), channel_id=1, source_target_pairs={{0,32},{32,64},{64,96},{96,128},{128,160},{160,192},{192,224},{224... | collective-permute-start | bytes 589832 | tf_op jit(solution)/shard_map/ppermute | solution.py:17
  12.5 11.4 %collective-permute-start.3 = (f32[22,12,128]{2,1,0:T(8,128)S(1)}, f32[22,12,128]{2,1,0:T(8,128)S(1)}, u32[]{:S(2)}, u32[]{:S(2)}) collective-permute-start(f32[22,12,128]{2,1,0:T(8,128)S(1)} %concatenate.68), channel_id=1, source_target_pairs={{1,0},{2,1},{3,2},{4,3},{5,4},{6,5},{7,6},{8,7},{9,8},{10,9},{11,1... | collective-permute-start | bytes 405512 | tf_op jit(solution)/shard_map/ppermute | solution.py:17
  22.0 4.3 %collective-permute-start.2 = (f32[22,12,128]{2,1,0:T(8,128)S(1)}, f32[22,12,128]{2,1,0:T(8,128)S(1)}, u32[]{:S(2)}, u32[]{:S(2)}) collective-permute-start(f32[22,12,128]{2,1,0:T(8,128)S(1)} %concatenate.67), channel_id=1, source_target_pairs={{0,1},{1,2},{2,3},{3,4},{4,5},{5,6},{6,7},{7,8},{8,9},{9,10},{10,1... | collective-permute-start | bytes 405512 | tf_op jit(solution)/shard_map/ppermute | solution.py:17
  89.7 0.7 copy-start.4
  90.4 1.4 %copy-start.5 = (f32[16,32,128]{2,1,0:T(8,128)}, f32[16,32,128]{2,1,0:T(8,128)S(1)}, u32[]{:S(2)}) copy-start(f32[16,32,128]{2,1,0:T(8,128)S(1)} %slice.607) | copy-start | bytes 786436

commit v2 on v1

v2 whole, which is shorter than its diff:
```python
import jax
import jax.numpy as jnp
from jax import lax
from jax.experimental import pallas as pl
from jax.experimental.pallas import tpu as pltpu
from jax.sharding import Mesh
from jax.sharding import PartitionSpec as P

GY = ("gy_0", "gy_1")
GZ = ("gz_0", "gz_1")

seed_pull = 4.0
screening = 0.05

ROWS, COLS, LANES = 16, 32, 128
FRAME = COLS + 8
WIDTHS = (3, 3, 2, 2, 2)
PLACES = (0, 3, 6, 8, 10)
MESSAGE = 12


def neighbours(last, first, axis):
    devices = lax.axis_size(axis)
    up = [(i, i + 1) for i in range(devices - 1)]
    return lax.ppermute(last, axis, up), lax.ppermute(first, axis, [(b, a) for a, b in up])


def over_copies(shard, axis):
    copies = jnp.broadcast_to(shard, (lax.axis_size(axis), *shard.shape))
    return jnp.sum(lax.all_to_all(copies, axis, split_axis=0, concat_axis=0, tiled=True), axis=0)


def recip_sum(first, second):
    return 1.0 / jnp.maximum(first + second, 1e-30)


def harmonic(first, second):
    return 2.0 * first * second * recip_sum(first, second)


def next_z(a):
    return pltpu.roll(a, FRAME - 1, 0)


def prev_z(a):
    return pltpu.roll(a, 1, 0)


def next_x(a):
    return pltpu.roll(a, LANES - 1, 1)


def prev_x(a):
    return pltpu.roll(a, 1, 1)


class Frame:
    def __init__(self, own, low, high, side):
        self.own, self.low, self.high, self.side = own, low, high, side

    def row(self, field, y):
        w, at = WIDTHS[field], PLACES[field]
        if y < 3:
            main = self.low[at + y - (3 - w)]
        elif y >= 3 + ROWS:
            main = self.high[at + y - 3 - ROWS]
        elif field < 3:
            main = self.own[field][y - 3]
        elif field == 3:
            main = self.own[3][y - 3].astype(jnp.float32)
        else:
            main = seed_pull * (self.own[3][y - 3] * self.own[4][y - 3]).astype(jnp.float32)
        return jnp.concatenate([main, self.side[field, y]], axis=0)


def moments_kernel(k, s, c, sd, lb, low, high, side, r_out, v_out, u_out, line_out, wx, wy, wz, res):
    frame = Frame((k, s, c, sd, lb), low, high, side)
    lane = lax.broadcasted_iota(jnp.int32, (FRAME, LANES), 1)
    inside_x = jnp.where(lane < LANES - 1, 1.0, 0.0)
    for y in range(3 + ROWS + 3):
        here = frame.row(0, y)
        wz[y] = harmonic(here, next_z(here))
        wx[y] = harmonic(here, next_x(here)) * inside_x
        if y < 3 + ROWS + 2:
            wy[y] = harmonic(here, frame.row(0, y + 1))

    def apply(row, y, diagonal):
        here = row(y)
        fz = wz[y] * (here - next_z(here))
        fx = wx[y] * (here - next_x(here))
        out = diagonal * here + fz - prev_z(fz) + fx - prev_x(fx)
        return out + wy[y] * (here - row(y + 1)) + wy[y - 1] * (here - row(y - 1))

    def diagonal(y):
        return seed_pull * frame.row(3, y) + screening

    for y in range(1, 21):
        res[y] = frame.row(4, y) - apply(lambda i: frame.row(1, i), y, diagonal(y))
    for y in range(2, 20):
        d = diagonal(y)
        v_out[y - 2] = apply(lambda i: res[i], y, d)
        u_out[y - 2] = apply(lambda i: frame.row(2, i), y, d)
        r_out[y - 2] = res[y]

    sums = [jnp.zeros((8, LANES), jnp.float32) for _ in range(8)]

    def fold(a):
        return a[0:8] + a[8:16] + a[16:24] + a[24:32]

    for y in range(3, 3 + ROWS):
        d = diagonal(y)[:COLS]
        for base, krylov0, krylov1 in ((0, lambda i: res[i], v_out), (4, lambda i: frame.row(2, i), u_out)):
            r, v = krylov0(y)[:COLS], krylov1[y - 2]
            dz, dx, dy = v - next_z(v), v - next_x(v), v - krylov1[y - 1]
            v = v[:COLS]
            energy = (wz[y] * dz * dz + wx[y] * dx * dx + wy[y] * dy * dy)[:COLS] + d * v * v
            for i, term in enumerate((r * r, r * v, v * v, energy)):
                sums[base + i] = sums[base + i] + fold(term)
    line = jnp.zeros((8, LANES), jnp.float32)
    at = lax.broadcasted_iota(jnp.int32, (8, LANES), 1)
    for i, total in enumerate(sums):
        line = line + jnp.where(at == i, jnp.sum(total, axis=1, keepdims=True), 0.0)
    line_out[...] = jnp.sum(line, axis=0, keepdims=True)


def steps(m0, m1, m2, m3):
    a0 = m0 / m1
    new = a0 * a0 * m2 - m0
    grow = 1.0 + new / m0
    a1 = new / (grow * grow * m1 - 2.0 * grow * a0 * m2 + a0 * a0 * m3)
    return a0 + a1 * grow, -a1 * a0


def finish_kernel(k, s, c, sd, lb, low, high, side, r, v, u, line, prob_out, adj_out, grad_out, p, q):
    frame = Frame((k, s, c, sd, lb), low, high, side)
    total = jnp.sum(line[...], axis=0)
    at = lax.broadcasted_iota(jnp.int32, (1, LANES), 1)
    m = [jnp.sum(jnp.where(at == i, total, 0.0), axis=1, keepdims=True) for i in range(8)]
    m = [jnp.broadcast_to(one, (1, LANES)) for one in m]
    on_r, on_v = steps(*m[:4])
    on_s, on_u = steps(*m[4:])
    lane = lax.broadcasted_iota(jnp.int32, (FRAME, LANES), 1)
    inside_x = jnp.where(lane < LANES - 1, 1.0, 0.0)
    for y in range(18):
        p[y] = frame.row(1, y + 2) + on_r * r[y] + on_v * v[y]
        q[y] = on_s * frame.row(2, y + 2) + on_u * u[y]
    above = None
    for y in range(17):
        kk, pp, qq = frame.row(0, y + 2), p[y], q[y]
        kn = frame.row(0, y + 3)
        share = recip_sum(kk, kn)
        product = -2.0 * (pp - p[y + 1]) * (qq - q[y + 1]) * share * share
        before, above = above, kk * kk * product
        if y == 0:
            continue
        out = before + kn * kn * product
        kn = next_z(kk)
        share = recip_sum(kk, kn)
        product = -2.0 * (pp - next_z(pp)) * (qq - next_z(qq)) * share * share
        out = out + kn * kn * product + prev_z(kk * kk * product)
        kn = next_x(kk)
        share = recip_sum(kk, kn)
        product = -2.0 * (pp - next_x(pp)) * (qq - next_x(qq)) * share * share * inside_x
        out = out + kn * kn * product + prev_x(kk * kk * product)
        grad_out[y - 1] = out[:COLS]
        prob_out[y - 1] = pp[:COLS]
        adj_out[y - 1] = qq[:COLS]


def per_device(conduct, seeds, labels, start, cotangent):
    free = seeds.astype(jnp.float32)
    rhs = seed_pull * (seeds * labels).astype(jnp.float32)
    fields = (conduct, start, cotangent, free, rhs)
    last = jnp.concatenate([f[ROWS - w :] for f, w in zip(fields, WIDTHS)], axis=0)
    first = jnp.concatenate([f[:w] for f, w in zip(fields, WIDTHS)], axis=0)
    low, high = neighbours(last, first, GY)

    def column(field, pick):
        f, w, at = fields[field], WIDTHS[field], PLACES[field]
        rows = jnp.concatenate([pick(low[at : at + w], w), pick(f, w), pick(high[at : at + w], w)], axis=0)
        return jnp.pad(rows, ((3 - w, 3 - w), (0, 0), (0, 0)))

    last = jnp.concatenate([column(i, lambda a, w: a[:, COLS - w :]) for i in range(5)], axis=1)
    first = jnp.concatenate([column(i, lambda a, w: a[:, :w]) for i in range(5)], axis=1)
    left, right = neighbours(last, first, GZ)
    side = jnp.stack(
        [
            jnp.concatenate(
                [right[:, at : at + w], jnp.zeros((ROWS + 6, 8 - 2 * w, LANES), jnp.float32), left[:, at : at + w]],
                axis=1,
            )
            for w, at in zip(WIDTHS, PLACES)
        ]
    )
    vmem = pl.BlockSpec(memory_space=pltpu.VMEM)
    f32 = lambda *shape: jax.ShapeDtypeStruct(shape, jnp.float32)
    params = pltpu.CompilerParams(vmem_limit_bytes=48 * 1024 * 1024)
    held = (conduct, start, cotangent, seeds, labels, low, high, side)
    r, v, u, line = pl.pallas_call(
        moments_kernel,
        out_shape=(f32(18, FRAME, LANES),) * 3 + (f32(1, LANES),),
        in_specs=[vmem] * 8,
        out_specs=(vmem,) * 4,
        scratch_shapes=[pltpu.VMEM((22, FRAME, LANES), jnp.float32)] * 4,
        compiler_params=params,
        name="moments",
    )(*held)
    part = over_copies(line, GZ)
    copies = jnp.broadcast_to(part, (lax.axis_size(GY), *part.shape))
    parts = lax.all_to_all(copies, GY, split_axis=0, concat_axis=0, tiled=True)
    return pl.pallas_call(
        finish_kernel,
        out_shape=(f32(ROWS, COLS, LANES),) * 3,
        in_specs=[vmem] * 12,
        out_specs=(vmem,) * 3,
        scratch_shapes=[pltpu.VMEM((18, FRAME, LANES), jnp.float32)] * 2,
        compiler_params=params,
        name="finish",
    )(*held, r, v, u, parts)


def solution(mesh):
    split = Mesh(mesh.devices.reshape(4, 4, 16, 2), ("gy_0", "gy_1", "gz_0", "gz_1"))
    spec = P(GY, GZ, None)
    return jax.shard_map(per_device, mesh=split, in_specs=(spec,) * 5, out_specs=(spec,) * 3, check_vma=False)
```

time: 92.4 us -> 74.9 us (0.81)
  between operations: 11.4 us -> 0.86 us
  local copies, waits for them, and re-layouts: 8.83 us -> 2.52 us
  other arithmetic: 7.73 us -> 1.6 us
  Pallas kernels: 0 us -> 6.13 us
    all_to_all x2 -> x1, blocking collectives: 41.7 us -> 25.8 us  [over_copies(): lax.all_to_all(copies, axis, split_axis=0, concat_axis=0, tiled=True)]
    all_to_all x0 -> x1, blocking collectives: none -> 15.8 us  [per_device(): parts = lax.all_to_all(copies, GY, split_axis=0, concat_axis=0, tiled=True)]
    pallas_call x0 -> x2, Pallas kernels: none -> 6.13 us  [the longest x1 4.68 us: per_device(): pl.pallas_call(moments_kernel, out_shape=(f32(18, FRAME, LANES),) * 3 + (...]
    another operation x1 -> x2, local copies, waits for them, and re-layouts: 5.12 us -> 0.01 us  [per_device(): jnp.stack(moments(resid[2:-2, 2:-2], image[1:-1, 1:-1], second) + moments...]
    reduce_sum x2 -> x0, other arithmetic: 2.32 us -> none  [moments(): return [jnp.sum(r * r), jnp.sum(r * v), jnp.sum(v * v), jnp.sum(v * av)]]
    add x4 -> x0, other arithmetic: 2.31 us -> none  [the longest x1 1.44 us: gradient(): return out + edge_term(ci, cx[..., :-2], ui, ux[..., :-2], vi, vx[..., :-2])]
    sub x3 -> x0, other arithmetic: 1.67 us -> none  [the longest x2 1.07 us: operate(): return out - coeffs[5] * along[..., 2:] - coeffs[6] * along[..., :-2]]
    unnamed x18 -> x14, local copies, waits for them, and re-layouts: 2.46 us -> 1.94 us
  transfers between devices with their start and end apart: 4 -> 4, of which waited for: 3 -> 3; matrix products, arithmetic and copies ran while one was open for 0% -> 1% of each run, Pallas kernels for 0% -> 0%
where the time goes in v2:
time: 74.9 us; the launch traced here: 74.6 us
  blocking collectives  41.7 us (56%)
  starting transfers between devices  17.1 us (23%)
  Pallas kernels  6.13 us (8%)
  waiting for transfers between devices  4.69 us (6%)
  local copies, waits for them, and re-layouts  2.52 us (3%)
  other arithmetic  1.6 us (2%)
  between operations  0.86 us (1%)
    all_to_all x1, blocking collectives, over_copies(): lax.all_to_all(copies, axis, split_axis=0, concat_axis=0, tiled=True)  25.8 us
    all_to_all x1, blocking collectives, per_device(): parts = lax.all_to_all(copies, GY, split_axis=0, concat_axis=0, tiled=True)  15.8 us
    ppermute x2, starting transfers between devices, neighbours(): lax.ppermute(first, axis, [(b, a) for a, b in up])  10.6 us
    ppermute x2, starting transfers between devices, neighbours(): lax.ppermute(last, axis, up)  6.51 us
    pallas_call x1, Pallas kernels, per_device(): pl.pallas_call(moments_kernel, out_shape=(f32(18, FRAME, LANES),) * 3 + (...  4.68 us
    ppermute x2, waiting for transfers between devices, neighbours(): lax.ppermute(last, axis, up)  3.85 us
    unnamed x14, local copies, waits for them, and re-layouts  1.94 us
  transfers between devices with their start and end apart: 4, of which 3 were waited for; matrix products, arithmetic and copies ran while one was open for 1% of the time, Pallas kernels for 0%

profile of v2, /device:TPU:1, one launch (start us, length us, event | category | flops | bytes accessed | tf_op | source)
XLA Modules:
  0.0 74.6 jit_solution(9902833297508831389)
XLA Ops:
  0.7 1.0 %convert_element_type.13 = f32[16,32,128]{2,1,0:T(8,128)S(1)} convert(s32[16,32,128]{2,1,0:T(8,128)} %sd.3) | non-fusion elementwise | flops 65536 | bytes 524288 | tf_op jit(solution)/shard_map/convert_element_type | solution.py:171
  1.8 0.9 %copy-done.2 = f32[16,32,128]{2,1,0:T(8,128)S(1)} copy-done((f32[16,32,128]{2,1,0:T(8,128)S(1)}, f32[16,32,128]{2,1,0:T(8,128)}, u32[]{:S(2)}) %copy-start.2) | copy-done | bytes 262168
  2.7 0.1 copy-done.3
  2.8 0.9 %copy-done.4 = f32[16,32,128]{2,1,0:T(8,128)S(1)} copy-done((f32[16,32,128]{2,1,0:T(8,128)S(1)}, f32[16,32,128]{2,1,0:T(8,128)}, u32[]{:S(2)}) %copy-start.4) | copy-done | bytes 262168
  3.7 1.3 %collective-permute-start.1 = (f32[12,32,128]{2,1,0:T(8,128)S(1)}, f32[12,32,128]{2,1,0:T(8,128)S(1)}, u32[]{:S(2)}, u32[]{:S(2)}) collective-permute-start(f32[12,32,128]{2,1,0:T(8,128)S(1)} %get-tuple-element.21), channel_id=1, source_target_pairs={{32,0},{64,32},{96,64},{128,96},{160,128},{192,160},{224,192},{256... | collective-permute-start | bytes 589832 | tf_op jit(solution)/shard_map/ppermute | solution.py:25
  5.0 4.6 %collective-permute-start = (f32[12,32,128]{2,1,0:T(8,128)S(1)}, f32[12,32,128]{2,1,0:T(8,128)S(1)}, u32[]{:S(2)}, u32[]{:S(2)}) collective-permute-start(f32[12,32,128]{2,1,0:T(8,128)S(1)} %get-tuple-element.22), channel_id=1, source_target_pairs={{0,32},{32,64},{64,96},{96,128},{128,160},{160,192},{192,224},{224... | collective-permute-start | bytes 589832 | tf_op jit(solution)/shard_map/ppermute | solution.py:25
  9.7 0.1 pad.38.clone
  9.8 0.1 pad.32.clone
  9.9 0.8 %collective-permute-done.1.high = f32[12,32,128]{2,1,0:T(8,128)S(1)} collective-permute-done((f32[12,32,128]{2,1,0:T(8,128)S(1)}, f32[12,32,128]{2,1,0:T(8,128)S(1)}, u32[]{:S(2)}, u32[]{:S(2)}) %collective-permute-start.1) | collective-permute-done | bytes 196640 | tf_op jit(solution)/shard_map/ppermute | solution.py:25
  10.7 1.5 %collective-permute-done.low = f32[12,32,128]{2,1,0:T(8,128)S(1)} collective-permute-done((f32[12,32,128]{2,1,0:T(8,128)S(1)}, f32[12,32,128]{2,1,0:T(8,128)S(1)}, u32[]{:S(2)}, u32[]{:S(2)}) %collective-permute-start) | collective-permute-done | bytes 196640 | tf_op jit(solution)/shard_map/ppermute | solution.py:25
  12.3 0.1 concatenate.64
  12.4 9.3 %collective-permute-start.2 = (f32[22,12,128]{2,1,0:T(8,128)S(1)}, f32[22,12,128]{2,1,0:T(8,128)S(1)}, u32[]{:S(2)}, u32[]{:S(2)}) collective-permute-start(f32[22,12,128]{2,1,0:T(8,128)S(1)} %concatenate.64), channel_id=1, source_target_pairs={{1,0},{2,1},{3,2},{4,3},{5,4},{6,5},{7,6},{8,7},{9,8},{10,9},{11,1... | collective-permute-start | bytes 405512 | tf_op jit(solution)/shard_map/ppermute | solution.py:25
  21.8 0.1 concatenate.70
  21.9 1.9 %collective-permute-start.3 = (f32[22,12,128]{2,1,0:T(8,128)S(1)}, f32[22,12,128]{2,1,0:T(8,128)S(1)}, u32[]{:S(2)}, u32[]{:S(2)}) collective-permute-start(f32[22,12,128]{2,1,0:T(8,128)S(1)} %concatenate.70), channel_id=1, source_target_pairs={{0,1},{1,2},{2,3},{3,4},{4,5},{5,6},{6,7},{7,8},{8,9},{9,10},{10,1... | collective-permute-start | bytes 405512 | tf_op jit(solution)/shard_map/ppermute | solution.py:25
  23.9 2.4 %collective-permute-done.3 = f32[22,12,128]{2,1,0:T(8,128)S(1)} collective-permute-done((f32[22,12,128]{2,1,0:T(8,128)S(1)}, f32[22,12,128]{2,1,0:T(8,128)S(1)}, u32[]{:S(2)}, u32[]{:S(2)}) %collective-permute-start.3) | collective-permute-done | bytes 135200 | tf_op jit(solution)/shard_map/ppermute | solution.py:25
  26.3 0.1 fusion
  26.4 0.1 fusion.1
  26.5 0.1 fusion.2
  26.6 0.1 fusion.3
  26.7 0.1 fusion.4.side
  26.8 4.7 %moments.1 = (f32[18,40,128]{2,1,0:T(8,128)S(1)}, f32[18,40,128]{2,1,0:T(8,128)S(1)}, f32[18,40,128]{2,1,0:T(8,128)S(1)}, f32[1,128]{1,0:T(1,128)S(1)}) custom-call(f32[16,32,128]{2,1,0:T(8,128)S(1)} %copy-done.2, f32[16,32,128]{2,1,0:T(8,128)S(1)} %copy-done.3, f32[16,32,128]{2,1,0:T(8,128)S(1)} %copy-done.4, s32[16,32,128]{2,1,0:T(8,128)S(1)} %copy-done, ...), custom_call_target="tpu_custom_call" | custom-call | tf_op jit(solution)/shard_map/moments/pallas_call | solution.py:199
  31.4 25.8 %all_to_all.10 = f32[32,1,128]{2,1,0:T(1,128)S(1)} all-to-all(f32[32,1,128]{2,1,0:T(1,128)S(1)} %broadcast_in_dim.6), channel_id=1, replica_groups=mesh['gy_0'=4,'gy_1'=4,'gz_0'=16,'gz_1'=2] {'gz_0','gz_1'}, dimensions={0} | all-to-all | bytes 32768 | tf_op jit(solution)/shard_map/all_to_all | solution.py:30
  57.3 15.8 %all_to_all.11.line = f32[16,1,128]{2,1,0:T(1,128)S(1)} all-to-all(f32[16,1,128]{2,1,0:T(1,128)S(1)} %broadcast_in_dim.7), channel_id=1, replica_groups=mesh['gy_0'=4,'gy_1'=4,'gz_0'=16,'gz_1'=2] {'gy_0','gy_1'}, dimensions={0} | all-to-all | bytes 16384 | tf_op jit(solution)/shard_map/all_to_all | solution.py:210
  73.1 1.4 %finish.1 = (f32[16,32,128]{2,1,0:T(8,128)}, f32[16,32,128]{2,1,0:T(8,128)}, f32[16,32,128]{2,1,0:T(8,128)}) custom-call(f32[16,32,128]{2,1,0:T(8,128)S(1)} %copy-done.2, f32[16,32,128]{2,1,0:T(8,128)S(1)} %copy-done.3, f32[16,32,128]{2,1,0:T(8,128)S(1)} %copy-done.4, s32[16,32,128]{2,1,0:T(8,128)S(1)} %copy-done, s32[16,32,128]{2,1,0:T(8,128)S(1)} %copy-done.1, ...), custom_call_target="tpu_custom_call" | custom-call | tf_op jit(solution)/shard_map/finish/pallas_call | solution.py:211
  (38 shorter events, 0.5 us)
Async XLA Ops:
  0.6 1.1 %copy-start = (s32[16,32,128]{2,1,0:T(8,128)S(1)}, s32[16,32,128]{2,1,0:T(8,128)}, u32[]{:S(2)}) copy-start(s32[16,32,128]{2,1,0:T(8,128)} %sd.3) | copy-start | bytes 786436
  0.6 1.1 %copy-start.1 = (s32[16,32,128]{2,1,0:T(8,128)S(1)}, s32[16,32,128]{2,1,0:T(8,128)}, u32[]{:S(2)}) copy-start(s32[16,32,128]{2,1,0:T(8,128)} %lb.3) | copy-start | bytes 786436
  1.7 0.9 %copy-start.2 = (f32[16,32,128]{2,1,0:T(8,128)S(1)}, f32[16,32,128]{2,1,0:T(8,128)}, u32[]{:S(2)}) copy-start(f32[16,32,128]{2,1,0:T(8,128)} %k.3) | copy-start | bytes 786436
  1.7 1.0 %copy-start.3 = (f32[16,32,128]{2,1,0:T(8,128)S(1)}, f32[16,32,128]{2,1,0:T(8,128)}, u32[]{:S(2)}) copy-start(f32[16,32,128]{2,1,0:T(8,128)} %s.3) | copy-start | bytes 786436
  2.7 1.0 %copy-start.4 = (f32[16,32,128]{2,1,0:T(8,128)S(1)}, f32[16,32,128]{2,1,0:T(8,128)}, u32[]{:S(2)}) copy-start(f32[16,32,128]{2,1,0:T(8,128)} %c.3) | copy-start | bytes 786436
  3.7 7.0 %collective-permute-start.1 = (f32[12,32,128]{2,1,0:T(8,128)S(1)}, f32[12,32,128]{2,1,0:T(8,128)S(1)}, u32[]{:S(2)}, u32[]{:S(2)}) collective-permute-start(f32[12,32,128]{2,1,0:T(8,128)S(1)} %get-tuple-element.21), channel_id=1, source_target_pairs={{32,0},{64,32},{96,64},{128,96},{160,128},{192,160},{224,192},{256... | collective-permute-start | bytes 589832 | tf_op jit(solution)/shard_map/ppermute | solution.py:25
  5.0 7.2 %collective-permute-start = (f32[12,32,128]{2,1,0:T(8,128)S(1)}, f32[12,32,128]{2,1,0:T(8,128)S(1)}, u32[]{:S(2)}, u32[]{:S(2)}) collective-permute-start(f32[12,32,128]{2,1,0:T(8,128)S(1)} %get-tuple-element.22), channel_id=1, source_target_pairs={{0,32},{32,64},{64,96},{96,128},{128,160},{160,192},{192,224},{224... | collective-permute-start | bytes 589832 | tf_op jit(solution)/shard_map/ppermute | solution.py:25
  12.4 11.5 %collective-permute-start.2 = (f32[22,12,128]{2,1,0:T(8,128)S(1)}, f32[22,12,128]{2,1,0:T(8,128)S(1)}, u32[]{:S(2)}, u32[]{:S(2)}) collective-permute-start(f32[22,12,128]{2,1,0:T(8,128)S(1)} %concatenate.64), channel_id=1, source_target_pairs={{1,0},{2,1},{3,2},{4,3},{5,4},{6,5},{7,6},{8,7},{9,8},{10,9},{11,1... | collective-permute-start | bytes 405512 | tf_op jit(solution)/shard_map/ppermute | solution.py:25
  21.9 4.3 %collective-permute-start.3 = (f32[22,12,128]{2,1,0:T(8,128)S(1)}, f32[22,12,128]{2,1,0:T(8,128)S(1)}, u32[]{:S(2)}, u32[]{:S(2)}) collective-permute-start(f32[22,12,128]{2,1,0:T(8,128)S(1)} %concatenate.70), channel_id=1, source_target_pairs={{0,1},{1,2},{2,3},{3,4},{4,5},{5,6},{6,7},{7,8},{8,9},{9,10},{10,1... | collective-permute-start | bytes 405512 | tf_op jit(solution)/shard_map/ppermute | solution.py:25

commit v3 on v1

v3 whole, which is shorter than its diff:
```python
import jax
import jax.numpy as jnp
from jax import lax
from jax.experimental import pallas as pl
from jax.experimental.pallas import tpu as pltpu
from jax.sharding import Mesh
from jax.sharding import PartitionSpec as P

GY = ("gy_0", "gy_1")
GZ = ("gz_0", "gz_1")

seed_pull = 4.0
screening = 0.05

ROWS, COLS, LANES = 16, 32, 128
TALL = 24
PARTS = 7
ROW_MESSAGE = PARTS * COLS + 8
COL_MESSAGE = PARTS * TALL


def swap(even_pairs, odd_pairs, axis):
    n = lax.axis_size(axis)

    def pairs(begin):
        return [p for i in range(begin, n - 1, 2) for p in ((i, i + 1), (i + 1, i))]

    return lax.ppermute(even_pairs, axis, pairs(0)), lax.ppermute(odd_pairs, axis, pairs(1))


def from_all(shard, axis):
    copies = jnp.broadcast_to(shard, (lax.axis_size(axis), *shard.shape))
    return lax.all_to_all(copies, axis, split_axis=0, concat_axis=0, tiled=True)


def recip_sum(first, second):
    return 1.0 / jnp.maximum(first + second, 1e-30)


def harmonic(first, second):
    return 2.0 * first * second * recip_sum(first, second)


def after(a, axis):
    return pltpu.roll(a, a.shape[axis] - 1, axis)


def before(a, axis):
    return pltpu.roll(a, 1, axis)


def below(shape, axis, limit):
    return jnp.where(lax.broadcasted_iota(jnp.int32, shape, axis) < limit, 1.0, 0.0)


def row(ref, y):
    return ref[pl.ds(y * COLS, COLS), :]


def column(ref, z, skip=0):
    return ref[pl.ds(skip * COLS + z, ROWS, stride=COLS), :]


def within(k):
    wx = harmonic(k, after(k, 1)) * below(k.shape, 1, LANES - 1)
    wz = harmonic(k, after(k, 0)) * below(k.shape, 0, COLS - 1)
    return wx, wz


def in_row(f, wx, wz, base):
    fx = wx * (f - after(f, 1))
    fz = wz * (f - after(f, 0))
    return base * f + fx - before(fx, 1) + fz - before(fz, 0)


def base_of(seeds):
    return seed_pull * seeds.astype(jnp.float32) + screening


def pull_of(seeds, labels):
    return seed_pull * (seeds * labels).astype(jnp.float32)


def pack_kernel(odd_ref, k, s, c, sd, lb, one_out, two_out, floats, ints, sems):
    running = []
    for end in range(2):
        at = end * (ROWS - 3) * COLS
        for i, field in enumerate((k, s, c)):
            running.append((field.at[pl.ds(at, 3 * COLS)], floats.at[i, pl.ds(end * 3 * COLS, 3 * COLS)]))
        for i, field in enumerate((sd, lb)):
            running.append((field.at[pl.ds(at, 3 * COLS)], ints.at[i, pl.ds(end * 3 * COLS, 3 * COLS)]))
    running = [pltpu.make_async_copy(src, dst, sems.at[i]) for i, (src, dst) in enumerate(running)]
    for one in running:
        one.start()
    for one in running:
        one.wait()
    for slot, out in enumerate((one_out, two_out)):
        first = odd_ref[0] if slot == 0 else 1 - odd_ref[0]
        places = [pl.multiple_of((first * i + (1 - first) * (5 - i)) * COLS, COLS) for i in range(3)]
        k0, k1, k2 = [floats[0, pl.ds(p, COLS)] for p in places]
        s0, s1, s2 = [floats[1, pl.ds(p, COLS)] for p in places]
        c0, c1, _ = [floats[2, pl.ds(p, COLS)] for p in places]
        seeds0, seeds1, _ = [ints[0, pl.ds(p, COLS)] for p in places]
        labels0, labels1, _ = [ints[1, pl.ds(p, COLS)] for p in places]
        (wx0, wz0), (wx1, wz1) = within(k0), within(k1)
        w01, w12 = harmonic(k0, k1), harmonic(k1, k2)
        base0, base1 = base_of(seeds0), base_of(seeds1)
        q0 = pull_of(seeds0, labels0) - (in_row(s0, wx0, wz0, base0) + w01 * (s0 - s1))
        q1 = pull_of(seeds1, labels1) - (in_row(s1, wx1, wz1, base1) + w01 * (s1 - s0) + w12 * (s1 - s2))
        image = in_row(q0, wx0, wz0, base0) + w01 * (q0 - q1)
        image_cot = in_row(c0, wx0, wz0, base0) + w01 * (c0 - c1)
        diagonal = base0 + wx0 + before(wx0, 1) + wz0 + before(wz0, 0) + w01
        for i, part in enumerate((k0, s0, c0, q0, image, image_cot, diagonal)):
            out[pl.ds(i * COLS, COLS), :] = part
        at = lax.broadcasted_iota(jnp.int32, (8, LANES), 0)
        corner = jnp.where(at == 0, k1[0:8], k1[COLS - 8 :])
        corner = jnp.where(at == 1, before(s1[0:8], 0), corner)
        out[pl.ds(PARTS * COLS, 8), :] = jnp.where(at == 6, after(s1[COLS - 8 :], 0), corner)


def block_kernel(k, s, c, sd, lb, wx_out, wy_out, wz_out, r_out, v_out, u_out):
    for y in range(ROWS):
        here = row(k, y)
        wx, wz = within(here)
        wx_out[pl.ds(y * COLS, COLS), :] = wx
        wz_out[pl.ds(y * COLS, COLS), :] = wz
        if y < ROWS - 1:
            wy_out[pl.ds(y * COLS, COLS), :] = harmonic(here, row(k, y + 1))
    def apply(read, y):
        f = read(y)
        out = in_row(f, row(wx_out, y), row(wz_out, y), base_of(row(sd, y)))
        if y < ROWS - 1:
            out = out + row(wy_out, y) * (f - read(y + 1))
        if y > 0:
            out = out + row(wy_out, y - 1) * (f - read(y - 1))
        return out

    for y in range(ROWS):
        r_out[pl.ds(y * COLS, COLS), :] = pull_of(row(sd, y), row(lb, y)) - apply(lambda i: row(s, i), y)
        u_out[pl.ds(y * COLS, COLS), :] = apply(lambda i: row(c, i), y)
    for y in range(ROWS):
        v_out[pl.ds(y * COLS, COLS), :] = apply(lambda i: row(r_out, i), y)


def tall(own, plus1, plus2, minus2, minus1):
    at = lax.broadcasted_iota(jnp.int32, (8, LANES), 0)
    tail = jnp.where(at == 0, plus1, jnp.where(at == 7, minus1, 0.0))
    if plus2 is not None:
        tail = jnp.where(at == 1, plus2, jnp.where(at == 6, minus2, tail))
    return jnp.concatenate([own, tail], axis=0)


def rows_kernel(odd_ref, one, two, k, s, c, sd, wx, wy, wz, r_in, v_in, u_in, r, v, u, rims_out, low_out, cols_out, one_out, two_out):
    odd_row, odd_col = odd_ref[0] == 1, odd_ref[1] == 1
    kept = pl.ds(COLS, ROWS * COLS)
    r[kept, :], v[kept, :], u[kept, :] = r_in[...], v_in[...], u_in[...]

    def arrived(up, at, size):
        first, second = one[pl.ds(at, size), :], two[pl.ds(at, size), :]
        return jnp.where(odd_row, second, first) if up else jnp.where(odd_row, first, second)

    outer, corners, edges, diagonals = [], [], [], []
    for up in (False, True):
        ko, so, co, qo, image, image_cot, diagonal = [arrived(up, i * COLS, COLS) for i in range(PARTS)]
        corners.append(arrived(up, PARTS * COLS, 8))
        y, inner, inner_edge, beyond = (ROWS - 1, ROWS - 2, ROWS - 2, ROWS) if up else (0, 1, 0, -1)
        here, w = lambda a: pl.ds((a + 1) * COLS, COLS), harmonic(ko, row(k, y))
        edges.append(w)
        outer.append((ko, so, co))
        diagonals.append(diagonal + w)
        change = w * (so - row(s, y))
        q = r[here(y), :] + change
        qo = qo - change
        r[here(y), :] = q
        r[here(beyond), :] = qo
        wxo, wzo = within(ko)
        change_o = -change
        spread = wxo * after(change_o, 1) + before(wxo * change_o, 1) + wzo * after(change_o, 0) + before(wzo * change_o, 0)
        v[here(beyond), :] = image + diagonal * change_o - spread + w * (qo - q)
        u[here(beyond), :] = image_cot + w * (co - row(c, y))
        own = in_row(change, row(wx, y), row(wz, y), base_of(row(sd, y))) + row(wy, inner_edge) * change
        v[here(y), :] = v[here(y), :] + own + w * (q - qo)
        v[here(inner), :] = v[here(inner), :] - row(wy, inner_edge) * change
        u[here(y), :] = u[here(y), :] + w * (row(c, y) - co)
    for i, part in enumerate(outer[0] + outer[1]):
        rims_out[pl.ds(i * COLS, COLS), :] = part
    low_out[...] = edges[0]

    sides = []
    for right in (False, True):
        z = COLS - 1 if right else 0
        zin = z - 1 if right else 1
        pick = lambda a, z=z: a[z : z + 1]
        ck, cs = (7, 6) if right else (0, 1)
        (kl, sl, cl), (kh, sh, ch) = outer
        kc = tall(column(k, z), pick(kh), corners[1][ck : ck + 1], corners[0][ck : ck + 1], pick(kl))
        sc = tall(column(s, z), pick(sh), corners[1][cs : cs + 1], corners[0][cs : cs + 1], pick(sl))
        cc = tall(column(c, z), pick(ch), None, None, pick(cl))
        kin = tall(column(k, zin), pick(kh, zin), None, None, pick(kl, zin))
        rc, vc, uc = (
            tall(column(f, z, 1), f[pl.ds((ROWS + 1) * COLS + z, 1), :], None, None, f[pl.ds(z, 1), :])
            for f in (r, v, u)
        )
        wxc = harmonic(kc, after(kc, 1)) * below(kc.shape, 1, LANES - 1)
        wyc = harmonic(kc, after(kc, 0))
        dc = wxc + before(wxc, 1) + wyc + before(wyc, 0) + harmonic(kc, kin)
        dc = tall(dc[:ROWS] + base_of(column(sd, z)), pick(diagonals[1]), None, None, pick(diagonals[0]))
        for i, part in enumerate((kc, sc, cc, dc, kin)):
            cols_out[pl.ds((5 * right + i) * TALL, TALL), :] = part
        sides.append((kc, sc, cc, rc, vc, uc, dc))
    for i, (first, last) in enumerate(zip(*sides)):
        one_out[pl.ds(i * TALL, TALL), :] = jnp.where(odd_col, first, last)
        two_out[pl.ds(i * TALL, TALL), :] = jnp.where(odd_col, last, first)


def inner_kernel(c, sd, wx, wy, wz, low, r, v, u, sums_out):
    at = lax.broadcasted_iota(jnp.int32, (COLS, LANES), 0)
    mask = jnp.where((at >= 2) & (at < COLS - 2), 1.0, 0.0)
    mask_z = jnp.where((at >= 2) & (at < COLS - 3), 1.0, 0.0)
    sums = [jnp.zeros((COLS, LANES), jnp.float32) for _ in range(8)]
    for y in range(ROWS):
        base = base_of(row(sd, y))
        wxy, wzy = row(wx, y) * mask, row(wz, y) * mask_z
        wyy = (row(wy, y - 1) if y else low[...]) * mask
        for i, first, second in ((0, row(r, y + 1), v), (4, row(c, y), u)):
            image, under = row(second, y + 1), row(second, y)
            dx, dz, dy = image - after(image, 1), image - after(image, 0), image - under
            kept, kept_first = image * mask, first * mask
            sums[i] = sums[i] + kept_first * first
            sums[i + 1] = sums[i + 1] + kept_first * image
            sums[i + 2] = sums[i + 2] + kept * image
            sums[i + 3] = sums[i + 3] + wxy * dx * dx + wzy * dz * dz + wyy * dy * dy + base * kept * image
    for i, total in enumerate(sums):
        sums_out[pl.ds(i * 8, 8), :] = total[0:8] + total[8:16] + total[16:24] + total[24:32]


def columns_kernel(odd_ref, one, two, cols, c, sd, wz, sums, r, v, u, side_out, line_out):
    odd_col = odd_ref[1] == 1
    totals = [sums[pl.ds(i * 8, 8), :] for i in range(8)]

    def get(ref, z):
        return tall(column(ref, z, 1), ref[pl.ds((ROWS + 1) * COLS + z, 1), :], None, None, ref[pl.ds(z, 1), :])

    def gather(base, wxc, wyc, pairs, z_edges):
        for i, (first, image, z_terms) in enumerate(zip((pairs[0], pairs[2]), (pairs[1], pairs[3]), z_edges)):
            dx, dy = image - after(image, 1), image - before(image, 0)
            energy = wxc * dx * dx + before(wyc, 0) * dy * dy
            own, energy = image[:ROWS], energy[:ROWS] + base * image[:ROWS] * image[:ROWS]
            for w, other in z_terms:
                dz = own - other[:ROWS]
                energy = energy + w[:ROWS] * dz * dz
            for j, term in enumerate((first * first, first * own, own * own, energy)):
                totals[4 * i + j] = totals[4 * i + j] + term[:8] + term[8:16]

    lanes = below((TALL, LANES), 1, LANES - 1)
    for right in (False, True):
        z, zin, zdeep = (COLS - 1, COLS - 2, COLS - 3) if right else (0, 1, 2)

        def arrived(i):
            first, second = one[pl.ds(i * TALL, TALL), :], two[pl.ds(i * TALL, TALL), :]
            return jnp.where(odd_col, second, first) if right else jnp.where(odd_col, first, second)

        ko, so, co, qo, image, image_cot, diagonal = [arrived(i) for i in range(PARTS)]
        kc, sc, cc, dc, kin = [cols[pl.ds((5 * right + i) * TALL, TALL), :] for i in range(5)]
        w = harmonic(ko, kc)
        win = harmonic(kc, kin)
        change = w * (so - sc)

        def spread(kk, f):
            wxk, wyk = harmonic(kk, after(kk, 1)) * lanes, harmonic(kk, after(kk, 0))
            return (
                wxk * after(f, 1) + before(wxk * f, 1) + wyk * after(f, 0) + before(wyk * f, 0),
                wxk,
                wyk,
            )

        q = get(r, z) + change
        qo = qo - change
        own, wxc, wyc = spread(kc, change)
        change_v = dc * change - own + w * (q - qo)
        change_in = -win * change
        change_u = w * (cc - co)
        vc, vin, uc = get(v, z) + change_v, get(v, zin) + change_in, get(u, z) + change_u
        uin = get(u, zin)
        other, _, _ = spread(ko, -change)
        vo = image - diagonal * change - other + w * (qo - q)
        uo = image_cot + w * (co - cc)
        for i, part in enumerate((ko, so, co, qo, vo, uo, change, change_v, change_in, change_u)):
            side_out[pl.ds((10 * right + i) * TALL, TALL), :] = part
        wdeep = column(wz, zdeep if right else zin)
        vdeep, udeep = column(v, zdeep, 1), column(u, zdeep, 1)
        outside = ([(w, vo)], [(w, uo)]) if right else ([], [])
        gather(
            base_of(column(sd, z)),
            wxc,
            wyc,
            (q[:ROWS], vc, cc[:ROWS], uc),
            (outside[0] + [(win, vin)], outside[1] + [(win, uin)]),
        )
        gather(
            base_of(column(sd, zin)),
            harmonic(kin, after(kin, 1)) * lanes,
            harmonic(kin, after(kin, 0)),
            (column(r, zin, 1), vin, column(c, zin), uin),
            ([(wdeep, vdeep)], [(wdeep, udeep)]),
        )
    line = jnp.zeros((8, LANES), jnp.float32)
    at = lax.broadcasted_iota(jnp.int32, (8, LANES), 1)
    for i, total in enumerate(totals):
        line = line + jnp.where(at == i, jnp.sum(total, axis=1, keepdims=True), 0.0)
    line_out[...] = jnp.sum(line, axis=0, keepdims=True)


def steps(m0, m1, m2, m3):
    a0 = m0 / m1
    new = a0 * a0 * m2 - m0
    grow = 1.0 + new / m0
    a1 = new / (grow * grow * m1 - 2.0 * grow * a0 * m2 + a0 * a0 * m3)
    return a0 + a1 * grow, -a1 * a0


def finish_kernel(k, s, c, rims, side, r, v, u, line, prob_out, adj_out, grad_out, p, q):
    total = jnp.sum(line[...], axis=0)
    at = lax.broadcasted_iota(jnp.int32, (1, LANES), 1)
    m = [jnp.sum(jnp.where(at == i, total, 0.0), axis=1, keepdims=True) for i in range(8)]
    m = [jnp.broadcast_to(one, (1, LANES)) for one in m]
    on_r, on_v = steps(*m[:4])
    on_s, on_u = steps(*m[4:])

    def rows(field, ref, y):
        if 0 <= y < ROWS:
            return row(ref, y)
        return row(rims, field + (3 if y > 0 else 0))

    for y in range(-1, ROWS + 1):
        here = pl.ds((y + 1) * COLS, COLS)
        p[here, :] = rows(1, s, y) + on_r * r[here, :] + on_v * v[here, :]
        q[here, :] = on_s * rows(2, c, y) + on_u * u[here, :]
    for right in (False, True):
        z = COLS - 1 if right else 0
        change, change_v, change_in, change_u = [side[pl.ds((10 * right + i) * TALL, TALL), :] for i in range(6, 10)]
        zin = z - 1 if right else 1
        for ref, col, value in (
            (p, z, on_r * change + on_v * change_v),
            (p, zin, on_v * change_in),
            (q, z, on_u * change_u),
        ):
            here = pl.ds(COLS + col, ROWS, stride=COLS)
            ref[here, :] = ref[here, :] + value[:ROWS]
            last = pl.ds((ROWS + 1) * COLS + col, 1)
            ref[last, :] = ref[last, :] + value[ROWS : ROWS + 1]
            ref[pl.ds(col, 1), :] = ref[pl.ds(col, 1), :] + value[TALL - 1 :]
    inside_x = below((COLS, LANES), 1, LANES - 1)
    inside_z = below((COLS, LANES), 0, COLS - 1)
    up = None
    for y in range(-1, ROWS):
        kk, pp, qq = rows(0, k, y), row(p, y + 1), row(q, y + 1)
        kn = rows(0, k, y + 1)
        share = recip_sum(kk, kn)
        product = -2.0 * (pp - row(p, y + 2)) * (qq - row(q, y + 2)) * share * share
        down, up = up, kk * kk * product
        if y < 0:
            continue
        out = down + kn * kn * product
        for axis, inside in ((0, inside_z), (1, inside_x)):
            kn = after(kk, axis)
            share = recip_sum(kk, kn)
            product = -2.0 * (pp - after(pp, axis)) * (qq - after(qq, axis)) * share * share * inside
            out = out + kn * kn * product + before(kk * kk * product, axis)
        here = pl.ds(y * COLS, COLS)
        grad_out[here, :] = out
        prob_out[here, :] = pp
        adj_out[here, :] = qq
    for right in (False, True):
        z = COLS - 1 if right else 0
        ko, so, co, ro, vo, uo = [side[pl.ds((10 * right + i) * TALL, ROWS), :] for i in range(6)]
        share = recip_sum(column(k, z), ko)
        po, qo = so + on_r * ro + on_v * vo, on_s * co + on_u * uo
        product = -2.0 * (column(p, z, 1) - po) * (column(q, z, 1) - qo) * share * share
        here = pl.ds(z, ROWS, stride=COLS)
        grad_out[here, :] = grad_out[here, :] + ko * ko * product


def per_device(*arguments):
    k, sd, lb, s, c = [a.reshape(ROWS * COLS, LANES) for a in arguments]
    vmem, smem = pl.BlockSpec(memory_space=pltpu.VMEM), pl.BlockSpec(memory_space=pltpu.SMEM)
    big = pltpu.CompilerParams(vmem_limit_bytes=40 * 1024 * 1024)

    def f32(*rows):
        return tuple(jax.ShapeDtypeStruct((n, LANES), jnp.float32) for n in rows)

    def cost(us):
        return pl.CostEstimate(flops=0, bytes_accessed=int(us * 3.0e6), transcendentals=0)

    odd = jnp.stack([lax.axis_index("gy_1") % 2, lax.axis_index("gz_1") % 2]).astype(jnp.int32)
    one, two = pl.pallas_call(
        pack_kernel,
        out_shape=f32(ROW_MESSAGE, ROW_MESSAGE),
        in_specs=[smem] + [pl.BlockSpec(memory_space=pl.ANY)] * 5,
        out_specs=(vmem,) * 2,
        scratch_shapes=[
            pltpu.VMEM((3, 6 * COLS, LANES), jnp.float32),
            pltpu.VMEM((2, 6 * COLS, LANES), jnp.int32),
            pltpu.SemaphoreType.DMA((10,)),
        ],
        compiler_params=pltpu.CompilerParams(vmem_limit_bytes=60 * 1024 * 1024),
        name="pack",
    )(odd, k, s, c, sd, lb)
    one, two = swap(one, two, GY)
    block, framed = ROWS * COLS, (ROWS + 2) * COLS
    wx, wy, wz, r, v, u = pl.pallas_call(
        block_kernel,
        out_shape=f32(*(block,) * 6),
        in_specs=[vmem] * 5,
        out_specs=(vmem,) * 6,
        compiler_params=big,
        cost_estimate=cost(2.0),
        name="block",
    )(k, s, c, sd, lb)
    r, v, u, rims, low, cols, zone, ztwo = pl.pallas_call(
        rows_kernel,
        out_shape=f32(framed, framed, framed, 6 * COLS, COLS, 10 * TALL, COL_MESSAGE, COL_MESSAGE),
        in_specs=[smem] + [vmem] * 12,
        out_specs=(vmem,) * 8,
        compiler_params=big,
        cost_estimate=cost(0.5),
        name="rows",
    )(odd, one, two, k, s, c, sd, wx, wy, wz, r, v, u)
    zone, ztwo = swap(zone, ztwo, GZ)
    (sums,) = pl.pallas_call(
        inner_kernel,
        out_shape=f32(64),
        in_specs=[vmem] * 9,
        out_specs=(vmem,),
        compiler_params=big,
        cost_estimate=cost(1.0),
        name="inner",
    )(c, sd, wx, wy, wz, low, r, v, u)
    side, line = pl.pallas_call(
        columns_kernel,
        out_shape=f32(20 * TALL, 1),
        in_specs=[smem] + [vmem] * 10,
        out_specs=(vmem,) * 2,
        compiler_params=big,
        cost_estimate=cost(0.5),
        name="columns",
    )(odd, zone, ztwo, cols, c, sd, wz, sums, r, v, u)
    parts = from_all(jnp.sum(from_all(line, GZ), axis=0), GY)
    outs = pl.pallas_call(
        finish_kernel,
        out_shape=f32(block, block, block),
        in_specs=[vmem] * 9,
        out_specs=(vmem,) * 3,
        scratch_shapes=[pltpu.VMEM((framed, LANES), jnp.float32)] * 2,
        compiler_params=big,
        name="finish",
    )(k, s, c, rims, side, r, v, u, parts)
    return tuple(a.reshape(ROWS, COLS, LANES) for a in outs)


def solution(mesh):
    split = Mesh(mesh.devices.reshape(4, 4, 16, 2), ("gy_0", "gy_1", "gz_0", "gz_1"))
    spec = P(GY, GZ, None)
    return jax.shard_map(per_device, mesh=split, in_specs=(spec,) * 5, out_specs=(spec,) * 3, check_vma=False)
```

time: 92.4 us -> 70.2 us (0.76)
  between operations: 11.4 us -> 0.8 us
  Pallas kernels: 0 us -> 9.76 us
  local copies, waits for them, and re-layouts: 8.83 us -> 0.69 us
  other arithmetic: 7.73 us -> 0.61 us
  starting transfers between devices: 17.3 us -> 14.4 us
  waiting for transfers between devices: 4.96 us -> 3.39 us
  blocking collectives: 41.7 us -> 40.2 us
    pallas_call x0 -> x6, Pallas kernels: none -> 9.76 us  [the longest x1 3.12 us: per_device(): pl.pallas_call(block_kernel, out_shape=f32(*(block,) * 6), in_specs=[vmem...]
    another operation x1 -> x0, local copies, waits for them, and re-layouts: 5.12 us -> none  [per_device(): jnp.stack(moments(resid[2:-2, 2:-2], image[1:-1, 1:-1], second) + moments...]
    ppermute x4, starting transfers between devices: 17.3 us -> 14.4 us  [the longest x2 11.8 us: swap(): lax.ppermute(even_pairs, axis, pairs(0))]
    reduce_sum x4 -> x1, other arithmetic: 2.4 us -> 0.02 us  [per_device(): parts = from_all(jnp.sum(from_all(line, GZ), axis=0), GY)]
    add x4 -> x0, other arithmetic: 2.31 us -> none  [the longest x1 1.44 us: gradient(): return out + edge_term(ci, cx[..., :-2], ui, ux[..., :-2], vi, vx[..., :-2])]
    unnamed x18 -> x12, local copies, waits for them, and re-layouts: 2.46 us -> 0.67 us
    sub x3 -> x0, other arithmetic: 1.67 us -> none  [the longest x2 1.07 us: operate(): return out - coeffs[5] * along[..., 2:] - coeffs[6] * along[..., :-2]]
    ppermute x4, waiting for transfers between devices: 4.96 us -> 3.39 us  [the longest x2 3.39 us: swap(): lax.ppermute(odd_pairs, axis, pairs(1))]
  transfers between devices with their start and end apart: 4 -> 4, of which waited for: 3 -> 1; matrix products, arithmetic and copies ran while one was open for 0% -> 0% of each run, Pallas kernels for 0% -> 5%
where the time goes in v3:
time: 70.2 us; the launch traced here: 69.9 us
  blocking collectives  40.2 us (57%)
  starting transfers between devices  14.4 us (21%)
  Pallas kernels  9.76 us (14%)
  waiting for transfers between devices  3.39 us (5%)
  between operations  0.8 us (1%)
    all_to_all x2, blocking collectives, from_all(): return lax.all_to_all(copies, axis, split_axis=0, concat_axis=0, tiled=True)  40.2 us
    ppermute x2, starting transfers between devices, swap(): lax.ppermute(even_pairs, axis, pairs(0))  11.8 us
    ppermute x2, waiting for transfers between devices, swap(): lax.ppermute(odd_pairs, axis, pairs(1))  3.39 us
    pallas_call x1, Pallas kernels, per_device(): pl.pallas_call(block_kernel, out_shape=f32(*(block,) * 6), in_specs=[vmem...  3.12 us
    pallas_call x1, Pallas kernels, per_device(): pl.pallas_call(pack_kernel, out_shape=f32(ROW_MESSAGE, ROW_MESSAGE), in_s...  2.91 us
    ppermute x2, starting transfers between devices, swap(): lax.ppermute(odd_pairs, axis, pairs(1))  2.59 us
    pallas_call x1, Pallas kernels, per_device(): pl.pallas_call(finish_kernel, out_shape=f32(block, block, block), in_spec...  1.55 us
  transfers between devices with their start and end apart: 4, of which 1 were waited for; matrix products, arithmetic and copies ran while one was open for 0% of the time, Pallas kernels for 5%

profile of v3, /device:TPU:1, one launch (start us, length us, event | category | flops | bytes accessed | tf_op | source)
XLA Modules:
  0.0 69.9 jit_solution(13569242469390044938)
XLA Ops:
  0.6 0.6 pad_add_fusion.odd_ref
  1.2 0.0 copy-start.4
  1.3 2.9 %pack.1 = (f32[232,128]{1,0:T(8,128)}, f32[232,128]{1,0:T(8,128)}) custom-call(s32[2]{0:T(128)} %pad_add_fusion.odd_ref, f32[512,128]{1,0:T(8,128)} %bitcast.23, f32[512,128]{1,0:T(8,128)} %bitcast.27, f32[512,128]{1,0:T(8,128)} %bitcast.12, s32[512,128]{1,0:T(8,128)} %bitcast.18, s32[512,128]{1,0:T(8,128)} %bitcast.31), custom_call_target="tpu_custom_call" | custom-call | tf_op jit(solution)/shard_map/pack/pallas_call | solution.py:396
  4.2 3.9 %collective-permute-start = (f32[232,128]{1,0:T(8,128)}, f32[232,128]{1,0:T(8,128)S(1)}, u32[]{:S(2)}, u32[]{:S(2)}) collective-permute-start(f32[232,128]{1,0:T(8,128)} %get-tuple-element.24), channel_id=1, source_target_pairs={{0,32},{32,0},{64,96},{96,64},{128,160},{160,128},{192,224},{224,1... | collective-permute-start | bytes 356360 | tf_op jit(solution)/shard_map/ppermute | solution.py:28
  8.1 0.7 collective-permute-start.1
  8.8 0.0 copy-done
  8.8 0.0 copy-done.1
  8.8 0.0 copy-done.2
  8.8 0.0 copy-done.3
  8.9 3.1 %block.1 = (f32[512,128]{1,0:T(8,128)S(1)}, f32[512,128]{1,0:T(8,128)S(1)}, f32[512,128]{1,0:T(8,128)S(1)}, f32[512,128]{1,0:T(8,128)S(1)}, f32[512,128]{1,0:T(8,128)S(1)}, /*index=5*/f32[512,128]{1,0:T(8,128)S(1)}) custom-call(f32[512,128]{1,0:T(8,128)S(1)} %bitcast.24, f32[512,128]{1,0:T(8,128)S(1)} %bitcast.28, f32[512,128]{1,0:T(8,128)S(1)} %bitcast.13, ...), custom_call_target="tpu_custom_call" | custom-call | bytes 6000000 | tf_op jit(solution)/shard_map/block/pallas_call | solution.py:411
  12.0 0.0 collective-permute-done.one
  12.0 0.0 collective-permute-done.1.two
  12.0 0.0 copy-start.5
  12.0 0.6 copy-done.5
  12.7 0.8 %rows.1 = (f32[576,128]{1,0:T(8,128)S(1)}, f32[576,128]{1,0:T(8,128)S(1)}, f32[576,128]{1,0:T(8,128)S(1)}, f32[192,128]{1,0:T(8,128)S(1)}, f32[32,128]{1,0:T(8,1...) custom-call(s32[2]{0:T(128)S(1)} %copy-done.5, ...), custom_call_target="tpu_custom_call" | custom-call | bytes 1500000 | tf_op jit(solution)/shard_map/rows/pallas_call | solution.py:420
  13.5 7.9 %collective-permute-start.2 = (f32[168,128]{1,0:T(8,128)S(1)}, f32[168,128]{1,0:T(8,128)S(1)}, u32[]{:S(2)}, u32[]{:S(2)}) collective-permute-start(f32[168,128]{1,0:T(8,128)S(1)} %get-tuple-element.33), channel_id=1, source_target_pairs={{0,1},{1,0},{2,3},{3,2},{4,5},{5,4},{6,7},{7,6},{8,9},{9,8},{10,11... | collective-permute-start | bytes 258056 | tf_op jit(solution)/shard_map/ppermute | solution.py:28
  21.4 1.9 %collective-permute-start.3 = (f32[168,128]{1,0:T(8,128)S(1)}, f32[168,128]{1,0:T(8,128)S(1)}, u32[]{:S(2)}, u32[]{:S(2)}) collective-permute-start(f32[168,128]{1,0:T(8,128)S(1)} %get-tuple-element.34), channel_id=1, source_target_pairs={{1,2},{2,1},{3,4},{4,3},{5,6},{6,5},{7,8},{8,7},{9,10},{10,9},{11,... | collective-permute-start | bytes 258056 | tf_op jit(solution)/shard_map/ppermute | solution.py:28
  23.3 0.5 inner.1.sums
  23.8 0.0 collective-permute-done.2.one
  23.8 3.4 %collective-permute-done.3.two = f32[168,128]{1,0:T(8,128)S(1)} collective-permute-done((f32[168,128]{1,0:T(8,128)S(1)}, f32[168,128]{1,0:T(8,128)S(1)}, u32[]{:S(2)}, u32[]{:S(2)}) %collective-permute-start.3) | collective-permute-done | bytes 86048 | tf_op jit(solution)/shard_map/ppermute | solution.py:28
  27.2 0.9 %columns.1 = (f32[480,128]{1,0:T(8,128)S(1)}, f32[1,128]{1,0:T(1,128)S(1)}) custom-call(s32[2]{0:T(128)S(1)} %copy-done.5, f32[168,128]{1,0:T(8,128)S(1)} %collective-permute-done.2.one, f32[168,128]{1,0:T(8,128)S(1)} %collective-permute-done.3.two, f32[240,128]{1,0:T(8,128)S(1)} %get-tuple-element.35.cols, f32[512,128]{1,0:T(8,128)S(1)} %bitcast.16, ...), custom_call_target="tpu_custom_call" | custom-call | bytes 1500000 | tf_op jit(solution)/shard_map/columns/pallas_call | solution.py:439
  28.1 23.0 %all_to_all.10 = f32[32,1,128]{2,1,0:T(1,128)S(1)} all-to-all(f32[32,1,128]{2,1,0:T(1,128)S(1)} %broadcast_in_dim.6), channel_id=1, replica_groups=mesh['gy_0'=4,'gy_1'=4,'gz_0'=16,'gz_1'=2] {'gz_0','gz_1'}, dimensions={0} | all-to-all | bytes 32768 | tf_op jit(solution)/shard_map/all_to_all | solution.py:33
  51.2 17.2 %all_to_all.11.line = f32[16,1,128]{2,1,0:T(1,128)S(1)} all-to-all(f32[16,1,128]{2,1,0:T(1,128)S(1)} %broadcast_in_dim.7), channel_id=1, replica_groups=mesh['gy_0'=4,'gy_1'=4,'gz_0'=16,'gz_1'=2] {'gy_0','gy_1'}, dimensions={0} | all-to-all | bytes 16384 | tf_op jit(solution)/shard_map/all_to_all | solution.py:33
  68.4 1.6 %finish.1 = (f32[512,128]{1,0:T(8,128)}, f32[512,128]{1,0:T(8,128)}, f32[512,128]{1,0:T(8,128)}) custom-call(f32[512,128]{1,0:T(8,128)S(1)} %bitcast.26, f32[512,128]{1,0:T(8,128)S(1)} %bitcast.30, f32[512,128]{1,0:T(8,128)S(1)} %bitcast.17, f32[192,128]{1,0:T(8,128)S(1)} %get-tuple-element.32.rims, f32[480,128]{1,0:T(8,128)S(1)} %get-tuple-element.40.side, ...), custom_call_target="tpu_custom_call" | custom-call | tf_op jit(solution)/shard_map/finish/pallas_call | solution.py:449
  (8 shorter events, 0.0 us)
Async XLA Ops:
  1.2 7.6 %copy-start = (f32[16,32,128]{2,1,0:T(8,128)S(1)}, f32[16,32,128]{2,1,0:T(8,128)}, u32[]{:S(2)}) copy-start(f32[16,32,128]{2,1,0:T(8,128)} %param.9) | copy-start | bytes 786436
  1.2 7.6 %copy-start.1 = (s32[16,32,128]{2,1,0:T(8,128)S(1)}, s32[16,32,128]{2,1,0:T(8,128)}, u32[]{:S(2)}) copy-start(s32[16,32,128]{2,1,0:T(8,128)} %param.6) | copy-start | bytes 786436
  1.2 7.6 %copy-start.2 = (f32[16,32,128]{2,1,0:T(8,128)S(1)}, f32[16,32,128]{2,1,0:T(8,128)}, u32[]{:S(2)}) copy-start(f32[16,32,128]{2,1,0:T(8,128)} %param.5) | copy-start | bytes 786436
  1.2 7.6 %copy-start.3 = (f32[16,32,128]{2,1,0:T(8,128)S(1)}, f32[16,32,128]{2,1,0:T(8,128)}, u32[]{:S(2)}) copy-start(f32[16,32,128]{2,1,0:T(8,128)} %param.8) | copy-start | bytes 786436
  1.2 7.6 %copy-start.4 = (s32[16,32,128]{2,1,0:T(8,128)S(1)}, s32[16,32,128]{2,1,0:T(8,128)}, u32[]{:S(2)}) copy-start(s32[16,32,128]{2,1,0:T(8,128)} %param.7) | copy-start | bytes 786436
  4.2 7.8 %collective-permute-start = (f32[232,128]{1,0:T(8,128)}, f32[232,128]{1,0:T(8,128)S(1)}, u32[]{:S(2)}, u32[]{:S(2)}) collective-permute-start(f32[232,128]{1,0:T(8,128)} %get-tuple-element.24), channel_id=1, source_target_pairs={{0,32},{32,0},{64,96},{96,64},{128,160},{160,128},{192,224},{224,1... | collective-permute-start | bytes 356360 | tf_op jit(solution)/shard_map/ppermute | solution.py:28
  8.1 3.9 %collective-permute-start.1 = (f32[232,128]{1,0:T(8,128)}, f32[232,128]{1,0:T(8,128)S(1)}, u32[]{:S(2)}, u32[]{:S(2)}) collective-permute-start(f32[232,128]{1,0:T(8,128)} %get-tuple-element.25), channel_id=1, source_target_pairs={{32,64},{64,32},{96,128},{128,96},{160,192},{192,160},{224,256},{2... | collective-permute-start | bytes 356360 | tf_op jit(solution)/shard_map/ppermute | solution.py:28
  12.0 0.7 copy-start.5
  13.5 10.3 %collective-permute-start.2 = (f32[168,128]{1,0:T(8,128)S(1)}, f32[168,128]{1,0:T(8,128)S(1)}, u32[]{:S(2)}, u32[]{:S(2)}) collective-permute-start(f32[168,128]{1,0:T(8,128)S(1)} %get-tuple-element.33), channel_id=1, source_target_pairs={{0,1},{1,0},{2,3},{3,2},{4,5},{5,4},{6,7},{7,6},{8,9},{9,8},{10,11... | collective-permute-start | bytes 258056 | tf_op jit(solution)/shard_map/ppermute | solution.py:28
  21.4 5.8 %collective-permute-start.3 = (f32[168,128]{1,0:T(8,128)S(1)}, f32[168,128]{1,0:T(8,128)S(1)}, u32[]{:S(2)}, u32[]{:S(2)}) collective-permute-start(f32[168,128]{1,0:T(8,128)S(1)} %get-tuple-element.34), channel_id=1, source_target_pairs={{1,2},{2,1},{3,4},{4,3},{5,6},{6,5},{7,8},{8,7},{9,10},{10,9},{11,... | collective-permute-start | bytes 258056 | tf_op jit(solution)/shard_map/ppermute | solution.py:28

commit v4 on v3

--- a/solution.py
+++ b/solution.py
@@ -25,7 +25,8 @@
     def pairs(begin):
         return [p for i in range(begin, n - 1, 2) for p in ((i, i + 1), (i + 1, i))]
 
-    return lax.ppermute(even_pairs, axis, pairs(0)), lax.ppermute(odd_pairs, axis, pairs(1))
+    odd_pairs = lax.ppermute(odd_pairs, axis, pairs(1))
+    return lax.ppermute(even_pairs, axis, pairs(0)), odd_pairs
 
 
 def from_all(shard, axis):
@@ -81,7 +82,12 @@
     return seed_pull * (seeds * labels).astype(jnp.float32)
 
 
-def pack_kernel(odd_ref, k, s, c, sd, lb, one_out, two_out, floats, ints, sems):
+def is_odd(axis):
+    return lax.rem(lax.axis_index(axis), 2) == 1
+
+
+def pack_kernel(k, s, c, sd, lb, two_out, one_out, floats, ints, sems):
+    odd_row = lax.rem(lax.axis_index("gy_1"), 2)
     running = []
     for end in range(2):
         at = end * (ROWS - 3) * COLS
@@ -95,7 +101,7 @@
     for one in running:
         one.wait()
     for slot, out in enumerate((one_out, two_out)):
-        first = odd_ref[0] if slot == 0 else 1 - odd_ref[0]
+        first = odd_row if slot == 0 else 1 - odd_row
         places = [pl.multiple_of((first * i + (1 - first) * (5 - i)) * COLS, COLS) for i in range(3)]
         k0, k1, k2 = [floats[0, pl.ds(p, COLS)] for p in places]
         s0, s1, s2 = [floats[1, pl.ds(p, COLS)] for p in places]
@@ -150,8 +156,8 @@
     return jnp.concatenate([own, tail], axis=0)
 
 
-def rows_kernel(odd_ref, one, two, k, s, c, sd, wx, wy, wz, r_in, v_in, u_in, r, v, u, rims_out, low_out, cols_out, one_out, two_out):
-    odd_row, odd_col = odd_ref[0] == 1, odd_ref[1] == 1
+def rows_kernel(two, one, k, s, c, sd, wx, wy, wz, r_in, v_in, u_in, r, v, u, rims_out, low_out, cols_out, two_out, one_out):
+    odd_row, odd_col = is_odd("gy_1"), is_odd("gz_1")
     kept = pl.ds(COLS, ROWS * COLS)
     r[kept, :], v[kept, :], u[kept, :] = r_in[...], v_in[...], u_in[...]
 
@@ -234,8 +240,8 @@
         sums_out[pl.ds(i * 8, 8), :] = total[0:8] + total[8:16] + total[16:24] + total[24:32]
 
 
-def columns_kernel(odd_ref, one, two, cols, c, sd, wz, sums, r, v, u, side_out, line_out):
-    odd_col = odd_ref[1] == 1
+def columns_kernel(two, one, cols, c, sd, wz, sums, r, v, u, side_out, line_out):
+    odd_col = is_odd("gz_1")
     totals = [sums[pl.ds(i * 8, 8), :] for i in range(8)]
 
     def get(ref, z):
@@ -383,7 +389,7 @@
 
 def per_device(*arguments):
     k, sd, lb, s, c = [a.reshape(ROWS * COLS, LANES) for a in arguments]
-    vmem, smem = pl.BlockSpec(memory_space=pltpu.VMEM), pl.BlockSpec(memory_space=pltpu.SMEM)
+    vmem = pl.BlockSpec(memory_space=pltpu.VMEM)
     big = pltpu.CompilerParams(vmem_limit_bytes=40 * 1024 * 1024)
 
     def f32(*rows):
@@ -392,11 +398,10 @@
     def cost(us):
         return pl.CostEstimate(flops=0, bytes_accessed=int(us * 3.0e6), transcendentals=0)
 
-    odd = jnp.stack([lax.axis_index("gy_1") % 2, lax.axis_index("gz_1") % 2]).astype(jnp.int32)
-    one, two = pl.pallas_call(
+    two, one = pl.pallas_call(
         pack_kernel,
         out_shape=f32(ROW_MESSAGE, ROW_MESSAGE),
-        in_specs=[smem] + [pl.BlockSpec(memory_space=pl.ANY)] * 5,
+        in_specs=[pl.BlockSpec(memory_space=pl.ANY)] * 5,
         out_specs=(vmem,) * 2,
         scratch_shapes=[
             pltpu.VMEM((3, 6 * COLS, LANES), jnp.float32),
@@ -405,7 +410,7 @@
         ],
         compiler_params=pltpu.CompilerParams(vmem_limit_bytes=60 * 1024 * 1024),
         name="pack",
-    )(odd, k, s, c, sd, lb)
+    )(k, s, c, sd, lb)
     one, two = swap(one, two, GY)
     block, framed = ROWS * COLS, (ROWS + 2) * COLS
     wx, wy, wz, r, v, u = pl.pallas_call(
@@ -417,15 +422,15 @@
         cost_estimate=cost(2.0),
         name="block",
     )(k, s, c, sd, lb)
-    r, v, u, rims, low, cols, zone, ztwo = pl.pallas_call(
+    r, v, u, rims, low, cols, ztwo, zone = pl.pallas_call(
         rows_kernel,
         out_shape=f32(framed, framed, framed, 6 * COLS, COLS, 10 * TALL, COL_MESSAGE, COL_MESSAGE),
-        in_specs=[smem] + [vmem] * 12,
+        in_specs=[vmem] * 12,
         out_specs=(vmem,) * 8,
         compiler_params=big,
         cost_estimate=cost(0.5),
         name="rows",
-    )(odd, one, two, k, s, c, sd, wx, wy, wz, r, v, u)
+    )(two, one, k, s, c, sd, wx, wy, wz, r, v, u)
     zone, ztwo = swap(zone, ztwo, GZ)
     (sums,) = pl.pallas_call(
         inner_kernel,
@@ -439,12 +444,12 @@
     side, line = pl.pallas_call(
         columns_kernel,
         out_shape=f32(20 * TALL, 1),
-        in_specs=[smem] + [vmem] * 10,
+        in_specs=[vmem] * 10,
         out_specs=(vmem,) * 2,
         compiler_params=big,
         cost_estimate=cost(0.5),
         name="columns",
-    )(odd, zone, ztwo, cols, c, sd, wz, sums, r, v, u)
+    )(ztwo, zone, cols, c, sd, wz, sums, r, v, u)
     parts = from_all(jnp.sum(from_all(line, GZ), axis=0), GY)
     outs = pl.pallas_call(
         finish_kernel,

time: 70.2 us -> 63.5 us (0.905)
  waiting for transfers between devices: 3.39 us -> 0.57 us
  Pallas kernels: 9.76 us -> 7.97 us
    ppermute x4, waiting for transfers between devices: 3.39 us -> 0.57 us  [the longest x2 0.57 us: swap(): return (lax.ppermute(even_pairs, axis, pairs(0)), odd_pairs)]
    pallas_call x1, Pallas kernels: 2.91 us -> 2.19 us  [per_device(): pl.pallas_call(pack_kernel, out_shape=f32(ROW_MESSAGE, ROW_MESSAGE), in_s...]
  transfers between devices with their start and end apart: 4 -> 4, of which waited for: 1 -> 1; matrix products, arithmetic and copies ran while one was open for 0% -> 0% of each run, Pallas kernels for 5% -> 6%
where the time goes in v4:
time: 63.5 us; the launch traced here: 63.2 us
  blocking collectives  40 us (63%)
  starting transfers between devices  13.8 us (22%)
  Pallas kernels  7.97 us (13%)
  between operations  0.81 us (1%)
    all_to_all x2, blocking collectives, from_all(): return lax.all_to_all(copies, axis, split_axis=0, concat_axis=0, tiled=True)  40 us
    ppermute x2, starting transfers between devices, swap(): return (lax.ppermute(even_pairs, axis, pairs(0)), odd_pairs)  8.51 us
    ppermute x2, starting transfers between devices, swap(): odd_pairs = lax.ppermute(odd_pairs, axis, pairs(1))  5.33 us
    pallas_call x1, Pallas kernels, per_device(): pl.pallas_call(block_kernel, out_shape=f32(*(block,) * 6), in_specs=[vmem...  3.12 us
    pallas_call x1, Pallas kernels, per_device(): pl.pallas_call(pack_kernel, out_shape=f32(ROW_MESSAGE, ROW_MESSAGE), in_s...  2.19 us
    pallas_call x1, Pallas kernels, per_device(): pl.pallas_call(finish_kernel, out_shape=f32(block, block, block), in_spec...  1.55 us
  transfers between devices with their start and end apart: 4, of which 1 were waited for; matrix products, arithmetic and copies ran while one was open for 0% of the time, Pallas kernels for 6%

profile of v4, /device:TPU:1, one launch (start us, length us, event | category | flops | bytes accessed | tf_op | source)
XLA Modules:
  0.0 63.2 jit_solution(11884535619662282542)
XLA Ops:
  0.6 0.0 copy-start
  0.6 0.0 copy-start.1
  0.7 0.0 copy-start.2
  0.7 0.0 copy-start.3
  0.7 0.0 copy-start.4
  0.7 2.2 %pack.1 = (f32[232,128]{1,0:T(8,128)}, f32[232,128]{1,0:T(8,128)}) custom-call(f32[512,128]{1,0:T(8,128)} %bitcast.21, f32[512,128]{1,0:T(8,128)} %bitcast.25, f32[512,128]{1,0:T(8,128)} %bitcast.10, s32[512,128]{1,0:T(8,128)} %bitcast.16, s32[512,128]{1,0:T(8,128)} %bitcast.29), custom_call_target="tpu_custom_call" | custom-call | tf_op jit(solution)/shard_map/pack/pallas_call | solution.py:401
  2.9 0.7 %collective-permute-start = (f32[232,128]{1,0:T(8,128)}, f32[232,128]{1,0:T(8,128)S(1)}, u32[]{:S(2)}, u32[]{:S(2)}) collective-permute-start(f32[232,128]{1,0:T(8,128)} %get-tuple-element.24), channel_id=1, source_target_pairs={{32,64},{64,32},{96,128},{128,96},{160,192},{192,160},{224,256},{2... | collective-permute-start | bytes 356360 | tf_op jit(solution)/shard_map/ppermute | solution.py:28
  3.6 6.4 %collective-permute-start.1 = (f32[232,128]{1,0:T(8,128)}, f32[232,128]{1,0:T(8,128)S(1)}, u32[]{:S(2)}, u32[]{:S(2)}) collective-permute-start(f32[232,128]{1,0:T(8,128)} %get-tuple-element.25), channel_id=1, source_target_pairs={{0,32},{32,0},{64,96},{96,64},{128,160},{160,128},{192,224},{224,1... | collective-permute-start | bytes 356360 | tf_op jit(solution)/shard_map/ppermute | solution.py:29
  10.0 0.0 copy-done
  10.0 0.0 copy-done.1
  10.0 0.0 copy-done.2
  10.0 3.1 %block.1 = (f32[512,128]{1,0:T(8,128)S(1)}, f32[512,128]{1,0:T(8,128)S(1)}, f32[512,128]{1,0:T(8,128)S(1)}, f32[512,128]{1,0:T(8,128)S(1)}, f32[512,128]{1,0:T(8,128)S(1)}, /*index=5*/f32[512,128]{1,0:T(8,128)S(1)}) custom-call(f32[512,128]{1,0:T(8,128)S(1)} %bitcast.22, f32[512,128]{1,0:T(8,128)S(1)} %bitcast.26, f32[512,128]{1,0:T(8,128)S(1)} %bitcast.11, ...), custom_call_target="tpu_custom_call" | custom-call | bytes 6000000 | tf_op jit(solution)/shard_map/block/pallas_call | solution.py:416
  13.1 0.0 collective-permute-done.two
  13.2 0.0 collective-permute-done.1.one
  13.2 0.3 rows.1
  13.4 4.7 %collective-permute-start.2 = (f32[168,128]{1,0:T(8,128)S(1)}, f32[168,128]{1,0:T(8,128)S(1)}, u32[]{:S(2)}, u32[]{:S(2)}) collective-permute-start(f32[168,128]{1,0:T(8,128)S(1)} %get-tuple-element.33), channel_id=1, source_target_pairs={{1,2},{2,1},{3,4},{4,3},{5,6},{6,5},{7,8},{8,7},{9,10},{10,9},{11,... | collective-permute-start | bytes 258056 | tf_op jit(solution)/shard_map/ppermute | solution.py:28
  18.1 2.1 %collective-permute-start.3 = (f32[168,128]{1,0:T(8,128)S(1)}, f32[168,128]{1,0:T(8,128)S(1)}, u32[]{:S(2)}, u32[]{:S(2)}) collective-permute-start(f32[168,128]{1,0:T(8,128)S(1)} %get-tuple-element.34), channel_id=1, source_target_pairs={{0,1},{1,0},{2,3},{3,2},{4,5},{5,4},{6,7},{7,6},{8,9},{9,8},{10,11... | collective-permute-start | bytes 258056 | tf_op jit(solution)/shard_map/ppermute | solution.py:29
  20.2 0.5 inner.1.sums
  20.7 0.0 collective-permute-done.2.two
  20.7 0.6 collective-permute-done.3.one
  21.3 0.4 columns.1
  21.7 27.2 %all_to_all.10 = f32[32,1,128]{2,1,0:T(1,128)S(1)} all-to-all(f32[32,1,128]{2,1,0:T(1,128)S(1)} %broadcast_in_dim.6), channel_id=1, replica_groups=mesh['gy_0'=4,'gy_1'=4,'gz_0'=16,'gz_1'=2] {'gz_0','gz_1'}, dimensions={0} | all-to-all | bytes 32768 | tf_op jit(solution)/shard_map/all_to_all | solution.py:34
  48.9 12.7 %all_to_all.11.line = f32[16,1,128]{2,1,0:T(1,128)S(1)} all-to-all(f32[16,1,128]{2,1,0:T(1,128)S(1)} %broadcast_in_dim.7), channel_id=1, replica_groups=mesh['gy_0'=4,'gy_1'=4,'gz_0'=16,'gz_1'=2] {'gy_0','gy_1'}, dimensions={0} | all-to-all | bytes 16384 | tf_op jit(solution)/shard_map/all_to_all | solution.py:34
  61.7 1.6 %finish.1 = (f32[512,128]{1,0:T(8,128)}, f32[512,128]{1,0:T(8,128)}, f32[512,128]{1,0:T(8,128)}) custom-call(f32[512,128]{1,0:T(8,128)S(1)} %bitcast.24, f32[512,128]{1,0:T(8,128)S(1)} %bitcast.28, f32[512,128]{1,0:T(8,128)S(1)} %bitcast.15, f32[192,128]{1,0:T(8,128)S(1)} %get-tuple-element.32.rims, f32[480,128]{1,0:T(8,128)S(1)} %get-tuple-element.40.side, ...), custom_call_target="tpu_custom_call" | custom-call | tf_op jit(solution)/shard_map/finish/pallas_call | solution.py:454
  (5 shorter events, 0.0 us)
Async XLA Ops:
  0.6 9.3 %copy-start = (f32[16,32,128]{2,1,0:T(8,128)S(1)}, f32[16,32,128]{2,1,0:T(8,128)}, u32[]{:S(2)}) copy-start(f32[16,32,128]{2,1,0:T(8,128)} %param.9) | copy-start | bytes 786436
  0.6 9.3 %copy-start.1 = (s32[16,32,128]{2,1,0:T(8,128)S(1)}, s32[16,32,128]{2,1,0:T(8,128)}, u32[]{:S(2)}) copy-start(s32[16,32,128]{2,1,0:T(8,128)} %param.6) | copy-start | bytes 786436
  0.7 9.3 %copy-start.2 = (f32[16,32,128]{2,1,0:T(8,128)S(1)}, f32[16,32,128]{2,1,0:T(8,128)}, u32[]{:S(2)}) copy-start(f32[16,32,128]{2,1,0:T(8,128)} %param.5) | copy-start | bytes 786436
  0.7 9.3 %copy-start.3 = (f32[16,32,128]{2,1,0:T(8,128)S(1)}, f32[16,32,128]{2,1,0:T(8,128)}, u32[]{:S(2)}) copy-start(f32[16,32,128]{2,1,0:T(8,128)} %param.8) | copy-start | bytes 786436
  0.7 9.3 %copy-start.4 = (s32[16,32,128]{2,1,0:T(8,128)S(1)}, s32[16,32,128]{2,1,0:T(8,128)}, u32[]{:S(2)}) copy-start(s32[16,32,128]{2,1,0:T(8,128)} %param.7) | copy-start | bytes 786436
  2.9 10.3 %collective-permute-start = (f32[232,128]{1,0:T(8,128)}, f32[232,128]{1,0:T(8,128)S(1)}, u32[]{:S(2)}, u32[]{:S(2)}) collective-permute-start(f32[232,128]{1,0:T(8,128)} %get-tuple-element.24), channel_id=1, source_target_pairs={{32,64},{64,32},{96,128},{128,96},{160,192},{192,160},{224,256},{2... | collective-permute-start | bytes 356360 | tf_op jit(solution)/shard_map/ppermute | solution.py:28
  3.6 9.6 %collective-permute-start.1 = (f32[232,128]{1,0:T(8,128)}, f32[232,128]{1,0:T(8,128)S(1)}, u32[]{:S(2)}, u32[]{:S(2)}) collective-permute-start(f32[232,128]{1,0:T(8,128)} %get-tuple-element.25), channel_id=1, source_target_pairs={{0,32},{32,0},{64,96},{96,64},{128,160},{160,128},{192,224},{224,1... | collective-permute-start | bytes 356360 | tf_op jit(solution)/shard_map/ppermute | solution.py:29
  13.4 7.3 %collective-permute-start.2 = (f32[168,128]{1,0:T(8,128)S(1)}, f32[168,128]{1,0:T(8,128)S(1)}, u32[]{:S(2)}, u32[]{:S(2)}) collective-permute-start(f32[168,128]{1,0:T(8,128)S(1)} %get-tuple-element.33), channel_id=1, source_target_pairs={{1,2},{2,1},{3,4},{4,3},{5,6},{6,5},{7,8},{8,7},{9,10},{10,9},{11,... | collective-permute-start | bytes 258056 | tf_op jit(solution)/shard_map/ppermute | solution.py:28
  18.1 3.2 %collective-permute-start.3 = (f32[168,128]{1,0:T(8,128)S(1)}, f32[168,128]{1,0:T(8,128)S(1)}, u32[]{:S(2)}, u32[]{:S(2)}) collective-permute-start(f32[168,128]{1,0:T(8,128)S(1)} %get-tuple-element.34), channel_id=1, source_target_pairs={{0,1},{1,0},{2,3},{3,2},{4,5},{5,4},{6,7},{7,6},{8,9},{9,8},{10,11... | collective-permute-start | bytes 258056 | tf_op jit(solution)/shard_map/ppermute | solution.py:29

commit v5 on v4

--- a/solution.py
+++ b/solution.py
@@ -17,6 +17,7 @@
 PARTS = 7
 ROW_MESSAGE = PARTS * COLS + 8
 COL_MESSAGE = PARTS * TALL
+CHUNK = 4
 
 
 def swap(even_pairs, odd_pairs, axis):
@@ -124,14 +125,47 @@
         out[pl.ds(PARTS * COLS, 8), :] = jnp.where(at == 6, after(s1[COLS - 8 :], 0), corner)
 
 
-def block_kernel(k, s, c, sd, lb, wx_out, wy_out, wz_out, r_out, v_out, u_out):
+def edge(here, there, inside=None):
+    share = recip_sum(here, there)
+    if inside is not None:
+        share = share * inside
+    return 2.0 * here * there * share, share
+
+
+def block_kernel(*refs):
+    far, (k, s, c, sd, wx_out, wy_out, wz_out, r_out, v_out, u_out, shares_out, lb, sems) = refs[:5], refs[5:]
+    coming = [
+        [
+            pltpu.make_async_copy(a.at[pl.ds(at, CHUNK * COLS)], b.at[pl.ds(at, CHUNK * COLS)], sems.at[i, at // (CHUNK * COLS)])
+            for at in range(0, ROWS * COLS, CHUNK * COLS)
+        ]
+        for i, (a, b) in enumerate(zip(far, (k, s, c, sd, lb)))
+    ]
+    for chunks in coming:
+        for chunk in chunks:
+            chunk.start()
+
+    def need(y, *fields):
+        if y < ROWS and y % CHUNK == 0:
+            for i in fields:
+                coming[i][y // CHUNK].wait()
+
+    inside_x = below((COLS, LANES), 1, LANES - 1)
+    inside_z = below((COLS, LANES), 0, COLS - 1)
+    need(0, 0)
     for y in range(ROWS):
+        need(y + 1, 0)
         here = row(k, y)
-        wx, wz = within(here)
-        wx_out[pl.ds(y * COLS, COLS), :] = wx
-        wz_out[pl.ds(y * COLS, COLS), :] = wz
+        edges = [
+            (wx_out, edge(here, after(here, 1), inside_x)),
+            (wz_out, edge(here, after(here, 0), inside_z)),
+        ]
         if y < ROWS - 1:
-            wy_out[pl.ds(y * COLS, COLS), :] = harmonic(here, row(k, y + 1))
+            edges.append((wy_out, edge(here, row(k, y + 1))))
+        for i, (out, (w, share)) in enumerate(edges):
+            out[pl.ds(y * COLS, COLS), :] = w
+            shares_out[pl.ds((i * ROWS + y) * COLS, COLS), :] = share
+
     def apply(read, y):
         f = read(y)
         out = in_row(f, row(wx_out, y), row(wz_out, y), base_of(row(sd, y)))
@@ -141,7 +175,9 @@
             out = out + row(wy_out, y - 1) * (f - read(y - 1))
         return out
 
+    need(0, 1, 2, 3, 4)
     for y in range(ROWS):
+        need(y + 1, 1, 2, 3, 4)
         r_out[pl.ds(y * COLS, COLS), :] = pull_of(row(sd, y), row(lb, y)) - apply(lambda i: row(s, i), y)
         u_out[pl.ds(y * COLS, COLS), :] = apply(lambda i: row(c, i), y)
     for y in range(ROWS):
@@ -156,7 +192,7 @@
     return jnp.concatenate([own, tail], axis=0)
 
 
-def rows_kernel(two, one, k, s, c, sd, wx, wy, wz, r_in, v_in, u_in, r, v, u, rims_out, low_out, cols_out, two_out, one_out):
+def rows_kernel(two, one, k, s, c, sd, wx, wy, wz, r_in, v_in, u_in, r, v, u, low_out, cols_out, two_out, one_out):
     odd_row, odd_col = is_odd("gy_1"), is_odd("gz_1")
     kept = pl.ds(COLS, ROWS * COLS)
     r[kept, :], v[kept, :], u[kept, :] = r_in[...], v_in[...], u_in[...]
@@ -189,7 +225,7 @@
         v[here(inner), :] = v[here(inner), :] - row(wy, inner_edge) * change
         u[here(y), :] = u[here(y), :] + w * (row(c, y) - co)
     for i, part in enumerate(outer[0] + outer[1]):
-        rims_out[pl.ds(i * COLS, COLS), :] = part
+        cols_out[pl.ds(10 * TALL + i * COLS, COLS), :] = part
     low_out[...] = edges[0]
 
     sides = []
@@ -325,7 +361,7 @@
     return a0 + a1 * grow, -a1 * a0
 
 
-def finish_kernel(k, s, c, rims, side, r, v, u, line, prob_out, adj_out, grad_out, p, q):
+def finish_kernel(k, s, c, shares, cols, side, r, v, u, line, prob_out, adj_out, grad_out, p, q, grad, sems):
     total = jnp.sum(line[...], axis=0)
     at = lax.broadcasted_iota(jnp.int32, (1, LANES), 1)
     m = [jnp.sum(jnp.where(at == i, total, 0.0), axis=1, keepdims=True) for i in range(8)]
@@ -336,7 +372,7 @@
     def rows(field, ref, y):
         if 0 <= y < ROWS:
             return row(ref, y)
-        return row(rims, field + (3 if y > 0 else 0))
+        return cols[pl.ds(10 * TALL + (field + (3 if y > 0 else 0)) * COLS, COLS), :]
 
     for y in range(-1, ROWS + 1):
         here = pl.ds((y + 1) * COLS, COLS)
@@ -356,35 +392,53 @@
             last = pl.ds((ROWS + 1) * COLS + col, 1)
             ref[last, :] = ref[last, :] + value[ROWS : ROWS + 1]
             ref[pl.ds(col, 1), :] = ref[pl.ds(col, 1), :] + value[TALL - 1 :]
-    inside_x = below((COLS, LANES), 1, LANES - 1)
-    inside_z = below((COLS, LANES), 0, COLS - 1)
+    own = pl.ds(COLS, ROWS * COLS)
+    sent = [
+        pltpu.make_async_copy(p.at[own], prob_out, sems.at[0]),
+        pltpu.make_async_copy(q.at[own], adj_out, sems.at[1]),
+    ]
+    for copy in sent:
+        copy.start()
+    outer = []
+    for right in (False, True):
+        z = COLS - 1 if right else 0
+        ko, so, co, ro, vo, uo = [side[pl.ds((10 * right + i) * TALL, ROWS), :] for i in range(6)]
+        share = ko * recip_sum(column(k, z), ko)
+        po, qo = so + on_r * ro + on_v * vo, on_s * co + on_u * uo
+        outer.append(-2.0 * (column(p, z, 1) - po) * (column(q, z, 1) - qo) * share * share)
+
+    def share_of(i, y):
+        return shares[pl.ds((i * ROWS + y) * COLS, COLS), :]
+
+    def gives(kk, kn, share, product):
+        to_here, to_there = kn * share, kk * share
+        return to_here * to_here * product, to_there * to_there * product
+
     up = None
     for y in range(-1, ROWS):
         kk, pp, qq = rows(0, k, y), row(p, y + 1), row(q, y + 1)
         kn = rows(0, k, y + 1)
-        share = recip_sum(kk, kn)
-        product = -2.0 * (pp - row(p, y + 2)) * (qq - row(q, y + 2)) * share * share
-        down, up = up, kk * kk * product
+        share = share_of(2, y) if 0 <= y < ROWS - 1 else recip_sum(kk, kn)
+        here, there = gives(kk, kn, share, -2.0 * (pp - row(p, y + 2)) * (qq - row(q, y + 2)))
+        down, up = up, there
         if y < 0:
             continue
-        out = down + kn * kn * product
-        for axis, inside in ((0, inside_z), (1, inside_x)):
-            kn = after(kk, axis)
-            share = recip_sum(kk, kn)
-            product = -2.0 * (pp - after(pp, axis)) * (qq - after(qq, axis)) * share * share * inside
-            out = out + kn * kn * product + before(kk * kk * product, axis)
-        here = pl.ds(y * COLS, COLS)
-        grad_out[here, :] = out
-        prob_out[here, :] = pp
-        adj_out[here, :] = qq
-    for right in (False, True):
-        z = COLS - 1 if right else 0
-        ko, so, co, ro, vo, uo = [side[pl.ds((10 * right + i) * TALL, ROWS), :] for i in range(6)]
-        share = recip_sum(column(k, z), ko)
-        po, qo = so + on_r * ro + on_v * vo, on_s * co + on_u * uo
-        product = -2.0 * (column(p, z, 1) - po) * (column(q, z, 1) - qo) * share * share
-        here = pl.ds(z, ROWS, stride=COLS)
-        grad_out[here, :] = grad_out[here, :] + ko * ko * product
+        out = down + here
+        for i, axis in ((0, 1), (1, 0)):
+            product = -2.0 * (pp - after(pp, axis)) * (qq - after(qq, axis))
+            here, there = gives(kk, after(kk, axis), share_of(i, y), product)
+            out = out + here + before(there, axis)
+        grad[pl.ds(y * COLS, COLS), :] = out
+        if y % CHUNK == CHUNK - 1:
+            at = y + 1 - CHUNK
+            for z, value in zip((0, COLS - 1), outer):
+                here = pl.ds(at * COLS + z, CHUNK, stride=COLS)
+                grad[here, :] = grad[here, :] + value[at : at + CHUNK]
+            here = pl.ds(at * COLS, CHUNK * COLS)
+            sent.append(pltpu.make_async_copy(grad.at[here], grad_out.at[here], sems.at[2 + at // CHUNK]))
+            sent[-1].start()
+    for copy in sent:
+        copy.wait()
 
 
 def per_device(*arguments):
@@ -398,35 +452,37 @@
     def cost(us):
         return pl.CostEstimate(flops=0, bytes_accessed=int(us * 3.0e6), transcendentals=0)
 
+    far = [pltpu.with_memory_space_constraint(a, pltpu.HBM) for a in (k, s, c, sd, lb)]
     two, one = pl.pallas_call(
         pack_kernel,
         out_shape=f32(ROW_MESSAGE, ROW_MESSAGE),
-        in_specs=[pl.BlockSpec(memory_space=pl.ANY)] * 5,
+        in_specs=[pl.BlockSpec(memory_space=pltpu.HBM)] * 5,
         out_specs=(vmem,) * 2,
         scratch_shapes=[
             pltpu.VMEM((3, 6 * COLS, LANES), jnp.float32),
             pltpu.VMEM((2, 6 * COLS, LANES), jnp.int32),
             pltpu.SemaphoreType.DMA((10,)),
         ],
-        compiler_params=pltpu.CompilerParams(vmem_limit_bytes=60 * 1024 * 1024),
+        compiler_params=pltpu.CompilerParams(vmem_limit_bytes=16 * 1024 * 1024),
         name="pack",
-    )(k, s, c, sd, lb)
+    )(*far)
     one, two = swap(one, two, GY)
     block, framed = ROWS * COLS, (ROWS + 2) * COLS
-    wx, wy, wz, r, v, u = pl.pallas_call(
+    k, s, c, sd, wx, wy, wz, r, v, u, shares = pl.pallas_call(
         block_kernel,
-        out_shape=f32(*(block,) * 6),
-        in_specs=[vmem] * 5,
-        out_specs=(vmem,) * 6,
+        out_shape=f32(*(block,) * 3) + (jax.ShapeDtypeStruct((block, LANES), jnp.int32),) + f32(*(block,) * 6, 3 * block),
+        in_specs=[pl.BlockSpec(memory_space=pltpu.HBM)] * 5,
+        out_specs=(vmem,) * 11,
+        scratch_shapes=[pltpu.VMEM((block, LANES), jnp.int32), pltpu.SemaphoreType.DMA((5, ROWS // CHUNK))],
         compiler_params=big,
-        cost_estimate=cost(2.0),
+        cost_estimate=cost(3.0),
         name="block",
-    )(k, s, c, sd, lb)
-    r, v, u, rims, low, cols, ztwo, zone = pl.pallas_call(
+    )(*far)
+    r, v, u, low, cols, ztwo, zone = pl.pallas_call(
         rows_kernel,
-        out_shape=f32(framed, framed, framed, 6 * COLS, COLS, 10 * TALL, COL_MESSAGE, COL_MESSAGE),
+        out_shape=f32(framed, framed, framed, COLS, 10 * TALL + 6 * COLS, COL_MESSAGE, COL_MESSAGE),
         in_specs=[vmem] * 12,
-        out_specs=(vmem,) * 8,
+        out_specs=(vmem,) * 7,
         compiler_params=big,
         cost_estimate=cost(0.5),
         name="rows",
@@ -454,12 +510,17 @@
     outs = pl.pallas_call(
         finish_kernel,
         out_shape=f32(block, block, block),
-        in_specs=[vmem] * 9,
-        out_specs=(vmem,) * 3,
-        scratch_shapes=[pltpu.VMEM((framed, LANES), jnp.float32)] * 2,
+        in_specs=[vmem] * 10,
+        out_specs=(pl.BlockSpec(memory_space=pltpu.HBM),) * 3,
+        scratch_shapes=[
+            pltpu.VMEM((framed, LANES), jnp.float32),
+            pltpu.VMEM((framed, LANES), jnp.float32),
+            pltpu.VMEM((block, LANES), jnp.float32),
+            pltpu.SemaphoreType.DMA((2 + ROWS // CHUNK,)),
+        ],
         compiler_params=big,
         name="finish",
-    )(k, s, c, rims, side, r, v, u, parts)
+    )(k, s, c, shares, cols, side, r, v, u, parts)
     return tuple(a.reshape(ROWS, COLS, LANES) for a in outs)
 
 

time: 63.5 us -> 62.5 us (0.984)
  Pallas kernels: 7.97 us -> 6.96 us
    pallas_call x1, Pallas kernels: 2.19 us -> 1.43 us  [per_device(): pl.pallas_call(pack_kernel, out_shape=f32(ROW_MESSAGE, ROW_MESSAGE), in_s...]
  transfers between devices with their start and end apart: 4 -> 4, of which waited for: 1 -> 1; matrix products, arithmetic and copies ran while one was open for 0% -> 0% of each run, Pallas kernels for 6% -> 5%
where the time goes in v5:
time: 62.5 us; the launch traced here: 62.1 us
  blocking collectives  40 us (64%)
  starting transfers between devices  13.9 us (22%)
  Pallas kernels  6.96 us (11%)
  between operations  0.73 us (1%)
    all_to_all x2, blocking collectives, from_all(): return lax.all_to_all(copies, axis, split_axis=0, concat_axis=0, tiled=True)  40 us
    ppermute x2, starting transfers between devices, swap(): return (lax.ppermute(even_pairs, axis, pairs(0)), odd_pairs)  8.56 us
    ppermute x2, starting transfers between devices, swap(): odd_pairs = lax.ppermute(odd_pairs, axis, pairs(1))  5.33 us
    pallas_call x1, Pallas kernels, per_device(): pl.pallas_call(block_kernel, out_shape=f32(*(block,) * 3) + (jax.ShapeDty...  2.92 us
    pallas_call x1, Pallas kernels, per_device(): pl.pallas_call(finish_kernel, out_shape=f32(block, block, block), in_spec...  1.51 us
    pallas_call x1, Pallas kernels, per_device(): pl.pallas_call(pack_kernel, out_shape=f32(ROW_MESSAGE, ROW_MESSAGE), in_s...  1.43 us
  transfers between devices with their start and end apart: 4, of which 1 were waited for; matrix products, arithmetic and copies ran while one was open for 0% of the time, Pallas kernels for 5%

profile of v5, /device:TPU:1, one launch (start us, length us, event | category | flops | bytes accessed | tf_op | source)
XLA Modules:
  0.0 62.1 jit_solution(6608624735208415194)
XLA Ops:
  0.6 1.4 %pack.1 = (f32[232,128]{1,0:T(8,128)S(1)}, f32[232,128]{1,0:T(8,128)S(1)}) custom-call(f32[512,128]{1,0:T(8,128)} %bitcast.11, f32[512,128]{1,0:T(8,128)} %bitcast.13, f32[512,128]{1,0:T(8,128)} %bitcast.15, s32[512,128]{1,0:T(8,128)} %bitcast.17, s32[512,128]{1,0:T(8,128)} %bitcast.19), custom_call_target="tpu_custom_call" | custom-call | tf_op jit(solution)/shard_map/pack/pallas_call | solution.py:456
  2.1 0.7 %collective-permute-start = (f32[232,128]{1,0:T(8,128)S(1)}, f32[232,128]{1,0:T(8,128)S(1)}, u32[]{:S(2)}, u32[]{:S(2)}) collective-permute-start(f32[232,128]{1,0:T(8,128)S(1)} %get-tuple-element.32), channel_id=1, source_target_pairs={{32,64},{64,32},{96,128},{128,96},{160,192},{192,160},{224,256},{2... | collective-permute-start | bytes 356360 | tf_op jit(solution)/shard_map/ppermute | solution.py:29
  2.7 6.4 %collective-permute-start.1 = (f32[232,128]{1,0:T(8,128)S(1)}, f32[232,128]{1,0:T(8,128)S(1)}, u32[]{:S(2)}, u32[]{:S(2)}) collective-permute-start(f32[232,128]{1,0:T(8,128)S(1)} %get-tuple-element.33), channel_id=1, source_target_pairs={{0,32},{32,0},{64,96},{96,64},{128,160},{160,128},{192,224},{224,1... | collective-permute-start | bytes 356360 | tf_op jit(solution)/shard_map/ppermute | solution.py:30
  9.1 2.9 %block.1 = (f32[512,128]{1,0:T(8,128)S(1)}, f32[512,128]{1,0:T(8,128)S(1)}, f32[512,128]{1,0:T(8,128)S(1)}, s32[512,128]{1,0:T(8,128)S(1)}, f32[512,128]{1,0:T(8...) custom-call(f32[512,128]{1,0:T(8,128)} %bitcast.12, ...), custom_call_target="tpu_custom_call" | custom-call | bytes 9000000 | tf_op jit(solution)/shard_map/block/pallas_call | solution.py:471
  12.1 0.0 collective-permute-done.two
  12.1 0.0 collective-permute-done.1.one
  12.1 0.3 rows.1
  12.4 4.7 %collective-permute-start.2 = (f32[168,128]{1,0:T(8,128)S(1)}, f32[168,128]{1,0:T(8,128)S(1)}, u32[]{:S(2)}, u32[]{:S(2)}) collective-permute-start(f32[168,128]{1,0:T(8,128)S(1)} %get-tuple-element.42), channel_id=1, source_target_pairs={{1,2},{2,1},{3,4},{4,3},{5,6},{6,5},{7,8},{8,7},{9,10},{10,9},{11,... | collective-permute-start | bytes 258056 | tf_op jit(solution)/shard_map/ppermute | solution.py:29
  17.0 2.2 %collective-permute-start.3 = (f32[168,128]{1,0:T(8,128)S(1)}, f32[168,128]{1,0:T(8,128)S(1)}, u32[]{:S(2)}, u32[]{:S(2)}) collective-permute-start(f32[168,128]{1,0:T(8,128)S(1)} %get-tuple-element.43), channel_id=1, source_target_pairs={{0,1},{1,0},{2,3},{3,2},{4,5},{5,4},{6,7},{7,6},{8,9},{9,8},{10,11... | collective-permute-start | bytes 258056 | tf_op jit(solution)/shard_map/ppermute | solution.py:30
  19.2 0.5 inner.1.sums
  19.7 0.0 collective-permute-done.2.two
  19.7 0.5 collective-permute-done.3.one
  20.2 0.3 columns.1
  20.6 27.2 %all_to_all.10 = f32[32,1,128]{2,1,0:T(1,128)S(1)} all-to-all(f32[32,1,128]{2,1,0:T(1,128)S(1)} %broadcast_in_dim.6), channel_id=1, replica_groups=mesh['gy_0'=4,'gy_1'=4,'gz_0'=16,'gz_1'=2] {'gz_0','gz_1'}, dimensions={0} | all-to-all | bytes 32768 | tf_op jit(solution)/shard_map/all_to_all | solution.py:35
  47.9 12.8 %all_to_all.11.line = f32[16,1,128]{2,1,0:T(1,128)S(1)} all-to-all(f32[16,1,128]{2,1,0:T(1,128)S(1)} %broadcast_in_dim.7), channel_id=1, replica_groups=mesh['gy_0'=4,'gy_1'=4,'gz_0'=16,'gz_1'=2] {'gy_0','gy_1'}, dimensions={0} | all-to-all | bytes 16384 | tf_op jit(solution)/shard_map/all_to_all | solution.py:35
  60.6 1.5 %finish.1 = (f32[512,128]{1,0:T(8,128)}, f32[512,128]{1,0:T(8,128)}, f32[512,128]{1,0:T(8,128)}) custom-call(f32[512,128]{1,0:T(8,128)S(1)} %get-tuple-element.28.k, f32[512,128]{1,0:T(8,128)S(1)} %get-tuple-element.29.s, f32[512,128]{1,0:T(8,128)S(1)} %get-tuple-element.30.c, f32[1536,128]{1,0:T(8,128)S(1)} %get-tuple-element.31.shares, ...), custom_call_target="tpu_custom_call" | custom-call | tf_op jit(solution)/shard_map/finish/pallas_call | solution.py:510
  (3 shorter events, 0.0 us)
Async XLA Ops:
  2.1 10.0 %collective-permute-start = (f32[232,128]{1,0:T(8,128)S(1)}, f32[232,128]{1,0:T(8,128)S(1)}, u32[]{:S(2)}, u32[]{:S(2)}) collective-permute-start(f32[232,128]{1,0:T(8,128)S(1)} %get-tuple-element.32), channel_id=1, source_target_pairs={{32,64},{64,32},{96,128},{128,96},{160,192},{192,160},{224,256},{2... | collective-permute-start | bytes 356360 | tf_op jit(solution)/shard_map/ppermute | solution.py:29
  2.7 9.3 %collective-permute-start.1 = (f32[232,128]{1,0:T(8,128)S(1)}, f32[232,128]{1,0:T(8,128)S(1)}, u32[]{:S(2)}, u32[]{:S(2)}) collective-permute-start(f32[232,128]{1,0:T(8,128)S(1)} %get-tuple-element.33), channel_id=1, source_target_pairs={{0,32},{32,0},{64,96},{96,64},{128,160},{160,128},{192,224},{224,1... | collective-permute-start | bytes 356360 | tf_op jit(solution)/shard_map/ppermute | solution.py:30
  12.4 7.3 %collective-permute-start.2 = (f32[168,128]{1,0:T(8,128)S(1)}, f32[168,128]{1,0:T(8,128)S(1)}, u32[]{:S(2)}, u32[]{:S(2)}) collective-permute-start(f32[168,128]{1,0:T(8,128)S(1)} %get-tuple-element.42), channel_id=1, source_target_pairs={{1,2},{2,1},{3,4},{4,3},{5,6},{6,5},{7,8},{8,7},{9,10},{10,9},{11,... | collective-permute-start | bytes 258056 | tf_op jit(solution)/shard_map/ppermute | solution.py:29
  17.0 3.2 %collective-permute-start.3 = (f32[168,128]{1,0:T(8,128)S(1)}, f32[168,128]{1,0:T(8,128)S(1)}, u32[]{:S(2)}, u32[]{:S(2)}) collective-permute-start(f32[168,128]{1,0:T(8,128)S(1)} %get-tuple-element.43), channel_id=1, source_target_pairs={{0,1},{1,0},{2,3},{3,2},{4,5},{5,4},{6,7},{7,6},{8,9},{9,8},{10,11... | collective-permute-start | bytes 258056 | tf_op jit(solution)/shard_map/ppermute | solution.py:30

commit v6 on v5

--- a/solution.py
+++ b/solution.py
@@ -16,7 +16,7 @@
 TALL = 24
 PARTS = 7
 ROW_MESSAGE = PARTS * COLS + 8
-COL_MESSAGE = PARTS * TALL
+COL_MESSAGE = PARTS * ROWS + 16
 CHUNK = 4
 
 
@@ -126,10 +126,10 @@
 
 
 def edge(here, there, inside=None):
-    share = recip_sum(here, there)
+    share = there * recip_sum(here, there)
     if inside is not None:
         share = share * inside
-    return 2.0 * here * there * share, share
+    return 2.0 * here * share, share
 
 
 def block_kernel(*refs):
@@ -190,6 +190,20 @@
     if plus2 is not None:
         tail = jnp.where(at == 1, plus2, jnp.where(at == 6, minus2, tail))
     return jnp.concatenate([own, tail], axis=0)
+
+
+def tail_rows(wide):
+    at = lax.broadcasted_iota(jnp.int32, (8, LANES), 0)
+    return (at < 2) | (at > 5) if wide else (at < 1) | (at > 6)
+
+
+def tails_packed(k, s, c, q):
+    return [jnp.where(tail_rows(True), k, pltpu.roll(s, 4, 0)), jnp.where(tail_rows(False), c, pltpu.roll(q, 4, 0))]
+
+
+def tails_unpacked(k_s, c_q):
+    pairs = ((k_s, True), (pltpu.roll(k_s, 4, 0), True), (c_q, False), (pltpu.roll(c_q, 4, 0), False))
+    return [jnp.where(tail_rows(wide), a, 0.0) for a, wide in pairs]
 
 
 def rows_kernel(two, one, k, s, c, sd, wx, wy, wz, r_in, v_in, u_in, r, v, u, low_out, cols_out, two_out, one_out):
@@ -250,9 +264,13 @@
         for i, part in enumerate((kc, sc, cc, dc, kin)):
             cols_out[pl.ds((5 * right + i) * TALL, TALL), :] = part
         sides.append((kc, sc, cc, rc, vc, uc, dc))
-    for i, (first, last) in enumerate(zip(*sides)):
-        one_out[pl.ds(i * TALL, TALL), :] = jnp.where(odd_col, first, last)
-        two_out[pl.ds(i * TALL, TALL), :] = jnp.where(odd_col, last, first)
+    packed = [[part[:ROWS] for part in side] + tails_packed(*(part[ROWS:] for part in side[:4])) for side in sides]
+    at = 0
+    for first, last in zip(*packed):
+        here = pl.ds(at, first.shape[0])
+        one_out[here, :] = jnp.where(odd_col, first, last)
+        two_out[here, :] = jnp.where(odd_col, last, first)
+        at += first.shape[0]
 
 
 def inner_kernel(c, sd, wx, wy, wz, low, r, v, u, sums_out):
@@ -298,11 +316,14 @@
     for right in (False, True):
         z, zin, zdeep = (COLS - 1, COLS - 2, COLS - 3) if right else (0, 1, 2)
 
-        def arrived(i):
-            first, second = one[pl.ds(i * TALL, TALL), :], two[pl.ds(i * TALL, TALL), :]
+        def arrived(at, size):
+            first, second = one[pl.ds(at, size), :], two[pl.ds(at, size), :]
             return jnp.where(odd_col, second, first) if right else jnp.where(odd_col, first, second)
 
-        ko, so, co, qo, image, image_cot, diagonal = [arrived(i) for i in range(PARTS)]
+        tails = tails_unpacked(*(arrived(PARTS * ROWS + at, 8) for at in (0, 8))) + [jnp.zeros((8, LANES), jnp.float32)] * 3
+        ko, so, co, qo, image, image_cot, diagonal = [
+            jnp.concatenate([arrived(i * ROWS, ROWS), tail], axis=0) for i, tail in enumerate(tails)
+        ]
         kc, sc, cc, dc, kin = [cols[pl.ds((5 * right + i) * TALL, TALL), :] for i in range(5)]
         w = harmonic(ko, kc)
         win = harmonic(kc, kin)
@@ -410,24 +431,28 @@
     def share_of(i, y):
         return shares[pl.ds((i * ROWS + y) * COLS, COLS), :]
 
-    def gives(kk, kn, share, product):
-        to_here, to_there = kn * share, kk * share
-        return to_here * to_here * product, to_there * to_there * product
-
+    insides = [below((COLS, LANES), axis, n - 1) for axis, n in ((0, COLS), (1, LANES))]
     up = None
     for y in range(-1, ROWS):
-        kk, pp, qq = rows(0, k, y), row(p, y + 1), row(q, y + 1)
-        kn = rows(0, k, y + 1)
-        share = share_of(2, y) if 0 <= y < ROWS - 1 else recip_sum(kk, kn)
-        here, there = gives(kk, kn, share, -2.0 * (pp - row(p, y + 2)) * (qq - row(q, y + 2)))
-        down, up = up, there
+        pp, qq = row(p, y + 1), row(q, y + 1)
+        product = (pp - row(p, y + 2)) * (qq - row(q, y + 2))
+        if 0 <= y < ROWS - 1:
+            far = share_of(2, y)
+            near = 1.0 - far
+        else:
+            kk, kn = rows(0, k, y), rows(0, k, y + 1)
+            share = recip_sum(kk, kn)
+            far, near = kn * share, kk * share
+        down, up = up, near * near * product
         if y < 0:
             continue
-        out = down + here
+        out = down + far * far * product
         for i, axis in ((0, 1), (1, 0)):
-            product = -2.0 * (pp - after(pp, axis)) * (qq - after(qq, axis))
-            here, there = gives(kk, after(kk, axis), share_of(i, y), product)
-            out = out + here + before(there, axis)
+            product = (pp - after(pp, axis)) * (qq - after(qq, axis))
+            far = share_of(i, y)
+            near = insides[axis] - far
+            out = out + far * far * product + before(near * near * product, axis)
+        out = -2.0 * out
         grad[pl.ds(y * COLS, COLS), :] = out
         if y % CHUNK == CHUNK - 1:
             at = y + 1 - CHUNK
@@ -506,7 +531,7 @@
         cost_estimate=cost(0.5),
         name="columns",
     )(ztwo, zone, cols, c, sd, wz, sums, r, v, u)
-    parts = from_all(jnp.sum(from_all(line, GZ), axis=0), GY)
+    parts = from_all(jnp.sum(from_all(line, GY + ("gz_1",)), axis=0), ("gz_0",))
     outs = pl.pallas_call(
         finish_kernel,
         out_shape=f32(block, block, block),

time: 62.5 us -> 62.4 us (level)
  no operation moved by 1% of the time
where the time goes in v6:
time: 62.4 us; the launch traced here: 62 us
  blocking collectives  39.9 us (64%)
  starting transfers between devices  13.9 us (22%)
  Pallas kernels  6.97 us (11%)
  between operations  0.73 us (1%)
    all_to_all x2, blocking collectives, from_all(): return lax.all_to_all(copies, axis, split_axis=0, concat_axis=0, tiled=True)  39.9 us
    ppermute x2, starting transfers between devices, swap(): return (lax.ppermute(even_pairs, axis, pairs(0)), odd_pairs)  8.57 us
    ppermute x2, starting transfers between devices, swap(): odd_pairs = lax.ppermute(odd_pairs, axis, pairs(1))  5.34 us
    pallas_call x1, Pallas kernels, per_device(): pl.pallas_call(block_kernel, out_shape=f32(*(block,) * 3) + (jax.ShapeDty...  2.9 us
    pallas_call x1, Pallas kernels, per_device(): pl.pallas_call(finish_kernel, out_shape=f32(block, block, block), in_spec...  1.53 us
    pallas_call x1, Pallas kernels, per_device(): pl.pallas_call(pack_kernel, out_shape=f32(ROW_MESSAGE, ROW_MESSAGE), in_s...  1.43 us
  transfers between devices with their start and end apart: 4, of which 1 were waited for; matrix products, arithmetic and copies ran while one was open for 0% of the time, Pallas kernels for 5%

profile of v6, /device:TPU:1, one launch (start us, length us, event | category | flops | bytes accessed | tf_op | source)
XLA Modules:
  0.0 62.0 jit_solution(9020071730971276723)
XLA Ops:
  0.6 1.4 %pack.1 = (f32[232,128]{1,0:T(8,128)S(1)}, f32[232,128]{1,0:T(8,128)S(1)}) custom-call(f32[512,128]{1,0:T(8,128)} %bitcast.11, f32[512,128]{1,0:T(8,128)} %bitcast.13, f32[512,128]{1,0:T(8,128)} %bitcast.15, s32[512,128]{1,0:T(8,128)} %bitcast.17, s32[512,128]{1,0:T(8,128)} %bitcast.19), custom_call_target="tpu_custom_call" | custom-call | tf_op jit(solution)/shard_map/pack/pallas_call | solution.py:481
  2.1 0.7 %collective-permute-start = (f32[232,128]{1,0:T(8,128)S(1)}, f32[232,128]{1,0:T(8,128)S(1)}, u32[]{:S(2)}, u32[]{:S(2)}) collective-permute-start(f32[232,128]{1,0:T(8,128)S(1)} %get-tuple-element.32), channel_id=1, source_target_pairs={{32,64},{64,32},{96,128},{128,96},{160,192},{192,160},{224,256},{2... | collective-permute-start | bytes 356360 | tf_op jit(solution)/shard_map/ppermute | solution.py:29
  2.7 6.4 %collective-permute-start.1 = (f32[232,128]{1,0:T(8,128)S(1)}, f32[232,128]{1,0:T(8,128)S(1)}, u32[]{:S(2)}, u32[]{:S(2)}) collective-permute-start(f32[232,128]{1,0:T(8,128)S(1)} %get-tuple-element.33), channel_id=1, source_target_pairs={{0,32},{32,0},{64,96},{96,64},{128,160},{160,128},{192,224},{224,1... | collective-permute-start | bytes 356360 | tf_op jit(solution)/shard_map/ppermute | solution.py:30
  9.1 2.9 %block.1 = (f32[512,128]{1,0:T(8,128)S(1)}, f32[512,128]{1,0:T(8,128)S(1)}, f32[512,128]{1,0:T(8,128)S(1)}, s32[512,128]{1,0:T(8,128)S(1)}, f32[512,128]{1,0:T(8...) custom-call(f32[512,128]{1,0:T(8,128)} %bitcast.12, ...), custom_call_target="tpu_custom_call" | custom-call | bytes 9000000 | tf_op jit(solution)/shard_map/block/pallas_call | solution.py:496
  12.1 0.0 collective-permute-done.two
  12.1 0.0 collective-permute-done.1.one
  12.1 0.3 rows.1
  12.4 4.7 %collective-permute-start.2 = (f32[128,128]{1,0:T(8,128)S(1)}, f32[128,128]{1,0:T(8,128)S(1)}, u32[]{:S(2)}, u32[]{:S(2)}) collective-permute-start(f32[128,128]{1,0:T(8,128)S(1)} %get-tuple-element.42), channel_id=1, source_target_pairs={{1,2},{2,1},{3,4},{4,3},{5,6},{6,5},{7,8},{8,7},{9,10},{10,9},{11,... | collective-permute-start | bytes 196616 | tf_op jit(solution)/shard_map/ppermute | solution.py:29
  17.0 2.2 %collective-permute-start.3 = (f32[128,128]{1,0:T(8,128)S(1)}, f32[128,128]{1,0:T(8,128)S(1)}, u32[]{:S(2)}, u32[]{:S(2)}) collective-permute-start(f32[128,128]{1,0:T(8,128)S(1)} %get-tuple-element.43), channel_id=1, source_target_pairs={{0,1},{1,0},{2,3},{3,2},{4,5},{5,4},{6,7},{7,6},{8,9},{9,8},{10,11... | collective-permute-start | bytes 196616 | tf_op jit(solution)/shard_map/ppermute | solution.py:30
  19.2 0.5 inner.1.sums
  19.7 0.0 collective-permute-done.2.two
  19.7 0.5 collective-permute-done.3.one
  20.2 0.3 columns.1
  20.6 13.8 %all_to_all.10 = f32[32,1,128]{2,1,0:T(1,128)S(1)} all-to-all(f32[32,1,128]{2,1,0:T(1,128)S(1)} %broadcast_in_dim.6), channel_id=1, replica_groups=mesh['gy_0'=4,'gy_1'=4,'gz_0'=16,'gz_1'=2] {'gy_0','gy_1','gz_1'}, dimensions={0} | all-to-all | bytes 32768 | tf_op jit(solution)/shard_map/all_to_all | solution.py:35
  34.4 26.1 %all_to_all.11.line = f32[16,1,128]{2,1,0:T(1,128)S(1)} all-to-all(f32[16,1,128]{2,1,0:T(1,128)S(1)} %broadcast_in_dim.7), channel_id=1, replica_groups=mesh['gy_0'=4,'gy_1'=4,'gz_0'=16,'gz_1'=2] {'gz_0'}, dimensions={0} | all-to-all | bytes 16384 | tf_op jit(solution)/shard_map/all_to_all | solution.py:35
  60.5 1.5 %finish.1 = (f32[512,128]{1,0:T(8,128)}, f32[512,128]{1,0:T(8,128)}, f32[512,128]{1,0:T(8,128)}) custom-call(f32[512,128]{1,0:T(8,128)S(1)} %get-tuple-element.28.k, f32[512,128]{1,0:T(8,128)S(1)} %get-tuple-element.29.s, f32[512,128]{1,0:T(8,128)S(1)} %get-tuple-element.30.c, f32[1536,128]{1,0:T(8,128)S(1)} %get-tuple-element.31.shares, ...), custom_call_target="tpu_custom_call" | custom-call | tf_op jit(solution)/shard_map/finish/pallas_call | solution.py:535
  (3 shorter events, 0.0 us)
Async XLA Ops:
  2.1 10.0 %collective-permute-start = (f32[232,128]{1,0:T(8,128)S(1)}, f32[232,128]{1,0:T(8,128)S(1)}, u32[]{:S(2)}, u32[]{:S(2)}) collective-permute-start(f32[232,128]{1,0:T(8,128)S(1)} %get-tuple-element.32), channel_id=1, source_target_pairs={{32,64},{64,32},{96,128},{128,96},{160,192},{192,160},{224,256},{2... | collective-permute-start | bytes 356360 | tf_op jit(solution)/shard_map/ppermute | solution.py:29
  2.7 9.3 %collective-permute-start.1 = (f32[232,128]{1,0:T(8,128)S(1)}, f32[232,128]{1,0:T(8,128)S(1)}, u32[]{:S(2)}, u32[]{:S(2)}) collective-permute-start(f32[232,128]{1,0:T(8,128)S(1)} %get-tuple-element.33), channel_id=1, source_target_pairs={{0,32},{32,0},{64,96},{96,64},{128,160},{160,128},{192,224},{224,1... | collective-permute-start | bytes 356360 | tf_op jit(solution)/shard_map/ppermute | solution.py:30
  12.4 7.3 %collective-permute-start.2 = (f32[128,128]{1,0:T(8,128)S(1)}, f32[128,128]{1,0:T(8,128)S(1)}, u32[]{:S(2)}, u32[]{:S(2)}) collective-permute-start(f32[128,128]{1,0:T(8,128)S(1)} %get-tuple-element.42), channel_id=1, source_target_pairs={{1,2},{2,1},{3,4},{4,3},{5,6},{6,5},{7,8},{8,7},{9,10},{10,9},{11,... | collective-permute-start | bytes 196616 | tf_op jit(solution)/shard_map/ppermute | solution.py:29
  17.0 3.1 %collective-permute-start.3 = (f32[128,128]{1,0:T(8,128)S(1)}, f32[128,128]{1,0:T(8,128)S(1)}, u32[]{:S(2)}, u32[]{:S(2)}) collective-permute-start(f32[128,128]{1,0:T(8,128)S(1)} %get-tuple-element.43), channel_id=1, source_target_pairs={{0,1},{1,0},{2,3},{3,2},{4,5},{5,4},{6,7},{7,6},{8,9},{9,8},{10,11... | collective-permute-start | bytes 196616 | tf_op jit(solution)/shard_map/ppermute | solution.py:30

commit v7 on v5

--- a/solution.py
+++ b/solution.py
@@ -16,7 +16,7 @@
 TALL = 24
 PARTS = 7
 ROW_MESSAGE = PARTS * COLS + 8
-COL_MESSAGE = PARTS * TALL
+COL_MESSAGE = PARTS * ROWS + 16
 CHUNK = 4
 
 
@@ -192,6 +192,20 @@
     return jnp.concatenate([own, tail], axis=0)
 
 
+def tail_rows(wide):
+    at = lax.broadcasted_iota(jnp.int32, (8, LANES), 0)
+    return (at < 2) | (at > 5) if wide else (at < 1) | (at > 6)
+
+
+def tails_packed(k, s, c, q):
+    return [jnp.where(tail_rows(True), k, pltpu.roll(s, 4, 0)), jnp.where(tail_rows(False), c, pltpu.roll(q, 4, 0))]
+
+
+def tails_unpacked(k_s, c_q):
+    pairs = ((k_s, True), (pltpu.roll(k_s, 4, 0), True), (c_q, False), (pltpu.roll(c_q, 4, 0), False))
+    return [jnp.where(tail_rows(wide), a, 0.0) for a, wide in pairs]
+
+
 def rows_kernel(two, one, k, s, c, sd, wx, wy, wz, r_in, v_in, u_in, r, v, u, low_out, cols_out, two_out, one_out):
     odd_row, odd_col = is_odd("gy_1"), is_odd("gz_1")
     kept = pl.ds(COLS, ROWS * COLS)
@@ -250,9 +264,13 @@
         for i, part in enumerate((kc, sc, cc, dc, kin)):
             cols_out[pl.ds((5 * right + i) * TALL, TALL), :] = part
         sides.append((kc, sc, cc, rc, vc, uc, dc))
-    for i, (first, last) in enumerate(zip(*sides)):
-        one_out[pl.ds(i * TALL, TALL), :] = jnp.where(odd_col, first, last)
-        two_out[pl.ds(i * TALL, TALL), :] = jnp.where(odd_col, last, first)
+    packed = [[part[:ROWS] for part in side] + tails_packed(*(part[ROWS:] for part in side[:4])) for side in sides]
+    at = 0
+    for first, last in zip(*packed):
+        here = pl.ds(at, first.shape[0])
+        one_out[here, :] = jnp.where(odd_col, first, last)
+        two_out[here, :] = jnp.where(odd_col, last, first)
+        at += first.shape[0]
 
 
 def inner_kernel(c, sd, wx, wy, wz, low, r, v, u, sums_out):
@@ -298,11 +316,14 @@
     for right in (False, True):
         z, zin, zdeep = (COLS - 1, COLS - 2, COLS - 3) if right else (0, 1, 2)
 
-        def arrived(i):
-            first, second = one[pl.ds(i * TALL, TALL), :], two[pl.ds(i * TALL, TALL), :]
+        def arrived(at, size):
+            first, second = one[pl.ds(at, size), :], two[pl.ds(at, size), :]
             return jnp.where(odd_col, second, first) if right else jnp.where(odd_col, first, second)
 
-        ko, so, co, qo, image, image_cot, diagonal = [arrived(i) for i in range(PARTS)]
+        tails = tails_unpacked(*(arrived(PARTS * ROWS + at, 8) for at in (0, 8))) + [jnp.zeros((8, LANES), jnp.float32)] * 3
+        ko, so, co, qo, image, image_cot, diagonal = [
+            jnp.concatenate([arrived(i * ROWS, ROWS), tail], axis=0) for i, tail in enumerate(tails)
+        ]
         kc, sc, cc, dc, kin = [cols[pl.ds((5 * right + i) * TALL, TALL), :] for i in range(5)]
         w = harmonic(ko, kc)
         win = harmonic(kc, kin)
@@ -357,7 +378,8 @@
     a0 = m0 / m1
     new = a0 * a0 * m2 - m0
     grow = 1.0 + new / m0
-    a1 = new / (grow * grow * m1 - 2.0 * grow * a0 * m2 + a0 * a0 * m3)
+    curve = grow * grow * m1 - 2.0 * grow * a0 * m2 + a0 * a0 * m3
+    a1 = jnp.where((new > 0.0) & (curve > 0.0), new / curve, 0.0)
     return a0 + a1 * grow, -a1 * a0
 
 
@@ -506,7 +528,7 @@
         cost_estimate=cost(0.5),
         name="columns",
     )(ztwo, zone, cols, c, sd, wz, sums, r, v, u)
-    parts = from_all(jnp.sum(from_all(line, GZ), axis=0), GY)
+    parts = from_all(jnp.sum(from_all(line, GY + ("gz_1",)), axis=0), ("gz_0",))
     outs = pl.pallas_call(
         finish_kernel,
         out_shape=f32(block, block, block),

time: 62.5 us -> 62.4 us (level)
  no operation moved by 1% of the time
where the time goes in v7:
time: 62.4 us; the launch traced here: 62 us
  blocking collectives  39.9 us (64%)
  starting transfers between devices  13.9 us (22%)
  Pallas kernels  6.95 us (11%)
  between operations  0.73 us (1%)
    all_to_all x2, blocking collectives, from_all(): return lax.all_to_all(copies, axis, split_axis=0, concat_axis=0, tiled=True)  39.9 us
    ppermute x2, starting transfers between devices, swap(): return (lax.ppermute(even_pairs, axis, pairs(0)), odd_pairs)  8.57 us
    ppermute x2, starting transfers between devices, swap(): odd_pairs = lax.ppermute(odd_pairs, axis, pairs(1))  5.34 us
    pallas_call x1, Pallas kernels, per_device(): pl.pallas_call(block_kernel, out_shape=f32(*(block,) * 3) + (jax.ShapeDty...  2.9 us
    pallas_call x1, Pallas kernels, per_device(): pl.pallas_call(finish_kernel, out_shape=f32(block, block, block), in_spec...  1.52 us
    pallas_call x1, Pallas kernels, per_device(): pl.pallas_call(pack_kernel, out_shape=f32(ROW_MESSAGE, ROW_MESSAGE), in_s...  1.43 us
  transfers between devices with their start and end apart: 4, of which 1 were waited for; matrix products, arithmetic and copies ran while one was open for 0% of the time, Pallas kernels for 5%

profile of v7, /device:TPU:1, one launch (start us, length us, event | category | flops | bytes accessed | tf_op | source)
XLA Modules:
  0.0 62.0 jit_solution(16212904324430176725)
XLA Ops:
  0.6 1.4 %pack.1 = (f32[232,128]{1,0:T(8,128)S(1)}, f32[232,128]{1,0:T(8,128)S(1)}) custom-call(f32[512,128]{1,0:T(8,128)} %bitcast.11, f32[512,128]{1,0:T(8,128)} %bitcast.13, f32[512,128]{1,0:T(8,128)} %bitcast.15, s32[512,128]{1,0:T(8,128)} %bitcast.17, s32[512,128]{1,0:T(8,128)} %bitcast.19), custom_call_target="tpu_custom_call" | custom-call | tf_op jit(solution)/shard_map/pack/pallas_call | solution.py:478
  2.1 0.7 %collective-permute-start = (f32[232,128]{1,0:T(8,128)S(1)}, f32[232,128]{1,0:T(8,128)S(1)}, u32[]{:S(2)}, u32[]{:S(2)}) collective-permute-start(f32[232,128]{1,0:T(8,128)S(1)} %get-tuple-element.32), channel_id=1, source_target_pairs={{32,64},{64,32},{96,128},{128,96},{160,192},{192,160},{224,256},{2... | collective-permute-start | bytes 356360 | tf_op jit(solution)/shard_map/ppermute | solution.py:29
  2.7 6.4 %collective-permute-start.1 = (f32[232,128]{1,0:T(8,128)S(1)}, f32[232,128]{1,0:T(8,128)S(1)}, u32[]{:S(2)}, u32[]{:S(2)}) collective-permute-start(f32[232,128]{1,0:T(8,128)S(1)} %get-tuple-element.33), channel_id=1, source_target_pairs={{0,32},{32,0},{64,96},{96,64},{128,160},{160,128},{192,224},{224,1... | collective-permute-start | bytes 356360 | tf_op jit(solution)/shard_map/ppermute | solution.py:30
  9.1 2.9 %block.1 = (f32[512,128]{1,0:T(8,128)S(1)}, f32[512,128]{1,0:T(8,128)S(1)}, f32[512,128]{1,0:T(8,128)S(1)}, s32[512,128]{1,0:T(8,128)S(1)}, f32[512,128]{1,0:T(8...) custom-call(f32[512,128]{1,0:T(8,128)} %bitcast.12, ...), custom_call_target="tpu_custom_call" | custom-call | bytes 9000000 | tf_op jit(solution)/shard_map/block/pallas_call | solution.py:493
  12.1 0.0 collective-permute-done.two
  12.1 0.0 collective-permute-done.1.one
  12.1 0.3 rows.1
  12.4 4.7 %collective-permute-start.2 = (f32[128,128]{1,0:T(8,128)S(1)}, f32[128,128]{1,0:T(8,128)S(1)}, u32[]{:S(2)}, u32[]{:S(2)}) collective-permute-start(f32[128,128]{1,0:T(8,128)S(1)} %get-tuple-element.42), channel_id=1, source_target_pairs={{1,2},{2,1},{3,4},{4,3},{5,6},{6,5},{7,8},{8,7},{9,10},{10,9},{11,... | collective-permute-start | bytes 196616 | tf_op jit(solution)/shard_map/ppermute | solution.py:29
  17.0 2.2 %collective-permute-start.3 = (f32[128,128]{1,0:T(8,128)S(1)}, f32[128,128]{1,0:T(8,128)S(1)}, u32[]{:S(2)}, u32[]{:S(2)}) collective-permute-start(f32[128,128]{1,0:T(8,128)S(1)} %get-tuple-element.43), channel_id=1, source_target_pairs={{0,1},{1,0},{2,3},{3,2},{4,5},{5,4},{6,7},{7,6},{8,9},{9,8},{10,11... | collective-permute-start | bytes 196616 | tf_op jit(solution)/shard_map/ppermute | solution.py:30
  19.2 0.5 inner.1.sums
  19.7 0.0 collective-permute-done.2.two
  19.7 0.5 collective-permute-done.3.one
  20.2 0.3 columns.1
  20.6 13.8 %all_to_all.10 = f32[32,1,128]{2,1,0:T(1,128)S(1)} all-to-all(f32[32,1,128]{2,1,0:T(1,128)S(1)} %broadcast_in_dim.6), channel_id=1, replica_groups=mesh['gy_0'=4,'gy_1'=4,'gz_0'=16,'gz_1'=2] {'gy_0','gy_1','gz_1'}, dimensions={0} | all-to-all | bytes 32768 | tf_op jit(solution)/shard_map/all_to_all | solution.py:35
  34.4 26.1 %all_to_all.11.line = f32[16,1,128]{2,1,0:T(1,128)S(1)} all-to-all(f32[16,1,128]{2,1,0:T(1,128)S(1)} %broadcast_in_dim.7), channel_id=1, replica_groups=mesh['gy_0'=4,'gy_1'=4,'gz_0'=16,'gz_1'=2] {'gz_0'}, dimensions={0} | all-to-all | bytes 16384 | tf_op jit(solution)/shard_map/all_to_all | solution.py:35
  60.5 1.5 %finish.1 = (f32[512,128]{1,0:T(8,128)}, f32[512,128]{1,0:T(8,128)}, f32[512,128]{1,0:T(8,128)}) custom-call(f32[512,128]{1,0:T(8,128)S(1)} %get-tuple-element.28.k, f32[512,128]{1,0:T(8,128)S(1)} %get-tuple-element.29.s, f32[512,128]{1,0:T(8,128)S(1)} %get-tuple-element.30.c, f32[1536,128]{1,0:T(8,128)S(1)} %get-tuple-element.31.shares, ...), custom_call_target="tpu_custom_call" | custom-call | tf_op jit(solution)/shard_map/finish/pallas_call | solution.py:532
  (3 shorter events, 0.0 us)
Async XLA Ops:
  2.1 10.0 %collective-permute-start = (f32[232,128]{1,0:T(8,128)S(1)}, f32[232,128]{1,0:T(8,128)S(1)}, u32[]{:S(2)}, u32[]{:S(2)}) collective-permute-start(f32[232,128]{1,0:T(8,128)S(1)} %get-tuple-element.32), channel_id=1, source_target_pairs={{32,64},{64,32},{96,128},{128,96},{160,192},{192,160},{224,256},{2... | collective-permute-start | bytes 356360 | tf_op jit(solution)/shard_map/ppermute | solution.py:29
  2.7 9.3 %collective-permute-start.1 = (f32[232,128]{1,0:T(8,128)S(1)}, f32[232,128]{1,0:T(8,128)S(1)}, u32[]{:S(2)}, u32[]{:S(2)}) collective-permute-start(f32[232,128]{1,0:T(8,128)S(1)} %get-tuple-element.33), channel_id=1, source_target_pairs={{0,32},{32,0},{64,96},{96,64},{128,160},{160,128},{192,224},{224,1... | collective-permute-start | bytes 356360 | tf_op jit(solution)/shard_map/ppermute | solution.py:30
  12.4 7.3 %collective-permute-start.2 = (f32[128,128]{1,0:T(8,128)S(1)}, f32[128,128]{1,0:T(8,128)S(1)}, u32[]{:S(2)}, u32[]{:S(2)}) collective-permute-start(f32[128,128]{1,0:T(8,128)S(1)} %get-tuple-element.42), channel_id=1, source_target_pairs={{1,2},{2,1},{3,4},{4,3},{5,6},{6,5},{7,8},{8,7},{9,10},{10,9},{11,... | collective-permute-start | bytes 196616 | tf_op jit(solution)/shard_map/ppermute | solution.py:29
  17.0 3.1 %collective-permute-start.3 = (f32[128,128]{1,0:T(8,128)S(1)}, f32[128,128]{1,0:T(8,128)S(1)}, u32[]{:S(2)}, u32[]{:S(2)}) collective-permute-start(f32[128,128]{1,0:T(8,128)S(1)} %get-tuple-element.43), channel_id=1, source_target_pairs={{0,1},{1,0},{2,3},{3,2},{4,5},{5,4},{6,7},{7,6},{8,9},{9,8},{10,11... | collective-permute-start | bytes 196616 | tf_op jit(solution)/shard_map/ppermute | solution.py:30

commit v8 on v7

--- a/solution.py
+++ b/solution.py
@@ -396,31 +396,27 @@
             return row(ref, y)
         return cols[pl.ds(10 * TALL + (field + (3 if y > 0 else 0)) * COLS, COLS), :]
 
-    for y in range(-1, ROWS + 1):
-        here = pl.ds((y + 1) * COLS, COLS)
-        p[here, :] = rows(1, s, y) + on_r * r[here, :] + on_v * v[here, :]
-        q[here, :] = on_s * rows(2, c, y) + on_u * u[here, :]
-    for right in (False, True):
-        z = COLS - 1 if right else 0
-        change, change_v, change_in, change_u = [side[pl.ds((10 * right + i) * TALL, TALL), :] for i in range(6, 10)]
-        zin = z - 1 if right else 1
-        for ref, col, value in (
-            (p, z, on_r * change + on_v * change_v),
-            (p, zin, on_v * change_in),
-            (q, z, on_u * change_u),
-        ):
-            here = pl.ds(COLS + col, ROWS, stride=COLS)
-            ref[here, :] = ref[here, :] + value[:ROWS]
-            last = pl.ds((ROWS + 1) * COLS + col, 1)
-            ref[last, :] = ref[last, :] + value[ROWS : ROWS + 1]
-            ref[pl.ds(col, 1), :] = ref[pl.ds(col, 1), :] + value[TALL - 1 :]
-    own = pl.ds(COLS, ROWS * COLS)
-    sent = [
-        pltpu.make_async_copy(p.at[own], prob_out, sems.at[0]),
-        pltpu.make_async_copy(q.at[own], adj_out, sems.at[1]),
-    ]
-    for copy in sent:
-        copy.start()
+    own, sent = pl.ds(COLS, ROWS * COLS), []
+    for i, (ref, out) in enumerate(((p, prob_out), (q, adj_out))):
+        for y in range(-1, ROWS + 1):
+            here = pl.ds((y + 1) * COLS, COLS)
+            if i == 0:
+                ref[here, :] = rows(1, s, y) + on_r * r[here, :] + on_v * v[here, :]
+            else:
+                ref[here, :] = on_s * rows(2, c, y) + on_u * u[here, :]
+        for right in (False, True):
+            z = COLS - 1 if right else 0
+            zin = z - 1 if right else 1
+            change, change_v, change_in, change_u = [side[pl.ds((10 * right + j) * TALL, TALL), :] for j in range(6, 10)]
+            added = ((z, on_r * change + on_v * change_v), (zin, on_v * change_in)) if i == 0 else ((z, on_u * change_u),)
+            for col, value in added:
+                here = pl.ds(COLS + col, ROWS, stride=COLS)
+                ref[here, :] = ref[here, :] + value[:ROWS]
+                last = pl.ds((ROWS + 1) * COLS + col, 1)
+                ref[last, :] = ref[last, :] + value[ROWS : ROWS + 1]
+                ref[pl.ds(col, 1), :] = ref[pl.ds(col, 1), :] + value[TALL - 1 :]
+        sent.append(pltpu.make_async_copy(ref.at[own], out, sems.at[i]))
+        sent[-1].start()
     outer = []
     for right in (False, True):
         z = COLS - 1 if right else 0

time: 62.4 us -> 62.4 us (level)
  no operation moved by 1% of the time
where the time goes in v8:
time: 62.4 us; the launch traced here: 62 us
  blocking collectives  39.9 us (64%)
  starting transfers between devices  13.9 us (22%)
  Pallas kernels  6.94 us (11%)
  between operations  0.73 us (1%)
    all_to_all x2, blocking collectives, from_all(): return lax.all_to_all(copies, axis, split_axis=0, concat_axis=0, tiled=True)  39.9 us
    ppermute x2, starting transfers between devices, swap(): return (lax.ppermute(even_pairs, axis, pairs(0)), odd_pairs)  8.57 us
    ppermute x2, starting transfers between devices, swap(): odd_pairs = lax.ppermute(odd_pairs, axis, pairs(1))  5.34 us
    pallas_call x1, Pallas kernels, per_device(): pl.pallas_call(block_kernel, out_shape=f32(*(block,) * 3) + (jax.ShapeDty...  2.9 us
    pallas_call x1, Pallas kernels, per_device(): pl.pallas_call(finish_kernel, out_shape=f32(block, block, block), in_spec...  1.5 us
    pallas_call x1, Pallas kernels, per_device(): pl.pallas_call(pack_kernel, out_shape=f32(ROW_MESSAGE, ROW_MESSAGE), in_s...  1.43 us
  transfers between devices with their start and end apart: 4, of which 1 were waited for; matrix products, arithmetic and copies ran while one was open for 0% of the time, Pallas kernels for 5%

profile of v8, /device:TPU:1, one launch (start us, length us, event | category | flops | bytes accessed | tf_op | source)
XLA Modules:
  0.0 62.0 jit_solution(17630043124849430242)
XLA Ops:
  0.6 1.4 %pack.1 = (f32[232,128]{1,0:T(8,128)S(1)}, f32[232,128]{1,0:T(8,128)S(1)}) custom-call(f32[512,128]{1,0:T(8,128)} %bitcast.11, f32[512,128]{1,0:T(8,128)} %bitcast.13, f32[512,128]{1,0:T(8,128)} %bitcast.15, s32[512,128]{1,0:T(8,128)} %bitcast.17, s32[512,128]{1,0:T(8,128)} %bitcast.19), custom_call_target="tpu_custom_call" | custom-call | tf_op jit(solution)/shard_map/pack/pallas_call | solution.py:474
  2.1 0.7 %collective-permute-start = (f32[232,128]{1,0:T(8,128)S(1)}, f32[232,128]{1,0:T(8,128)S(1)}, u32[]{:S(2)}, u32[]{:S(2)}) collective-permute-start(f32[232,128]{1,0:T(8,128)S(1)} %get-tuple-element.32), channel_id=1, source_target_pairs={{32,64},{64,32},{96,128},{128,96},{160,192},{192,160},{224,256},{2... | collective-permute-start | bytes 356360 | tf_op jit(solution)/shard_map/ppermute | solution.py:29
  2.7 6.4 %collective-permute-start.1 = (f32[232,128]{1,0:T(8,128)S(1)}, f32[232,128]{1,0:T(8,128)S(1)}, u32[]{:S(2)}, u32[]{:S(2)}) collective-permute-start(f32[232,128]{1,0:T(8,128)S(1)} %get-tuple-element.33), channel_id=1, source_target_pairs={{0,32},{32,0},{64,96},{96,64},{128,160},{160,128},{192,224},{224,1... | collective-permute-start | bytes 356360 | tf_op jit(solution)/shard_map/ppermute | solution.py:30
  9.1 2.9 %block.1 = (f32[512,128]{1,0:T(8,128)S(1)}, f32[512,128]{1,0:T(8,128)S(1)}, f32[512,128]{1,0:T(8,128)S(1)}, s32[512,128]{1,0:T(8,128)S(1)}, f32[512,128]{1,0:T(8...) custom-call(f32[512,128]{1,0:T(8,128)} %bitcast.12, ...), custom_call_target="tpu_custom_call" | custom-call | bytes 9000000 | tf_op jit(solution)/shard_map/block/pallas_call | solution.py:489
  12.1 0.0 collective-permute-done.two
  12.1 0.0 collective-permute-done.1.one
  12.1 0.3 rows.1
  12.4 4.7 %collective-permute-start.2 = (f32[128,128]{1,0:T(8,128)S(1)}, f32[128,128]{1,0:T(8,128)S(1)}, u32[]{:S(2)}, u32[]{:S(2)}) collective-permute-start(f32[128,128]{1,0:T(8,128)S(1)} %get-tuple-element.42), channel_id=1, source_target_pairs={{1,2},{2,1},{3,4},{4,3},{5,6},{6,5},{7,8},{8,7},{9,10},{10,9},{11,... | collective-permute-start | bytes 196616 | tf_op jit(solution)/shard_map/ppermute | solution.py:29
  17.0 2.2 %collective-permute-start.3 = (f32[128,128]{1,0:T(8,128)S(1)}, f32[128,128]{1,0:T(8,128)S(1)}, u32[]{:S(2)}, u32[]{:S(2)}) collective-permute-start(f32[128,128]{1,0:T(8,128)S(1)} %get-tuple-element.43), channel_id=1, source_target_pairs={{0,1},{1,0},{2,3},{3,2},{4,5},{5,4},{6,7},{7,6},{8,9},{9,8},{10,11... | collective-permute-start | bytes 196616 | tf_op jit(solution)/shard_map/ppermute | solution.py:30
  19.2 0.5 inner.1.sums
  19.7 0.0 collective-permute-done.2.two
  19.7 0.5 collective-permute-done.3.one
  20.2 0.3 columns.1
  20.6 13.8 %all_to_all.10 = f32[32,1,128]{2,1,0:T(1,128)S(1)} all-to-all(f32[32,1,128]{2,1,0:T(1,128)S(1)} %broadcast_in_dim.6), channel_id=1, replica_groups=mesh['gy_0'=4,'gy_1'=4,'gz_0'=16,'gz_1'=2] {'gy_0','gy_1','gz_1'}, dimensions={0} | all-to-all | bytes 32768 | tf_op jit(solution)/shard_map/all_to_all | solution.py:35
  34.4 26.1 %all_to_all.11.line = f32[16,1,128]{2,1,0:T(1,128)S(1)} all-to-all(f32[16,1,128]{2,1,0:T(1,128)S(1)} %broadcast_in_dim.7), channel_id=1, replica_groups=mesh['gy_0'=4,'gy_1'=4,'gz_0'=16,'gz_1'=2] {'gz_0'}, dimensions={0} | all-to-all | bytes 16384 | tf_op jit(solution)/shard_map/all_to_all | solution.py:35
  60.5 1.5 %finish.1 = (f32[512,128]{1,0:T(8,128)}, f32[512,128]{1,0:T(8,128)}, f32[512,128]{1,0:T(8,128)}) custom-call(f32[512,128]{1,0:T(8,128)S(1)} %get-tuple-element.28.k, f32[512,128]{1,0:T(8,128)S(1)} %get-tuple-element.29.s, f32[512,128]{1,0:T(8,128)S(1)} %get-tuple-element.30.c, f32[1536,128]{1,0:T(8,128)S(1)} %get-tuple-element.31.shares, ...), custom_call_target="tpu_custom_call" | custom-call | tf_op jit(solution)/shard_map/finish/pallas_call | solution.py:528
  (3 shorter events, 0.0 us)
Async XLA Ops:
  2.1 10.0 %collective-permute-start = (f32[232,128]{1,0:T(8,128)S(1)}, f32[232,128]{1,0:T(8,128)S(1)}, u32[]{:S(2)}, u32[]{:S(2)}) collective-permute-start(f32[232,128]{1,0:T(8,128)S(1)} %get-tuple-element.32), channel_id=1, source_target_pairs={{32,64},{64,32},{96,128},{128,96},{160,192},{192,160},{224,256},{2... | collective-permute-start | bytes 356360 | tf_op jit(solution)/shard_map/ppermute | solution.py:29
  2.7 9.3 %collective-permute-start.1 = (f32[232,128]{1,0:T(8,128)S(1)}, f32[232,128]{1,0:T(8,128)S(1)}, u32[]{:S(2)}, u32[]{:S(2)}) collective-permute-start(f32[232,128]{1,0:T(8,128)S(1)} %get-tuple-element.33), channel_id=1, source_target_pairs={{0,32},{32,0},{64,96},{96,64},{128,160},{160,128},{192,224},{224,1... | collective-permute-start | bytes 356360 | tf_op jit(solution)/shard_map/ppermute | solution.py:30
  12.4 7.3 %collective-permute-start.2 = (f32[128,128]{1,0:T(8,128)S(1)}, f32[128,128]{1,0:T(8,128)S(1)}, u32[]{:S(2)}, u32[]{:S(2)}) collective-permute-start(f32[128,128]{1,0:T(8,128)S(1)} %get-tuple-element.42), channel_id=1, source_target_pairs={{1,2},{2,1},{3,4},{4,3},{5,6},{6,5},{7,8},{8,7},{9,10},{10,9},{11,... | collective-permute-start | bytes 196616 | tf_op jit(solution)/shard_map/ppermute | solution.py:29
  17.0 3.1 %collective-permute-start.3 = (f32[128,128]{1,0:T(8,128)S(1)}, f32[128,128]{1,0:T(8,128)S(1)}, u32[]{:S(2)}, u32[]{:S(2)}) collective-permute-start(f32[128,128]{1,0:T(8,128)S(1)} %get-tuple-element.43), channel_id=1, source_target_pairs={{0,1},{1,0},{2,3},{3,2},{4,5},{5,4},{6,7},{7,6},{8,9},{9,8},{10,11... | collective-permute-start | bytes 196616 | tf_op jit(solution)/shard_map/ppermute | solution.py:30
